TPU v7x, 512 devices: a whole 4x4x16 slice. The times are simulated.
512 devices in a mesh: kg: 16 (over z_hi, y, core), pt: 32 (over x, z_lo).
Axes of the slice: x: 4, y: 4, z: 16 (z_hi: 2, z_lo: 8; z = z_hi * 8 + z_lo), core: 2. Of those that a mesh axis runs over, the one named last changes fastest.
Arguments:
- left_orbitals: bfloat16 [2, 64, 4096, 512], P(None, 'kg', 'pt'), may hold values from -6 to 6
- right_orbitals: bfloat16 [2, 64, 512, 512], P(None, 'kg', 'pt'), may hold values from -0.25 to 0.25
- coulomb: bfloat16 [64, 512, 4096], P(None, 'kg', 'pt'), may hold values from 0.049804688 to 0.5
Outputs:
- exchange_applied: float32 [2, 64, 4096, 512], P(None, 'kg', 'pt')
All inputs are finite; a program needn't handle non-finite values.
Results may differ from a plain program's by a relative error of at most 0.0038.
Values may be sent and summed in bfloat16 or wider, within the bound.
No kernel may reach another device: no remote copies, remote signals or barrier semaphores. Data moves between devices by JAX's collectives and lax.ppermute only.
A program may use at most 64 MiB of HBM per device.

v0:
```python
import jax
import jax.numpy as jnp
from jax import lax
from jax.sharding import PartitionSpec as P


def dft_tables(count):
    index = jnp.arange(count, dtype=jnp.int32)
    digit_one = index // 16
    digit_two = index // 4 % 4
    digit_three = index % 4
    phase = (
        digit_one[:, None] * digit_one[None, :]
        + digit_two[:, None] * digit_two[None, :]
        + digit_three[:, None] * digit_three[None, :]
    ) % 4
    cos_table = jnp.where(phase == 0, 1.0, jnp.where(phase == 2, -1.0, 0.0)).astype(jnp.float32)
    sin_table = jnp.where(phase == 1, 1.0, jnp.where(phase == 3, -1.0, 0.0)).astype(jnp.float32)
    return (cos_table, sin_table)


def cross(first, second):
    return jnp.einsum("kni,kmi->knm", first, second, preferred_element_type=jnp.float32)


def apply(first, second):
    return jnp.einsum("knm,kni->kmi", first, second, preferred_element_type=jnp.float32)


def kernel_terms(kernel, piece):
    out_re = apply(kernel[0], piece[0]) - apply(kernel[1], piece[1])
    out_im = apply(kernel[0], piece[1]) + apply(kernel[1], piece[0])
    return jnp.stack([out_re, out_im])


def spectral(columns, coulomb):
    shape = columns.shape
    count = shape[1]
    cos_table, sin_table = dft_tables(count)
    forward = jnp.concatenate(
        [jnp.concatenate([cos_table, sin_table], 1), jnp.concatenate([-sin_table, cos_table], 1)], 0
    ).astype(jnp.bfloat16)
    backward = jnp.concatenate(
        [jnp.concatenate([cos_table, -sin_table], 1), jnp.concatenate([sin_table, cos_table], 1)], 0
    ).astype(jnp.bfloat16)
    freq = jnp.dot(
        forward, columns.reshape(2 * count, -1), preferred_element_type=jnp.float32
    ).reshape(shape)
    weighted = (coulomb[None].astype(jnp.float32) * freq).astype(jnp.bfloat16)
    spatial = jnp.dot(
        backward, weighted.reshape(2 * count, -1), preferred_element_type=jnp.float32
    ) * (1.0 / count)
    return spatial.astype(jnp.bfloat16).reshape(shape)


def on_device(left_orbitals, right_orbitals, coulomb):
    left_re = left_orbitals[0]
    left_im = left_orbitals[1]
    piece = lax.all_gather(right_orbitals, "pt", axis=2, tiled=True)
    pair_re = cross(piece[0], left_re) + cross(piece[1], left_im)
    pair_im = cross(piece[0], left_im) - cross(piece[1], left_re)
    pairs = jnp.stack([pair_re, pair_im]).astype(jnp.bfloat16)
    columns = lax.all_to_all(pairs, "kg", split_axis=2, concat_axis=1, tiled=True)
    spatial = spectral(columns, coulomb)
    kernel = lax.all_to_all(spatial, "kg", split_axis=1, concat_axis=2, tiled=True)
    return kernel_terms(kernel, lax.all_gather(right_orbitals, "pt", axis=2, tiled=True))


def solution(mesh):
    in_specs = (P(None, "kg", "pt", None), P(None, "kg", "pt", None), P(None, "kg", "pt"))
    out_specs = P(None, "kg", "pt", None)
    return jax.shard_map(
        on_device, mesh=mesh, in_specs=in_specs, out_specs=out_specs, check_vma=False
    )
```

profile of v0, /device:TPU:39, one launch (start us, length us, event | category | flops | bytes accessed | tf_op | source)
XLA Modules:
  0.0 376.8 jit_solution(10838197598014243151)
XLA Ops:
  6.5 0.0 all-gather.2.cloned.1.call-start
  6.5 0.7 all-gather.2.cloned.1.call-update
  7.3 203.8 %all-gather.2.cloned.1.call-done = bf16[2,4,512,512]{3,2,1,0:T(8,128)(2,1)} async-done(((bf16[2,4,16,512]{3,2,1,0:T(8,128)(2,1)}), bf16[2,4,512,512]{3,2,1,0:T(8,128)(2,1)}) %all-gather.2.cloned.1.call-update) | async-done | bytes 4194320 | tf_op jit(solution)/shard_map/all_gather | solution.py:59
  211.0 0.0 copy-start
  211.0 2.5 fusion.5
  213.5 0.4 copy-done
  214.0 0.0 copy-start.3
  214.0 1.8 fusion.6
  215.8 0.0 copy-done.3
  215.8 0.7 fusion.10
  216.6 0.7 fusion.11
  217.3 0.1 pad_maximum_fusion.1
  217.4 0.0 copy-start.2
  217.4 1.8 copy.25
  219.2 31.8 %all-to-all-start = ((bf16[2,4,512,128]{3,1,0,2:T(4,128)(2,1)}), bf16[2,4,512,128]{3,1,0,2:T(4,128)(2,1)S(1)}, u32[]{:S(2)}, u32[]{:S(2)}) async-start(bf16[2,4,512,128]{3,1,0,2:T(4,128)(2,1)} %copy.25), calls=%async_computation | async-start | bytes 2097152 | tf_op jit(solution)/shard_map/all_to_all | solution.py:63
  251.0 0.0 copy-done.2
  251.0 0.2 copy.24
  251.2 0.1 fusion.28
  251.3 0.1 fusion.24
  251.4 35.3 %all-to-all-done = bf16[2,4,512,128]{3,1,0,2:T(4,128)(2,1)S(1)} async-done(((bf16[2,4,512,128]{3,1,0,2:T(4,128)(2,1)}), bf16[2,4,512,128]{3,1,0,2:T(4,128)(2,1)S(1)}, u32[]{:S(2)}, u32[]{:S(2)}) %all-to-all-start) | async-done | bytes 1048608 | tf_op jit(solution)/shard_map/all_to_all | solution.py:63
  286.8 0.3 copy.26
  287.0 0.5 copy.50
  287.5 0.7 copy.27
  288.1 0.4 multiply_convert_fusion
  288.6 0.7 copy.28
  289.3 0.5 fusion.1
  289.8 0.2 copy.44
  290.1 0.1 copy.29
  290.2 73.9 %all_to_all.30 = bf16[2,64,32,128]{3,2,0,1:T(8,128)(2,1)S(1)} all-to-all(bf16[2,64,32,128]{3,2,0,1:T(8,128)(2,1)S(1)} %copy.29), channel_id=1, replica_groups=mesh['kg'=16,'pt'=32] {'kg'}, dimensions={1} | all-to-all | bytes 2097152 | tf_op jit(solution)/shard_map/all_to_all | solution.py:65
  364.1 0.1 copy.30
  364.2 0.0 copy-start.1
  364.2 0.1 fusion.31
  364.4 2.0 copy-done.1
  366.4 0.5 fusion.7
  366.9 0.5 fusion.4
  367.4 0.5 fusion.2
  367.9 0.5 fusion.3
  368.4 1.6 pad_maximum_fusion
  (4 shorter events, 0.1 us)
Async XLA Ops:
  6.5 204.5 %all-gather.2.cloned.1.call-start = ((), (), s32[]{:S(2)}) async-start(), calls=%async_computation.2 | async-start | bytes 4325376 | tf_op jit(solution)/shard_map/all_gather | solution.py:59
  211.0 3.0 copy-start
  214.0 1.8 copy-start.3
  217.4 33.6 %copy-start.2 = (bf16[64,32,128]{2,1,0:T(8,128)(2,1)S(1)}, bf16[64,32,128]{2,1,0:T(8,128)(2,1)}, u32[]{:S(2)}) copy-start(bf16[64,32,128]{2,1,0:T(8,128)(2,1)} %param.5) | copy-start | bytes 1572868
  219.2 67.6 %all-to-all-start = ((bf16[2,4,512,128]{3,1,0,2:T(4,128)(2,1)}), bf16[2,4,512,128]{3,1,0,2:T(4,128)(2,1)S(1)}, u32[]{:S(2)}, u32[]{:S(2)}) async-start(bf16[2,4,512,128]{3,1,0,2:T(4,128)(2,1)} %copy.25), calls=%async_computation | async-start | bytes 2097152 | tf_op jit(solution)/shard_map/all_to_all | solution.py:63
  364.2 2.2 copy-start.1
Sparse Core Ops, SparseCore 0:
  9.4 201.5 all-gather.1
where the time goes:
time: 377 us
  waiting for transfers between devices  240 us (64%)
  blocking collectives  73.9 us (20%)
  starting transfers between devices  31.8 us (8%)
  between operations  13.6 us (4%)
  matrix products  8.71 us (2%)
  local copies, waits for them, and re-layouts  7.07 us (2%)
    all_gather x1, waiting for transfers between devices, on_device(): piece = lax.all_gather(right_orbitals, 'pt', axis=2, tiled=True)  204 us
    all_to_all x1, blocking collectives, on_device(): lax.all_to_all(spatial, 'kg', split_axis=1, concat_axis=2, tiled=True)  73.9 us
    all_to_all x1, waiting for transfers between devices, on_device(): lax.all_to_all(pairs, 'kg', split_axis=2, concat_axis=1, tiled=True)  35.3 us
    all_to_all x1, starting transfers between devices, on_device(): lax.all_to_all(pairs, 'kg', split_axis=2, concat_axis=1, tiled=True)  31.8 us
  transfers between devices with their start and end apart: 2, of which 2 were waited for; matrix products, arithmetic and copies ran while one was open for 0% of the time, Pallas kernels for 0%

commit v1 on v0

v1 whole, which is shorter than its diff:
```python
import jax
import jax.numpy as jnp
from jax import lax
from jax.experimental import pallas as pl
from jax.experimental.pallas import tpu as pltpu
from jax.sharding import PartitionSpec as P

XS, ZS = 4, 8
KG = 16
KL = 4
VMEM = pltpu.CompilerParams(vmem_limit_bytes=48 << 20)
Z_GROUPS = [[x * ZS + z for z in range(ZS)] for x in range(XS)]
X_GROUPS = [[x * ZS + z for x in range(XS)] for z in range(ZS)]


def pairs_kernel(left_ref, right_ref, out_ref):
    a_re, a_im = left_ref[0, 0], left_ref[1, 0]
    mu, orbitals = a_re.shape
    b_re = right_ref[:, 0, 0].reshape(-1, orbitals)
    b_im = right_ref[:, 1, 0].reshape(-1, orbitals)
    nt = (((1,), (1,)), ((), ()))
    first = jnp.concatenate([a_re, a_im], 0)
    second = jnp.concatenate([a_im, -a_re], 0)
    both = lax.dot_general(b_re, first, nt, preferred_element_type=jnp.float32) + lax.dot_general(
        b_im, second, nt, preferred_element_type=jnp.float32
    )
    both = both.astype(jnp.bfloat16)
    shape = (out_ref.shape[0], out_ref.shape[3], mu)
    out_ref[:, 0, 0] = both[:, :mu].reshape(shape)
    out_ref[:, 1, 0] = both[:, mu:].reshape(shape)


def make_pairs(left, right):
    pts, _, kl, nus, orbitals = right.shape
    mu = left.shape[2]
    rows = pts * nus // KG
    return pl.pallas_call(
        pairs_kernel,
        grid=(kl,),
        in_specs=[
            pl.BlockSpec((2, 1, mu, orbitals), lambda k: (0, k, 0, 0)),
            pl.BlockSpec((pts, 2, 1, nus, orbitals), lambda k: (0, 0, k, 0, 0)),
        ],
        out_specs=pl.BlockSpec((KG, 2, 1, rows, mu), lambda k: (0, 0, k, 0, 0)),
        out_shape=jax.ShapeDtypeStruct((KG, 2, kl, rows, mu), jnp.bfloat16),
        compiler_params=VMEM,
        cost_estimate=pl.CostEstimate(
            flops=8 * kl * pts * nus * mu * orbitals, bytes_accessed=6 << 20, transcendentals=0
        ),
        name="pairs",
    )(left, right)


def dft4(values, sign):
    (r0, i0), (r1, i1), (r2, i2), (r3, i3) = values
    ar, ai, br, bi = r0 + r2, i0 + i2, r0 - r2, i0 - i2
    cr, ci, dr, di = r1 + r3, i1 + i3, r1 - r3, i1 - i3
    if sign < 0:
        return [(ar + cr, ai + ci), (br + di, bi - dr), (ar - cr, ai - ci), (br - di, bi + dr)]
    return [(ar + cr, ai + ci), (br - di, bi + dr), (ar - cr, ai - ci), (br + di, bi - dr)]


def dft16(values, sign):
    out = list(values)
    for slow in range(4):
        out[4 * slow : 4 * slow + 4] = dft4(out[4 * slow : 4 * slow + 4], sign)
    for fast in range(4):
        out[fast::4] = dft4(out[fast::4], sign)
    return out


def spectral_kernel(x_ref, c_ref, out_ref, work_ref):
    rows = work_ref.shape[2]
    for top in range(4):
        values = []
        for low in range(16):
            kg, kl = 4 * top + low // 4, low % 4
            values.append(tuple(x_ref[kg, part, kl].astype(jnp.float32) for part in range(2)))
        for low, (re, im) in enumerate(dft16(values, -1)):
            work_ref[0, 16 * top + low] = re
            work_ref[1, 16 * top + low] = im
    for low in range(16):
        values = [(work_ref[0, 16 * top + low], work_ref[1, 16 * top + low]) for top in range(4)]
        freq = dft4(values, -1)
        weighted = []
        for top, (re, im) in enumerate(freq):
            c = c_ref[16 * top + low].astype(jnp.float32)
            weighted.append(tuple((c * part).astype(jnp.bfloat16).astype(jnp.float32) for part in (re, im)))
        for top, (re, im) in enumerate(dft4(weighted, 1)):
            work_ref[0, 16 * top + low] = re
            work_ref[1, 16 * top + low] = im
    for top in range(4):
        values = [(work_ref[0, 16 * top + low], work_ref[1, 16 * top + low]) for low in range(16)]
        for low, parts in enumerate(dft16(values, 1)):
            kg, kl = 4 * top + low // 4, low % 4
            for part in range(2):
                out_ref[kg, part, kl] = (parts[part] * (1.0 / 64.0)).astype(jnp.bfloat16)


def spectral(x, coulomb):
    kg, _, kl, nus, mu = x.shape
    rows = 16
    return pl.pallas_call(
        spectral_kernel,
        grid=(nus // rows,),
        in_specs=[
            pl.BlockSpec((kg, 2, kl, rows, mu), lambda n: (0, 0, 0, n, 0)),
            pl.BlockSpec((kg * kl, rows, mu), lambda n: (0, n, 0)),
        ],
        out_specs=pl.BlockSpec((kg, 2, kl, rows, mu), lambda n: (0, 0, 0, n, 0)),
        out_shape=jax.ShapeDtypeStruct(x.shape, jnp.bfloat16),
        scratch_shapes=[pltpu.VMEM((2, kg * kl, rows, mu), jnp.float32)],
        compiler_params=VMEM,
        cost_estimate=pl.CostEstimate(flops=32 * kg * kl * nus * mu, bytes_accessed=5 << 19, transcendentals=0),
        name="spectral",
    )(x, coulomb)


def apply_kernel(kernel_ref, right_ref, out_ref):
    mu = kernel_ref.shape[4]
    orbitals = right_ref.shape[4]
    k_re = kernel_ref[:, 0, 0].reshape(-1, mu)
    k_im = kernel_ref[:, 1, 0].reshape(-1, mu)
    b_re = right_ref[:, 0, 0].reshape(-1, orbitals)
    b_im = right_ref[:, 1, 0].reshape(-1, orbitals)
    tn = (((0,), (0,)), ((), ()))
    first = jnp.concatenate([k_re, k_im], 1)
    second = jnp.concatenate([-k_im, k_re], 1)
    both = lax.dot_general(first, b_re, tn, preferred_element_type=jnp.float32) + lax.dot_general(
        second, b_im, tn, preferred_element_type=jnp.float32
    )
    out_ref[0, 0] = both[:mu]
    out_ref[1, 0] = both[mu:]


def apply(kernel, right):
    kg, _, kl, rows, mu = kernel.shape
    pts, _, _, nus, orbitals = right.shape
    return pl.pallas_call(
        apply_kernel,
        grid=(kl,),
        in_specs=[
            pl.BlockSpec((kg, 2, 1, rows, mu), lambda k: (0, 0, k, 0, 0)),
            pl.BlockSpec((pts, 2, 1, nus, orbitals), lambda k: (0, 0, k, 0, 0)),
        ],
        out_specs=pl.BlockSpec((2, 1, mu, orbitals), lambda k: (0, k, 0, 0)),
        out_shape=jax.ShapeDtypeStruct((2, kl, mu, orbitals), jnp.float32),
        compiler_params=VMEM,
        cost_estimate=pl.CostEstimate(
            flops=8 * kl * pts * nus * mu * orbitals, bytes_accessed=7 << 20, transcendentals=0
        ),
        name="apply",
    )(kernel, right)


def spread(block, groups):
    count = len(groups[0])
    stacked = jnp.broadcast_to(block[None], (count, *block.shape))
    return lax.all_to_all(stacked, "pt", split_axis=0, concat_axis=0, tiled=True, axis_index_groups=groups)


def on_device(left, right, coulomb):
    column = spread(right, Z_GROUPS)
    whole = spread(column, X_GROUPS).reshape(XS * ZS, *right.shape)
    pairs = make_pairs(left, whole)
    columns = lax.all_to_all(pairs, "kg", split_axis=0, concat_axis=0, tiled=True)
    spatial = spectral(columns, coulomb)
    kernel = lax.all_to_all(spatial, "kg", split_axis=0, concat_axis=0, tiled=True)
    return apply(kernel, whole)


def solution(mesh):
    in_specs = (P(None, "kg", "pt", None), P(None, "kg", "pt", None), P(None, "kg", "pt"))
    out_specs = P(None, "kg", "pt", None)
    return jax.shard_map(on_device, mesh=mesh, in_specs=in_specs, out_specs=out_specs, check_vma=False)
```

time: 377 us -> 242 us (0.64)
  the two profiles are of different devices: /device:TPU:39 before, /device:TPU:1 now
where the time goes in v1:
time: 242 us
  blocking collectives  231 us (95%)
  Pallas kernels  9.06 us (4%)
    all_to_all x2, blocking collectives, spread(): lax.all_to_all(stacked, 'pt', split_axis=0, concat_axis=0, tiled=True, ax...  114 us
    all_to_all x1, blocking collectives, on_device(): lax.all_to_all(pairs, 'kg', split_axis=0, concat_axis=0, tiled=True)  59.5 us
    all_to_all x1, blocking collectives, on_device(): lax.all_to_all(spatial, 'kg', split_axis=0, concat_axis=0, tiled=True)  57.7 us

profile of v1, /device:TPU:1, one launch (start us, length us, event | category | flops | bytes accessed | tf_op | source)
XLA Modules:
  0.0 241.6 jit_solution(7540944112817853148)
XLA Ops:
  0.0 1.0 broadcast_in_dim.4
  1.0 63.2 %all_to_all.20 = bf16[8,2,4,16,512]{4,3,2,1,0:T(8,128)(2,1)S(1)} all-to-all(bf16[8,2,4,16,512]{4,3,2,1,0:T(8,128)(2,1)S(1)} %broadcast_in_dim.4), channel_id=1, replica_groups={{0,1,2,3,4,5,6,7},{8,9,10,11,12,13,14,15},{16,17,18,19,20,21,22,23},{24..., dimensions={0} | all-to-all | bytes 2097152 | tf_op jit(solution)/shard_map/all_to_all | solution.py:159
  64.3 0.5 broadcast_in_dim.5
  64.8 0.0 copy-start.1
  64.8 50.5 %all_to_all.21 = bf16[4,8,2,4,16,512]{5,4,3,2,1,0:T(8,128)(2,1)} all-to-all(bf16[4,8,2,4,16,512]{5,4,3,2,1,0:T(8,128)(2,1)S(1)} %broadcast_in_dim.5), channel_id=1, replica_groups={{0,8,16,24},{1,9,17,25},{2,10,18,26},{3,11,19,27},{4,12,20,28},{5,13,21..., dimensions={0} | all-to-all | bytes 8388608 | tf_op jit(solution)/shard_map/all_to_all | solution.py:159
  115.3 0.0 copy-done.1
  115.3 0.0 copy-start.2
  115.3 4.1 %pairs.1 = bf16[16,2,4,32,128]{4,3,2,1,0:T(8,128)(2,1)S(1)} custom-call(bf16[2,4,128,512]{3,2,1,0:T(8,128)(2,1)S(1)} %copy-done.1, bf16[32,2,4,16,512]{4,3,2,1,0:T(8,128)(2,1)} %bitcast.1), custom_call_target="tpu_custom_call" | custom-call | flops 1073741824 | bytes 6291456 | tf_op jit(solution)/shard_map/pairs/pallas_call | solution.py:37
  119.5 0.0 copy-start
  119.5 59.5 %all_to_all.22.x_ref = bf16[16,2,4,32,128]{4,3,2,1,0:T(8,128)(2,1)S(1)} all-to-all(bf16[16,2,4,32,128]{4,3,2,1,0:T(8,128)(2,1)S(1)} %pairs.1), channel_id=1, replica_groups=mesh['kg'=16,'pt'=32] {'kg'}, dimensions={0} | all-to-all | bytes 2097152 | tf_op jit(solution)/shard_map/all_to_all | solution.py:166
  179.0 0.0 copy-done.2
  179.0 1.7 spectral.1
  180.7 57.7 %all_to_all.23.kernel_ref = bf16[16,2,4,32,128]{4,3,2,1,0:T(8,128)(2,1)S(1)} all-to-all(bf16[16,2,4,32,128]{4,3,2,1,0:T(8,128)(2,1)S(1)} %spectral.1), channel_id=1, replica_groups=mesh['kg'=16,'pt'=32] {'kg'}, dimensions={0} | all-to-all | bytes 2097152 | tf_op jit(solution)/shard_map/all_to_all | solution.py:168
  238.3 0.0 copy-done
  238.3 3.3 %apply.1 = f32[2,4,128,512]{3,2,1,0:T(8,128)} custom-call(bf16[16,2,4,32,128]{4,3,2,1,0:T(8,128)(2,1)S(1)} %all_to_all.23.kernel_ref, bf16[32,2,4,16,512]{4,3,2,1,0:T(8,128)(2,1)S(1)} %bitcast.2), custom_call_target="tpu_custom_call" | custom-call | flops 1073741824 | bytes 7340032 | tf_op jit(solution)/shard_map/apply/pallas_call | solution.py:139
Async XLA Ops:
  64.8 50.5 %copy-start.1 = (bf16[2,4,128,512]{3,2,1,0:T(8,128)(2,1)S(1)}, bf16[2,4,128,512]{3,2,1,0:T(8,128)(2,1)}, u32[]{:S(2)}) copy-start(bf16[2,4,128,512]{3,2,1,0:T(8,128)(2,1)} %left_ref.1) | copy-start | bytes 3145732
  115.3 63.7 %copy-start.2 = (bf16[64,32,128]{2,1,0:T(8,128)(2,1)S(1)}, bf16[64,32,128]{2,1,0:T(8,128)(2,1)}, u32[]{:S(2)}) copy-start(bf16[64,32,128]{2,1,0:T(8,128)(2,1)} %c_ref.1) | copy-start | bytes 1572868
  119.5 118.9 %copy-start = (bf16[4,8,2,4,16,512]{5,4,3,2,1,0:T(8,128)(2,1)S(1)}, bf16[4,8,2,4,16,512]{5,4,3,2,1,0:T(8,128)(2,1)}, u32[]{:S(2)}) copy-start(bf16[4,8,2,4,16,512]{5,4,3,2,1,0:T(8,128)(2,1)} %all_to_all.21) | copy-start | bytes 12582916

commit v2 on v1

v2 whole, which is shorter than its diff:
```python
import functools

import jax
import jax.numpy as jnp
from jax import lax
from jax.experimental import pallas as pl
from jax.experimental.pallas import tpu as pltpu
from jax.sharding import Mesh, PartitionSpec as P

XS, ZH, ZQ = 4, 2, 4
KG, KL = 16, 4
VMEM = pltpu.CompilerParams(vmem_limit_bytes=48 << 20)


def pairs_kernel(zh_ref, left_ref, right_ref, out_ref):
    a_re, a_im = left_ref[0, 0], left_ref[0, 1]
    mu, orbitals = a_re.shape
    nt = (((1,), (1,)), ((), ()))
    first = jnp.concatenate([a_re, a_im], 0)
    second = jnp.concatenate([a_im, -a_re], 0)
    for side in range(2):
        b_re = right_ref[:, :, 0, side].reshape(-1, orbitals)
        b_im = right_ref[:, :, 1, side].reshape(-1, orbitals)
        both = lax.dot_general(b_re, first, nt, preferred_element_type=jnp.float32) + lax.dot_general(
            b_im, second, nt, preferred_element_type=jnp.float32
        )
        both = both.astype(jnp.bfloat16)
        at = zh_ref[0] if side == 0 else 1 - zh_ref[0]
        shape = (XS, ZQ // 2, out_ref.shape[5], mu)
        out_ref[:, at, :, 0, 0] = both[:, :mu].reshape(shape)
        out_ref[:, at, :, 0, 1] = both[:, mu:].reshape(shape)


def make_pairs(zh, left, right):
    blocks, _, mu, orbitals = left.shape
    nus = right.shape[4]
    whole = pl.BlockSpec(right.shape, lambda m, zh: (0,) * 6)
    return pl.pallas_call(
        pairs_kernel,
        grid_spec=pltpu.PrefetchScalarGridSpec(
            num_scalar_prefetch=1,
            grid=(blocks,),
            in_specs=[pl.BlockSpec((1, 2, mu, orbitals), lambda m, zh: (m, 0, 0, 0)), whole],
            out_specs=pl.BlockSpec((XS, ZH, ZQ // 2, 1, 2, 2 * nus, mu), lambda m, zh: (0, 0, 0, m, 0, 0, 0)),
        ),
        out_shape=jax.ShapeDtypeStruct((XS, ZH, ZQ // 2, blocks, 2, 2 * nus, mu), jnp.bfloat16),
        compiler_params=VMEM,
        cost_estimate=pl.CostEstimate(
            flops=8 * blocks * 32 * nus * mu * orbitals, bytes_accessed=3 << 20, transcendentals=0
        ),
        name="pairs",
    )(zh, left, right)


def dft4(values, sign):
    (r0, i0), (r1, i1), (r2, i2), (r3, i3) = values
    ar, ai, br, bi = r0 + r2, i0 + i2, r0 - r2, i0 - i2
    cr, ci, dr, di = r1 + r3, i1 + i3, r1 - r3, i1 - i3
    if sign < 0:
        return [(ar + cr, ai + ci), (br + di, bi - dr), (ar - cr, ai - ci), (br - di, bi + dr)]
    return [(ar + cr, ai + ci), (br - di, bi + dr), (ar - cr, ai - ci), (br + di, bi - dr)]


def dft16(values, sign):
    out = list(values)
    for slow in range(4):
        out[4 * slow : 4 * slow + 4] = dft4(out[4 * slow : 4 * slow + 4], sign)
    for fast in range(4):
        out[fast::4] = dft4(out[fast::4], sign)
    return out


def spectral_kernel(x_ref, c_ref, out_ref, work_ref):
    for top in range(4):
        values = [
            tuple(x_ref[16 * top + low, part].astype(jnp.float32) for part in range(2)) for low in range(16)
        ]
        for low, (re, im) in enumerate(dft16(values, -1)):
            work_ref[0, 16 * top + low] = re
            work_ref[1, 16 * top + low] = im
    for low in range(16):
        values = [(work_ref[0, 16 * top + low], work_ref[1, 16 * top + low]) for top in range(4)]
        weighted = []
        for top, (re, im) in enumerate(dft4(values, -1)):
            c = c_ref[16 * top + low].astype(jnp.float32)
            weighted.append(tuple((c * part).astype(jnp.bfloat16).astype(jnp.float32) for part in (re, im)))
        for top, (re, im) in enumerate(dft4(weighted, 1)):
            work_ref[0, 16 * top + low] = re
            work_ref[1, 16 * top + low] = im
    for top in range(4):
        values = [(work_ref[0, 16 * top + low], work_ref[1, 16 * top + low]) for low in range(16)]
        for low, parts in enumerate(dft16(values, 1)):
            for part in range(2):
                out_ref[16 * top + low, part] = (parts[part] * (1.0 / 64.0)).astype(jnp.bfloat16)


def spectral(x, coulomb):
    count, _, nus, mu = x.shape
    rows = 16
    block = pl.BlockSpec((count, 2, rows, mu), lambda n: (0, 0, n, 0))
    return pl.pallas_call(
        spectral_kernel,
        grid=(nus // rows,),
        in_specs=[block, pl.BlockSpec((count, rows, mu), lambda n: (0, n, 0))],
        out_specs=block,
        out_shape=jax.ShapeDtypeStruct(x.shape, jnp.bfloat16),
        scratch_shapes=[pltpu.VMEM((2, count, rows, mu), jnp.float32)],
        compiler_params=VMEM,
        cost_estimate=pl.CostEstimate(flops=32 * count * nus * mu, bytes_accessed=5 << 19, transcendentals=0),
        name="spectral",
    )(x, coulomb)


def apply_kernel(zh_ref, kernel_ref, right_ref, out_ref):
    mu, orbitals = out_ref.shape[2:]
    tn = (((0,), (0,)), ((), ()))
    total = None
    for side in range(2):
        at = zh_ref[0] if side == 0 else 1 - zh_ref[0]
        k_re = kernel_ref[:, at, :, 0, 0].reshape(-1, mu)
        k_im = kernel_ref[:, at, :, 0, 1].reshape(-1, mu)
        b_re = right_ref[0, :, :, 0, side].reshape(-1, orbitals)
        b_im = right_ref[0, :, :, 1, side].reshape(-1, orbitals)
        first = jnp.concatenate([k_re, k_im], 1)
        second = jnp.concatenate([-k_im, k_re], 1)
        term = lax.dot_general(first, b_re, tn, preferred_element_type=jnp.float32) + lax.dot_general(
            second, b_im, tn, preferred_element_type=jnp.float32
        )
        total = term if total is None else total + term
    out_ref[0, 0] = total[:mu]
    out_ref[1, 0] = total[mu:]


def apply(zh, kernel, right):
    xs, zhs, pairs, kl, _, rows, mu = kernel.shape
    orbitals = right.shape[-1]
    return pl.pallas_call(
        apply_kernel,
        grid_spec=pltpu.PrefetchScalarGridSpec(
            num_scalar_prefetch=1,
            grid=(kl,),
            in_specs=[
                pl.BlockSpec((xs, zhs, pairs, 1, 2, rows, mu), lambda k, zh: (0, 0, 0, k, 0, 0, 0)),
                pl.BlockSpec((1, *right.shape[1:]), lambda k, zh: (k, 0, 0, 0, 0, 0, 0)),
            ],
            out_specs=pl.BlockSpec((2, 1, mu, orbitals), lambda k, zh: (0, k, 0, 0)),
        ),
        out_shape=jax.ShapeDtypeStruct((2, kl, mu, orbitals), jnp.float32),
        compiler_params=VMEM,
        cost_estimate=pl.CostEstimate(
            flops=8 * kl * xs * zhs * pairs * rows * mu * orbitals, bytes_accessed=7 << 20, transcendentals=0
        ),
        name="apply",
    )(zh, kernel, right)


def swap(blocks, axes):
    return lax.all_to_all(blocks, axes, split_axis=0, concat_axis=0, tiled=True)


def on_device(left, right, coulomb):
    parts, kl, nus, orbitals = right.shape
    mu = left.shape[2]
    zh = jnp.full((1,), lax.axis_index("zh"), jnp.int32)
    sides = jnp.stack([right, lax.ppermute(right, "zh", [(0, 1), (1, 0)])], 2)
    sides = jnp.broadcast_to(
        sides.transpose(1, 0, 2, 3, 4)[:, None], (kl, ZQ, parts, 2, nus, orbitals)
    )
    mine = swap(sides.reshape(kl * ZQ, parts, 2, nus, orbitals), ("x", "zq"))
    mine = mine.reshape(XS, ZQ, parts, 2, nus, orbitals)
    rows = swap(jnp.swapaxes(left, 0, 1), "x")
    pairs = make_pairs(zh, rows, mine)
    columns = swap(pairs.reshape(KG * XS, parts, 2 * nus, mu), ("kg", "x"))
    kernel = swap(spectral(columns, coulomb).reshape(KG, KL, parts, 2 * nus, mu), "kg")
    whole = lax.all_gather(mine, "x", axis=0)
    return apply(zh, kernel.reshape(XS, ZH, ZQ // 2, KL, parts, 2 * nus, mu), whole)


def solution(mesh):
    split = Mesh(mesh.devices.reshape(KG, XS, ZH, ZQ), ("kg", "x", "zh", "zq"))
    points = ("x", "zh", "zq")
    in_specs = (P(None, "kg", points, None), P(None, "kg", points, None), P(None, "kg", points))
    out_specs = P(None, "kg", points, None)
    return jax.shard_map(on_device, mesh=split, in_specs=in_specs, out_specs=out_specs, check_vma=False)
```

time: 242 us -> 216 us (0.89)
  the two profiles are of different devices: /device:TPU:1 before, /device:TPU:33 now
where the time goes in v2:
time: 216 us
  waiting for transfers between devices  143 us (66%)
  starting transfers between devices  45.6 us (21%)
  between operations  13.5 us (6%)
  Pallas kernels  8.29 us (4%)
  local copies, waits for them, and re-layouts  5.61 us (3%)
    all_to_all x4, waiting for transfers between devices, swap(): return lax.all_to_all(blocks, axes, split_axis=0, concat_axis=0, tiled=True)  133 us
    all_to_all x4, starting transfers between devices, swap(): return lax.all_to_all(blocks, axes, split_axis=0, concat_axis=0, tiled=True)  36.8 us
    ppermute x1, starting transfers between devices, on_device(): sides = jnp.stack([right, lax.ppermute(right, 'zh', [(0, 1), (1, 0)])], 2)  8.81 us
    ppermute x1, waiting for transfers between devices, on_device(): sides = jnp.stack([right, lax.ppermute(right, 'zh', [(0, 1), (1, 0)])], 2)  8.55 us
    unnamed x9, local copies, waits for them, and re-layouts  4.5 us
  transfers between devices with their start and end apart: 6, of which 4 were waited for; matrix products, arithmetic and copies ran while one was open for 0% of the time, Pallas kernels for 1%

profile of v2, /device:TPU:33, one launch (start us, length us, event | category | flops | bytes accessed | tf_op | source)
XLA Modules:
  0.0 215.6 jit_solution(17014008468426846051)
XLA Ops:
  6.5 0.0 copy-start.3
  6.5 2.3 %copy.9 = bf16[2,4,128,512]{3,2,0,1:T(8,128)(2,1)} copy(bf16[2,4,128,512]{3,2,1,0:T(8,128)(2,1)} %param.3) | data formatting | bytes 2097152 | tf_op args[0]
  8.8 4.0 %all-to-all-start = ((bf16[4,2,128,512]{3,2,1,0:T(8,128)(2,1)}), bf16[4,2,128,512]{3,2,1,0:T(8,128)(2,1)S(1)}, u32[]{:S(2)}, u32[]{:S(2)}) async-start(bf16[4,2,128,512]{3,2,1,0:T(8,128)(2,1)} %bitcast.13), calls=%async_computation | async-start | bytes 2097152 | tf_op jit(solution)/shard_map/all_to_all | solution.py:158
  12.8 0.0 copy-done.3
  12.8 8.8 %collective-permute-start = (bf16[2,4,16,512]{3,2,1,0:T(8,128)(2,1)S(1)}, bf16[2,4,16,512]{3,2,1,0:T(8,128)(2,1)S(1)}, u32[]{:S(2)}, u32[]{:S(2)}) collective-permute-start(bf16[2,4,16,512]{3,2,1,0:T(8,128)(2,1)S(1)} %copy-done.3), channel_id=1, source_target_pairs={{0,4},{4,0},{1,5},{5,1},{2,6},{6,2},{3,7},{7,3},{8,12},{12,8},{9,1... | collective-permute-start | bytes 393224 | tf_op jit(solution)/shard_map/ppermute | solution.py:165
  21.7 8.6 %collective-permute-done = bf16[2,4,16,512]{3,2,1,0:T(8,128)(2,1)S(1)} collective-permute-done((bf16[2,4,16,512]{3,2,1,0:T(8,128)(2,1)S(1)}, bf16[2,4,16,512]{3,2,1,0:T(8,128)(2,1)S(1)}, u32[]{:S(2)}, u32[]{:S(2)}) %collective-permute-start) | collective-permute-done | bytes 131104 | tf_op jit(solution)/shard_map/ppermute | solution.py:165
  30.3 0.0 all-to-all-done.left_ref
  30.3 1.1 broadcast_in_dim.10
  31.4 0.0 copy-start.2
  31.4 10.0 %all-to-all-start.1 = ((bf16[16,2,2,16,512]{4,3,2,1,0:T(8,128)(2,1)}), bf16[16,2,2,16,512]{4,3,2,1,0:T(8,128)(2,1)S(1)}, u32[]{:S(2)}, u32[]{:S(2)}) async-start(bf16[16,2,2,16,512]{4,3,2,1,0:T(8,128)(2,1)} %bitcast.17), calls=%async_computation.1 | async-start | bytes 2097152 | tf_op jit(solution)/shard_map/all_to_all | solution.py:158
  41.4 23.3 %all-to-all-done.1 = bf16[16,2,2,16,512]{4,3,2,1,0:T(8,128)(2,1)S(1)} async-done(((bf16[16,2,2,16,512]{4,3,2,1,0:T(8,128)(2,1)}), bf16[16,2,2,16,512]{4,3,2,1,0:T(8,128)(2,1)S(1)}, u32[]{:S(2)}, u32[]{:S(2)}) %all-to-all-start.1) | async-done | bytes 1048608 | tf_op jit(solution)/shard_map/all_to_all | solution.py:158
  64.6 0.0 copy-start.1
  64.6 2.9 %pairs.1 = bf16[4,2,2,4,2,32,128]{6,5,4,3,2,1,0:T(8,128)(2,1)} custom-call(s32[1]{0:T(128)} %bitcast.zh_ref, bf16[4,2,128,512]{3,2,1,0:T(8,128)(2,1)S(1)} %all-to-all-done.left_ref, bf16[4,4,2,2,16,512]{5,4,3,2,1,0:T(8,128)(2,1)S(1)} %bitcast.14), custom_call_target="tpu_custom_call" | custom-call | flops 1073741824 | bytes 3145728 | tf_op jit(solution)/shard_map/pairs/pallas_call | solution.py:38
  67.5 18.3 %all-to-all-start.2 = ((bf16[64,2,32,128]{3,2,1,0:T(8,128)(2,1)}), bf16[64,2,32,128]{3,2,1,0:T(8,128)(2,1)S(1)}, u32[]{:S(2)}, u32[]{:S(2)}) async-start(bf16[64,2,32,128]{3,2,1,0:T(8,128)(2,1)} %bitcast.7), calls=%async_computation.2 | async-start | bytes 2097152 | tf_op jit(solution)/shard_map/all_to_all | solution.py:158
  85.8 0.0 all-gather.2.cloned.1.call-start
  85.8 0.0 copy-done.1
  85.8 0.7 all-gather.2.cloned.1.call-update
  86.5 58.7 %all-to-all-done.2.x_ref = bf16[64,2,32,128]{3,2,1,0:T(8,128)(2,1)S(1)} async-done(((bf16[64,2,32,128]{3,2,1,0:T(8,128)(2,1)}), bf16[64,2,32,128]{3,2,1,0:T(8,128)(2,1)S(1)}, u32[]{:S(2)}, u32[]{:S(2)}) %all-to-all-start.2) | async-done | bytes 1048608 | tf_op jit(solution)/shard_map/all_to_all | solution.py:158
  145.2 0.0 copy-done.2
  145.2 2.4 %spectral.1 = bf16[64,2,32,128]{3,2,1,0:T(8,128)(2,1)} custom-call(bf16[64,2,32,128]{3,2,1,0:T(8,128)(2,1)S(1)} %all-to-all-done.2.x_ref, bf16[64,32,128]{2,1,0:T(8,128)(2,1)S(1)} %copy-done.2), custom_call_target="tpu_custom_call" | custom-call | flops 8388608 | bytes 2621440 | tf_op jit(solution)/shard_map/spectral/pallas_call | solution.py:101
  147.6 4.5 %all-to-all-start.3 = ((bf16[16,4,2,32,128]{4,3,2,1,0:T(8,128)(2,1)}), bf16[16,4,2,32,128]{4,3,2,1,0:T(8,128)(2,1)S(1)}, u32[]{:S(2)}, u32[]{:S(2)}) async-start(bf16[16,4,2,32,128]{4,3,2,1,0:T(8,128)(2,1)} %bitcast.8), calls=%async_computation.3 | async-start | bytes 2097152 | tf_op jit(solution)/shard_map/all_to_all | solution.py:158
  152.1 0.0 all-gather.2.cloned.1.call-done.right_ref
  152.1 51.4 %all-to-all-done.3 = bf16[16,4,2,32,128]{4,3,2,1,0:T(8,128)(2,1)S(1)} async-done(((bf16[16,4,2,32,128]{4,3,2,1,0:T(8,128)(2,1)}), bf16[16,4,2,32,128]{4,3,2,1,0:T(8,128)(2,1)S(1)}, u32[]{:S(2)}, u32[]{:S(2)}) %all-to-all-start.3) | async-done | bytes 1048608 | tf_op jit(solution)/shard_map/all_to_all | solution.py:158
  203.5 0.0 copy-start
  203.5 2.2 %copy-done = bf16[4,4,4,2,2,16,512]{6,5,4,3,2,1,0:T(8,128)(2,1)S(1)} copy-done((bf16[4,4,4,2,2,16,512]{6,5,4,3,2,1,0:T(8,128)(2,1)S(1)}, bf16[4,4,4,2,2,16,512]{6,5,4,3,2,1,0:T(8,128)(2,1)}, u32[]{:S(2)}) %copy-start) | copy-done | bytes 4194328
  205.7 3.1 %apply.1 = f32[2,4,128,512]{3,2,1,0:T(8,128)} custom-call(s32[1]{0:T(128)} %bitcast.zh_ref, bf16[4,2,2,4,2,32,128]{6,5,4,3,2,1,0:T(8,128)(2,1)S(1)} %bitcast.16, bf16[4,4,4,2,2,16,512]{6,5,4,3,2,1,0:T(8,128)(2,1)S(1)} %copy-done), custom_call_target="tpu_custom_call" | custom-call | flops 1073741824 | bytes 7340032 | tf_op jit(solution)/shard_map/apply/pallas_call | solution.py:137
  (2 shorter events, 0.0 us)
Async XLA Ops:
  6.5 6.3 %copy-start.3 = (bf16[2,4,16,512]{3,2,1,0:T(8,128)(2,1)S(1)}, bf16[2,4,16,512]{3,2,1,0:T(8,128)(2,1)}, u32[]{:S(2)}) copy-start(bf16[2,4,16,512]{3,2,1,0:T(8,128)(2,1)} %param.4) | copy-start | bytes 393220
  8.8 21.4 %all-to-all-start = ((bf16[4,2,128,512]{3,2,1,0:T(8,128)(2,1)}), bf16[4,2,128,512]{3,2,1,0:T(8,128)(2,1)S(1)}, u32[]{:S(2)}, u32[]{:S(2)}) async-start(bf16[4,2,128,512]{3,2,1,0:T(8,128)(2,1)} %bitcast.13), calls=%async_computation | async-start | bytes 2097152 | tf_op jit(solution)/shard_map/all_to_all | solution.py:158
  12.8 17.4 %collective-permute-start = (bf16[2,4,16,512]{3,2,1,0:T(8,128)(2,1)S(1)}, bf16[2,4,16,512]{3,2,1,0:T(8,128)(2,1)S(1)}, u32[]{:S(2)}, u32[]{:S(2)}) collective-permute-start(bf16[2,4,16,512]{3,2,1,0:T(8,128)(2,1)S(1)} %copy-done.3), channel_id=1, source_target_pairs={{0,4},{4,0},{1,5},{5,1},{2,6},{6,2},{3,7},{7,3},{8,12},{12,8},{9,1... | collective-permute-start | bytes 393224 | tf_op jit(solution)/shard_map/ppermute | solution.py:165
  31.4 113.8 %copy-start.2 = (bf16[64,32,128]{2,1,0:T(8,128)(2,1)S(1)}, bf16[64,32,128]{2,1,0:T(8,128)(2,1)}, u32[]{:S(2)}) copy-start(bf16[64,32,128]{2,1,0:T(8,128)(2,1)} %c_ref.1) | copy-start | bytes 1572868
  31.4 33.2 %all-to-all-start.1 = ((bf16[16,2,2,16,512]{4,3,2,1,0:T(8,128)(2,1)}), bf16[16,2,2,16,512]{4,3,2,1,0:T(8,128)(2,1)S(1)}, u32[]{:S(2)}, u32[]{:S(2)}) async-start(bf16[16,2,2,16,512]{4,3,2,1,0:T(8,128)(2,1)} %bitcast.17), calls=%async_computation.1 | async-start | bytes 2097152 | tf_op jit(solution)/shard_map/all_to_all | solution.py:158
  64.6 21.2 %copy-start.1 = (bf16[16,2,2,16,512]{4,3,2,1,0:T(8,128)(2,1)}, bf16[16,2,2,16,512]{4,3,2,1,0:T(8,128)(2,1)S(1)}, u32[]{:S(2)}) copy-start(bf16[16,2,2,16,512]{4,3,2,1,0:T(8,128)(2,1)S(1)} %all-to-all-done.1) | copy-start | bytes 3145732
  67.5 77.7 %all-to-all-start.2 = ((bf16[64,2,32,128]{3,2,1,0:T(8,128)(2,1)}), bf16[64,2,32,128]{3,2,1,0:T(8,128)(2,1)S(1)}, u32[]{:S(2)}, u32[]{:S(2)}) async-start(bf16[64,2,32,128]{3,2,1,0:T(8,128)(2,1)} %bitcast.7), calls=%async_computation.2 | async-start | bytes 2097152 | tf_op jit(solution)/shard_map/all_to_all | solution.py:158
  85.8 66.3 %all-gather.2.cloned.1.call-start = ((), (), s32[]{:S(2)}) async-start(), calls=%async_computation.4 | async-start | bytes 5242880 | tf_op jit(solution)/shard_map/all_gather | solution.py:175
  147.6 55.9 %all-to-all-start.3 = ((bf16[16,4,2,32,128]{4,3,2,1,0:T(8,128)(2,1)}), bf16[16,4,2,32,128]{4,3,2,1,0:T(8,128)(2,1)S(1)}, u32[]{:S(2)}, u32[]{:S(2)}) async-start(bf16[16,4,2,32,128]{4,3,2,1,0:T(8,128)(2,1)} %bitcast.8), calls=%async_computation.3 | async-start | bytes 2097152 | tf_op jit(solution)/shard_map/all_to_all | solution.py:158
  203.5 2.2 %copy-start = (bf16[4,4,4,2,2,16,512]{6,5,4,3,2,1,0:T(8,128)(2,1)S(1)}, bf16[4,4,4,2,2,16,512]{6,5,4,3,2,1,0:T(8,128)(2,1)}, u32[]{:S(2)}) copy-start(bf16[4,4,4,2,2,16,512]{6,5,4,3,2,1,0:T(8,128)(2,1)} %all-gather.2.cloned.1.call-done.right_ref) | copy-start | bytes 12582916
Sparse Core Ops, SparseCore 0:
  88.7 61.3 all-gather.1

commit v3 on v2

v3 whole, which is shorter than its diff:
```python
import functools

import jax
import jax.numpy as jnp
from jax import lax
from jax.experimental import pallas as pl
from jax.experimental.pallas import tpu as pltpu
from jax.sharding import Mesh, PartitionSpec as P

XS, ZH, ZQ = 4, 2, 4
KG, KL = 16, 4
VMEM = pltpu.CompilerParams(vmem_limit_bytes=48 << 20)


def pairs_kernel(place_ref, *refs):
    lefts, right_ref, out_ref = refs[:XS], refs[XS], refs[-1]
    mu, orbitals = lefts[0].shape[2:]
    nt = (((1,), (1,)), ((), ()))
    b_re = right_ref[:, :, 0, 0].reshape(-1, orbitals)
    b_im = right_ref[:, :, 1, 0].reshape(-1, orbitals)
    shape = (XS, ZQ // 2, out_ref.shape[5], mu)
    for d, left_ref in enumerate(lefts):
        a_re, a_im = left_ref[0, 0], left_ref[1, 0]
        first = jnp.concatenate([a_re, a_im], 0)
        second = jnp.concatenate([a_im, -a_re], 0)
        both = lax.dot_general(b_re, first, nt, preferred_element_type=jnp.float32) + lax.dot_general(
            b_im, second, nt, preferred_element_type=jnp.float32
        )
        both = both.astype(jnp.bfloat16)
        at = (place_ref[1] + XS - d) % XS
        out_ref[:, 0, :, at, 0] = both[:, :mu].reshape(shape)
        out_ref[:, 0, :, at, 1] = both[:, mu:].reshape(shape)


def make_pairs(place, lefts, right):
    _, _, mu, orbitals = lefts[0].shape
    nus = right.shape[4]
    one = (2, 1, mu, orbitals)
    left_specs = [pl.BlockSpec(one, lambda side, place: (0, place[1], 0, 0))]
    left_specs += [pl.BlockSpec(one, lambda side, place: (0, 0, 0, 0))] * (XS - 1)
    return pl.pallas_call(
        pairs_kernel,
        grid_spec=pltpu.PrefetchScalarGridSpec(
            num_scalar_prefetch=1,
            grid=(2,),
            in_specs=left_specs
            + [pl.BlockSpec((XS, ZQ, 2, 1, nus, orbitals), lambda side, place: (0, 0, 0, side, 0, 0))],
            out_specs=pl.BlockSpec(
                (XS, 1, ZQ // 2, XS, 2, 2 * nus, mu), lambda side, place: (0, (place[0] + side) % ZH, 0, 0, 0, 0, 0)
            ),
        ),
        out_shape=jax.ShapeDtypeStruct((XS, ZH, ZQ // 2, XS, 2, 2 * nus, mu), jnp.bfloat16),
        compiler_params=VMEM,
        cost_estimate=pl.CostEstimate(
            flops=16 * XS * XS * ZQ * nus * mu * orbitals, bytes_accessed=3 << 20, transcendentals=0
        ),
        name="pairs",
    )(place, *lefts, right)


def dft4(values, sign):
    (r0, i0), (r1, i1), (r2, i2), (r3, i3) = values
    ar, ai, br, bi = r0 + r2, i0 + i2, r0 - r2, i0 - i2
    cr, ci, dr, di = r1 + r3, i1 + i3, r1 - r3, i1 - i3
    if sign < 0:
        return [(ar + cr, ai + ci), (br + di, bi - dr), (ar - cr, ai - ci), (br - di, bi + dr)]
    return [(ar + cr, ai + ci), (br - di, bi + dr), (ar - cr, ai - ci), (br + di, bi - dr)]


def dft16(values, sign):
    out = list(values)
    for slow in range(4):
        out[4 * slow : 4 * slow + 4] = dft4(out[4 * slow : 4 * slow + 4], sign)
    for fast in range(4):
        out[fast::4] = dft4(out[fast::4], sign)
    return out


def spectral_kernel(x_ref, c_ref, out_ref, work_ref):
    for top in range(4):
        values = [
            tuple(x_ref[16 * top + low, part].astype(jnp.float32) for part in range(2)) for low in range(16)
        ]
        for low, (re, im) in enumerate(dft16(values, -1)):
            work_ref[0, 16 * top + low] = re
            work_ref[1, 16 * top + low] = im
    for low in range(16):
        values = [(work_ref[0, 16 * top + low], work_ref[1, 16 * top + low]) for top in range(4)]
        weighted = []
        for top, (re, im) in enumerate(dft4(values, -1)):
            c = c_ref[16 * top + low].astype(jnp.float32)
            weighted.append(tuple((c * part).astype(jnp.bfloat16).astype(jnp.float32) for part in (re, im)))
        for top, (re, im) in enumerate(dft4(weighted, 1)):
            work_ref[0, 16 * top + low] = re
            work_ref[1, 16 * top + low] = im
    for top in range(4):
        values = [(work_ref[0, 16 * top + low], work_ref[1, 16 * top + low]) for low in range(16)]
        for low, parts in enumerate(dft16(values, 1)):
            for part in range(2):
                out_ref[16 * top + low, part] = (parts[part] * (1.0 / 64.0)).astype(jnp.bfloat16)


def spectral(x, coulomb):
    count, _, nus, mu = x.shape
    rows = 16
    block = pl.BlockSpec((count, 2, rows, mu), lambda n: (0, 0, n, 0))
    return pl.pallas_call(
        spectral_kernel,
        grid=(nus // rows,),
        in_specs=[block, pl.BlockSpec((count, rows, mu), lambda n: (0, n, 0))],
        out_specs=block,
        out_shape=jax.ShapeDtypeStruct(x.shape, jnp.bfloat16),
        scratch_shapes=[pltpu.VMEM((2, count, rows, mu), jnp.float32)],
        compiler_params=VMEM,
        cost_estimate=pl.CostEstimate(flops=32 * count * nus * mu, bytes_accessed=5 << 19, transcendentals=0),
        name="spectral",
    )(x, coulomb)


def apply_kernel(place_ref, kernel_ref, *refs):
    rights, out_ref = refs[:XS], refs[XS]
    mu, orbitals = out_ref.shape[2:]
    tn = (((0,), (0,)), ((), ()))

    def product(right_ref):
        total = None
        for side in range(2):
            at = (place_ref[0] + side) % ZH
            k_re = kernel_ref[:, at, :, 0, 0].reshape(-1, mu)
            k_im = kernel_ref[:, at, :, 0, 1].reshape(-1, mu)
            b_re = right_ref[:, :, 0, side].reshape(-1, orbitals)
            b_im = right_ref[:, :, 1, side].reshape(-1, orbitals)
            first = jnp.concatenate([k_re, k_im], 1)
            second = jnp.concatenate([-k_im, k_re], 1)
            term = lax.dot_general(first, b_re, tn, preferred_element_type=jnp.float32) + lax.dot_general(
                second, b_im, tn, preferred_element_type=jnp.float32
            )
            total = term if total is None else total + term
        out_ref[0, 0] = total[:mu]
        out_ref[1, 0] = total[mu:]

    for d in range(XS):
        pl.when(pl.program_id(0) == d)(functools.partial(product, rights[d]))


def apply(place, kernel, rights):
    xs, zhs, pairs, kl, _, rows, mu = kernel.shape
    orbitals = rights[0].shape[-1]
    return pl.pallas_call(
        apply_kernel,
        grid_spec=pltpu.PrefetchScalarGridSpec(
            num_scalar_prefetch=1,
            grid=(XS,),
            in_specs=[
                pl.BlockSpec(
                    (xs, zhs, pairs, 1, 2, rows, mu), lambda d, place: (0, 0, 0, (place[1] + XS - d) % XS, 0, 0, 0)
                )
            ]
            + [pl.BlockSpec(rights[0].shape, lambda d, place: (0,) * 6)] * XS,
            out_specs=pl.BlockSpec((2, 1, mu, orbitals), lambda d, place: (0, (place[1] + XS - d) % XS, 0, 0)),
        ),
        out_shape=jax.ShapeDtypeStruct((2, kl, mu, orbitals), jnp.float32),
        compiler_params=VMEM,
        cost_estimate=pl.CostEstimate(
            flops=8 * kl * xs * zhs * pairs * rows * mu * orbitals, bytes_accessed=7 << 20, transcendentals=0
        ),
        name="apply",
    )(place, kernel, *rights)


def swap(blocks, axes):
    return lax.all_to_all(blocks, axes, split_axis=0, concat_axis=0, tiled=True)


def shift(block, d):
    return lax.ppermute(block, "x", [(i, (i + d) % XS) for i in range(XS)])


def on_device(left, right, coulomb):
    parts, kl, nus, orbitals = right.shape
    mu = left.shape[2]
    x = lax.axis_index("x")
    place = jnp.stack([lax.axis_index("zh"), x]).astype(jnp.int32)
    sides = jnp.stack([right, lax.ppermute(right, "zh", [(0, 1), (1, 0)])], 2)
    sides = jnp.broadcast_to(sides.transpose(1, 0, 2, 3, 4)[:, None], (kl, ZQ, parts, 2, nus, orbitals))
    mine = swap(sides.reshape(kl * ZQ, parts, 2, nus, orbitals), ("x", "zq"))
    mine = mine.reshape(XS, ZQ, parts, 2, nus, orbitals)
    lefts = [left]
    for d in range(1, XS):
        block = lax.dynamic_slice_in_dim(left, (x + d) % XS, 1, 1)
        lefts.append(shift(block, d))
    pairs = make_pairs(place, lefts, mine)
    rights = [mine] + [shift(mine, d) for d in range(1, XS)]
    columns = swap(pairs.reshape(KG * XS, parts, 2 * nus, mu), ("kg", "x"))
    columns, rights[1], rights[3] = lax.optimization_barrier((columns, rights[1], rights[3]))
    kernel = swap(spectral(columns, coulomb).reshape(KG, KL, parts, 2 * nus, mu), "kg")
    return apply(place, kernel.reshape(XS, ZH, ZQ // 2, KL, parts, 2 * nus, mu), rights)


def solution(mesh):
    split = Mesh(mesh.devices.reshape(KG, XS, ZH, ZQ), ("kg", "x", "zh", "zq"))
    points = ("x", "zh", "zq")
    in_specs = (P(None, "kg", points, None), P(None, "kg", points, None), P(None, "kg", points))
    out_specs = P(None, "kg", points, None)
    return jax.shard_map(on_device, mesh=split, in_specs=in_specs, out_specs=out_specs, check_vma=False)
```

time: 216 us -> 198 us (0.917)
  waiting for transfers between devices: 143 us -> 124 us
  between operations: 13.5 us -> 0.1 us
  starting transfers between devices: 45.6 us -> 55.9 us
    all_to_all x4 -> x3, waiting for transfers between devices: 133 us -> 45.5 us  [swap(): return lax.all_to_all(blocks, axes, split_axis=0, concat_axis=0, tiled=True)]
    ppermute x0 -> x6, waiting for transfers between devices: none -> 69.1 us  [shift(): return lax.ppermute(block, 'x', [(i, (i + d) % XS) for i in range(XS)])]
    ppermute x0 -> x6, starting transfers between devices: none -> 18.5 us  [shift(): return lax.ppermute(block, 'x', [(i, (i + d) % XS) for i in range(XS)])]
    all_to_all x4 -> x3, starting transfers between devices: 36.8 us -> 28.6 us  [swap(): return lax.all_to_all(blocks, axes, split_axis=0, concat_axis=0, tiled=True)]
    unnamed x9 -> x12, local copies, waits for them, and re-layouts: 4.5 us -> 5.46 us
  transfers between devices with their start and end apart: 6 -> 10, of which waited for: 4 -> 9; matrix products, arithmetic and copies ran while one was open for 0% -> 0% of each run, Pallas kernels for 1% -> 0%
where the time goes in v3:
time: 198 us; the launch traced here: 197 us
  waiting for transfers between devices  124 us (63%)
  starting transfers between devices  55.9 us (28%)
  Pallas kernels  9.12 us (5%)
  local copies, waits for them, and re-layouts  7.33 us (4%)
    ppermute x6, waiting for transfers between devices, shift(): return lax.ppermute(block, 'x', [(i, (i + d) % XS) for i in range(XS)])  69.1 us
    all_to_all x3, waiting for transfers between devices, swap(): return lax.all_to_all(blocks, axes, split_axis=0, concat_axis=0, tiled=True)  45.5 us
    all_to_all x3, starting transfers between devices, swap(): return lax.all_to_all(blocks, axes, split_axis=0, concat_axis=0, tiled=True)  28.6 us
    ppermute x6, starting transfers between devices, shift(): return lax.ppermute(block, 'x', [(i, (i + d) % XS) for i in range(XS)])  18.5 us
    ppermute x1, waiting for transfers between devices, on_device(): sides = jnp.stack([right, lax.ppermute(right, 'zh', [(0, 1), (1, 0)])], 2)  9.08 us
    ppermute x1, starting transfers between devices, on_device(): sides = jnp.stack([right, lax.ppermute(right, 'zh', [(0, 1), (1, 0)])], 2)  8.8 us
    unnamed x12, local copies, waits for them, and re-layouts  5.46 us
  transfers between devices with their start and end apart: 10, of which 9 were waited for; matrix products, arithmetic and copies ran while one was open for 0% of the time, Pallas kernels for 0%

profile of v3, /device:TPU:33, one launch (start us, length us, event | category | flops | bytes accessed | tf_op | source)
XLA Modules:
  0.0 197.1 jit_solution(4578328263405139670)
XLA Ops:
  0.0 8.8 %collective-permute-start.3 = (bf16[2,4,16,512]{3,2,1,0:T(8,128)(2,1)}, bf16[2,4,16,512]{3,2,1,0:T(8,128)(2,1)S(1)}, u32[]{:S(2)}, u32[]{:S(2)}) collective-permute-start(bf16[2,4,16,512]{3,2,1,0:T(8,128)(2,1)} %param.4), channel_id=1, source_target_pairs={{0,4},{4,0},{1,5},{5,1},{2,6},{6,2},{3,7},{7,3},{8,12},{12,8},{9,1... | collective-permute-start | bytes 393224 | tf_op jit(solution)/shard_map/ppermute | solution.py:184
  8.8 9.1 %collective-permute-done.3 = bf16[2,4,16,512]{3,2,1,0:T(8,128)(2,1)S(1)} collective-permute-done((bf16[2,4,16,512]{3,2,1,0:T(8,128)(2,1)}, bf16[2,4,16,512]{3,2,1,0:T(8,128)(2,1)S(1)}, u32[]{:S(2)}, u32[]{:S(2)}) %collective-permute-start.3) | collective-permute-done | bytes 131104 | tf_op jit(solution)/shard_map/ppermute | solution.py:184
  17.9 0.9 maximum_bitcast_fusion
  18.8 0.0 copy-start.4
  18.9 1.1 broadcast_in_dim.2
  20.0 9.4 %all-to-all-start = ((bf16[16,2,2,16,512]{4,3,2,1,0:T(8,128)(2,1)}), bf16[16,2,2,16,512]{4,3,2,1,0:T(8,128)(2,1)S(1)}, u32[]{:S(2)}, u32[]{:S(2)}) async-start(bf16[16,2,2,16,512]{4,3,2,1,0:T(8,128)(2,1)} %bitcast.5), calls=%async_computation | async-start | bytes 2097152 | tf_op jit(solution)/shard_map/all_to_all | solution.py:172
  29.4 0.0 copy-done.4
  29.4 0.8 constant_dynamic-slice_fusion
  30.1 4.3 %collective-permute-start.2 = (bf16[2,1,128,512]{3,2,1,0:T(8,128)(2,1)}, bf16[2,1,128,512]{3,2,1,0:T(8,128)(2,1)S(1)}, u32[]{:S(2)}, u32[]{:S(2)}) collective-permute-start(bf16[2,1,128,512]{3,2,1,0:T(8,128)(2,1)} %get-tuple-element.11), channel_id=1, source_target_pairs={{0,24},{8,0},{16,8},{24,16},{1,25},{9,1},{17,9},{25,17},{2,26},{10... | collective-permute-start | bytes 786440 | tf_op jit(solution)/shard_map/ppermute | solution.py:176
  34.4 2.5 %collective-permute-start.1 = (bf16[2,1,128,512]{3,2,1,0:T(8,128)(2,1)S(1)}, bf16[2,1,128,512]{3,2,1,0:T(8,128)(2,1)S(1)}, u32[]{:S(2)}, u32[]{:S(2)}) collective-permute-start(bf16[2,1,128,512]{3,2,1,0:T(8,128)(2,1)S(1)} %get-tuple-element.12), channel_id=1, source_target_pairs={{0,16},{8,24},{16,0},{24,8},{1,17},{9,25},{17,1},{25,9},{2,18},{10... | collective-permute-start | bytes 786440 | tf_op jit(solution)/shard_map/ppermute | solution.py:176
  36.9 2.5 %collective-permute-start = (bf16[2,1,128,512]{3,2,1,0:T(8,128)(2,1)S(1)}, bf16[2,1,128,512]{3,2,1,0:T(8,128)(2,1)S(1)}, u32[]{:S(2)}, u32[]{:S(2)}) collective-permute-start(bf16[2,1,128,512]{3,2,1,0:T(8,128)(2,1)S(1)} %get-tuple-element.13), channel_id=1, source_target_pairs={{0,8},{8,16},{16,24},{24,0},{1,9},{9,17},{17,25},{25,1},{2,10},{10... | collective-permute-start | bytes 786440 | tf_op jit(solution)/shard_map/ppermute | solution.py:176
  39.4 0.1 pad_add_fusion.place_ref
  39.5 3.6 %collective-permute-done.2.refs_3_ = bf16[2,1,128,512]{3,2,1,0:T(8,128)(2,1)S(1)} collective-permute-done((bf16[2,1,128,512]{3,2,1,0:T(8,128)(2,1)}, bf16[2,1,128,512]{3,2,1,0:T(8,128)(2,1)S(1)}, u32[]{:S(2)}, u32[]{:S(2)}) %collective-permute-start.2) | collective-permute-done | bytes 262176 | tf_op jit(solution)/shard_map/ppermute | solution.py:176
  43.1 4.4 %collective-permute-done.1.refs_2_ = bf16[2,1,128,512]{3,2,1,0:T(8,128)(2,1)S(1)} collective-permute-done((bf16[2,1,128,512]{3,2,1,0:T(8,128)(2,1)S(1)}, bf16[2,1,128,512]{3,2,1,0:T(8,128)(2,1)S(1)}, u32[]{:S(2)}, u32[]{:S(2)}) %collective-permute-start.1) | collective-permute-done | bytes 262176 | tf_op jit(solution)/shard_map/ppermute | solution.py:176
  47.5 10.6 %collective-permute-done.refs_1_ = bf16[2,1,128,512]{3,2,1,0:T(8,128)(2,1)S(1)} collective-permute-done((bf16[2,1,128,512]{3,2,1,0:T(8,128)(2,1)S(1)}, bf16[2,1,128,512]{3,2,1,0:T(8,128)(2,1)S(1)}, u32[]{:S(2)}, u32[]{:S(2)}) %collective-permute-start) | collective-permute-done | bytes 262176 | tf_op jit(solution)/shard_map/ppermute | solution.py:176
  58.1 0.0 all-to-all-done
  58.1 3.0 %pairs.1 = bf16[4,2,2,4,2,32,128]{6,5,4,3,2,1,0:T(8,128)(2,1)} custom-call(s32[2]{0:T(128)S(1)} %pad_add_fusion.place_ref, bf16[2,4,128,512]{3,2,1,0:T(8,128)(2,1)S(1)} %copy-done.4, bf16[2,1,128,512]{3,2,1,0:T(8,128)(2,1)S(1)} %collective-permute-done.refs_1_, bf16[2,1,128,512]{3,2,1,0:T(8,128)(2,1)S(1)} %collective-permute-done.1.refs_2_, ...), custom_call_target="tpu_custom_call" | custom-call | flops 1073741824 | bytes 3145728 | tf_op jit(solution)/shard_map/pairs/pallas_call | solution.py:41
  61.2 15.1 %all-to-all-start.1 = ((bf16[64,2,32,128]{3,2,1,0:T(8,128)(2,1)}), bf16[64,2,32,128]{3,2,1,0:T(8,128)(2,1)S(1)}, u32[]{:S(2)}, u32[]{:S(2)}) async-start(bf16[64,2,32,128]{3,2,1,0:T(8,128)(2,1)} %bitcast.7), calls=%async_computation.1 | async-start | bytes 2097152 | tf_op jit(solution)/shard_map/all_to_all | solution.py:172
  76.2 4.5 %collective-permute-start.5 = (bf16[4,4,2,2,16,512]{5,4,3,2,1,0:T(8,128)(2,1)S(1)}, bf16[4,4,2,2,16,512]{5,4,3,2,1,0:T(8,128)(2,1)S(1)}, u32[]{:S(2)}, u32[]{:S(2)}) collective-permute-start(bf16[4,4,2,2,16,512]{5,4,3,2,1,0:T(8,128)(2,1)S(1)} %bitcast.12), channel_id=1, source_target_pairs={{0,24},{8,0},{16,8},{24,16},{1,25},{9,1},{17,9},{25,17},{2,26},{10... | collective-permute-start | bytes 3145736 | tf_op jit(solution)/shard_map/ppermute | solution.py:176
  80.8 1.9 collective-permute-start.4
  82.7 23.6 %collective-permute-done.5.refs_3_ = bf16[4,4,2,2,16,512]{5,4,3,2,1,0:T(8,128)(2,1)S(1)} collective-permute-done((bf16[4,4,2,2,16,512]{5,4,3,2,1,0:T(8,128)(2,1)S(1)}, bf16[4,4,2,2,16,512]{5,4,3,2,1,0:T(8,128)(2,1)S(1)}, u32[]{:S(2)}, u32[]{:S(2)}) %collective-permute-start.5) | collective-permute-done | bytes 1048608 | tf_op jit(solution)/shard_map/ppermute | solution.py:176
  106.3 1.7 collective-permute-done.4.refs_1_
  108.1 0.0 copy-start
  108.1 1.0 copy-done
  109.0 27.2 %all-to-all-done.1.x_ref = bf16[64,2,32,128]{3,2,1,0:T(8,128)(2,1)S(1)} async-done(((bf16[64,2,32,128]{3,2,1,0:T(8,128)(2,1)}), bf16[64,2,32,128]{3,2,1,0:T(8,128)(2,1)S(1)}, u32[]{:S(2)}, u32[]{:S(2)}) %all-to-all-start.1) | async-done | bytes 1048608 | tf_op jit(solution)/shard_map/all_to_all | solution.py:172
  136.2 0.0 copy-start.5
  136.2 1.0 copy-done.5
  137.3 2.4 %spectral.1 = bf16[64,2,32,128]{3,2,1,0:T(8,128)(2,1)} custom-call(bf16[64,2,32,128]{3,2,1,0:T(8,128)(2,1)S(1)} %all-to-all-done.1.x_ref, bf16[64,32,128]{2,1,0:T(8,128)(2,1)S(1)} %copy-done.5), custom_call_target="tpu_custom_call" | custom-call | flops 8388608 | bytes 2621440 | tf_op jit(solution)/shard_map/spectral/pallas_call | solution.py:107
  139.7 4.1 %all-to-all-start.2 = ((bf16[16,4,2,32,128]{4,3,2,1,0:T(8,128)(2,1)}), bf16[16,4,2,32,128]{4,3,2,1,0:T(8,128)(2,1)S(1)}, u32[]{:S(2)}, u32[]{:S(2)}) async-start(bf16[16,4,2,32,128]{4,3,2,1,0:T(8,128)(2,1)} %bitcast.8), calls=%async_computation.2 | async-start | bytes 2097152 | tf_op jit(solution)/shard_map/all_to_all | solution.py:172
  143.8 2.8 %collective-permute-start.6 = (bf16[4,4,2,2,16,512]{5,4,3,2,1,0:T(8,128)(2,1)S(1)}, bf16[4,4,2,2,16,512]{5,4,3,2,1,0:T(8,128)(2,1)S(1)}, u32[]{:S(2)}, u32[]{:S(2)}) collective-permute-start(bf16[4,4,2,2,16,512]{5,4,3,2,1,0:T(8,128)(2,1)S(1)} %bitcast.14), channel_id=1, source_target_pairs={{0,16},{8,24},{16,0},{24,8},{1,17},{9,25},{17,1},{25,9},{2,18},{10... | collective-permute-start | bytes 3145736 | tf_op jit(solution)/shard_map/ppermute | solution.py:176
  146.6 25.1 %collective-permute-done.6.refs_2_ = bf16[4,4,2,2,16,512]{5,4,3,2,1,0:T(8,128)(2,1)S(1)} collective-permute-done((bf16[4,4,2,2,16,512]{5,4,3,2,1,0:T(8,128)(2,1)S(1)}, bf16[4,4,2,2,16,512]{5,4,3,2,1,0:T(8,128)(2,1)S(1)}, u32[]{:S(2)}, u32[]{:S(2)}) %collective-permute-start.6) | collective-permute-done | bytes 1048608 | tf_op jit(solution)/shard_map/ppermute | solution.py:176
  171.7 0.0 copy-start.2
  171.7 1.0 copy-done.2
  172.7 18.2 %all-to-all-done.2 = bf16[16,4,2,32,128]{4,3,2,1,0:T(8,128)(2,1)S(1)} async-done(((bf16[16,4,2,32,128]{4,3,2,1,0:T(8,128)(2,1)}), bf16[16,4,2,32,128]{4,3,2,1,0:T(8,128)(2,1)S(1)}, u32[]{:S(2)}, u32[]{:S(2)}) %all-to-all-start.2) | async-done | bytes 1048608 | tf_op jit(solution)/shard_map/all_to_all | solution.py:172
  190.9 0.0 copy-start.1
  190.9 1.2 copy-done.1
  192.2 0.0 copy-start.3
  192.2 1.2 copy-done.3
  193.4 3.7 %apply.1 = f32[2,4,128,512]{3,2,1,0:T(8,128)} custom-call(s32[2]{0:T(128)S(1)} %pad_add_fusion.place_ref, bf16[4,2,2,4,2,32,128]{6,5,4,3,2,1,0:T(8,128)(2,1)S(1)} %bitcast.16, bf16[4,4,2,2,16,512]{5,4,3,2,1,0:T(8,128)(2,1)S(1)} %bitcast.15, bf16[4,4,2,2,16,512]{5,4,3,2,1,0:T(8,128)(2,1)S(1)} %copy-done.1, bf16[4,4,2,2,16,512]{5,4,3,2,1,0:T(8,128)(2,1)S(1)} %copy-done.3, ...), custom_call_target="tpu_custom_call" | custom-call | flops 1073741824 | bytes 7340032 | tf_op jit(solution)/shard_map/apply/pallas_call | solution.py:149
  (1 shorter events, 0.0 us)
Async XLA Ops:
  0.0 17.9 %collective-permute-start.3 = (bf16[2,4,16,512]{3,2,1,0:T(8,128)(2,1)}, bf16[2,4,16,512]{3,2,1,0:T(8,128)(2,1)S(1)}, u32[]{:S(2)}, u32[]{:S(2)}) collective-permute-start(bf16[2,4,16,512]{3,2,1,0:T(8,128)(2,1)} %param.4), channel_id=1, source_target_pairs={{0,4},{4,0},{1,5},{5,1},{2,6},{6,2},{3,7},{7,3},{8,12},{12,8},{9,1... | collective-permute-start | bytes 393224 | tf_op jit(solution)/shard_map/ppermute | solution.py:184
  18.8 10.6 %copy-start.4 = (bf16[2,4,128,512]{3,2,1,0:T(8,128)(2,1)S(1)}, bf16[2,4,128,512]{3,2,1,0:T(8,128)(2,1)}, u32[]{:S(2)}) copy-start(bf16[2,4,128,512]{3,2,1,0:T(8,128)(2,1)} %refs_0_.1) | copy-start | bytes 3145732
  20.0 38.2 %all-to-all-start = ((bf16[16,2,2,16,512]{4,3,2,1,0:T(8,128)(2,1)}), bf16[16,2,2,16,512]{4,3,2,1,0:T(8,128)(2,1)S(1)}, u32[]{:S(2)}, u32[]{:S(2)}) async-start(bf16[16,2,2,16,512]{4,3,2,1,0:T(8,128)(2,1)} %bitcast.5), calls=%async_computation | async-start | bytes 2097152 | tf_op jit(solution)/shard_map/all_to_all | solution.py:172
  30.1 13.0 %collective-permute-start.2 = (bf16[2,1,128,512]{3,2,1,0:T(8,128)(2,1)}, bf16[2,1,128,512]{3,2,1,0:T(8,128)(2,1)S(1)}, u32[]{:S(2)}, u32[]{:S(2)}) collective-permute-start(bf16[2,1,128,512]{3,2,1,0:T(8,128)(2,1)} %get-tuple-element.11), channel_id=1, source_target_pairs={{0,24},{8,0},{16,8},{24,16},{1,25},{9,1},{17,9},{25,17},{2,26},{10... | collective-permute-start | bytes 786440 | tf_op jit(solution)/shard_map/ppermute | solution.py:176
  34.4 13.1 %collective-permute-start.1 = (bf16[2,1,128,512]{3,2,1,0:T(8,128)(2,1)S(1)}, bf16[2,1,128,512]{3,2,1,0:T(8,128)(2,1)S(1)}, u32[]{:S(2)}, u32[]{:S(2)}) collective-permute-start(bf16[2,1,128,512]{3,2,1,0:T(8,128)(2,1)S(1)} %get-tuple-element.12), channel_id=1, source_target_pairs={{0,16},{8,24},{16,0},{24,8},{1,17},{9,25},{17,1},{25,9},{2,18},{10... | collective-permute-start | bytes 786440 | tf_op jit(solution)/shard_map/ppermute | solution.py:176
  36.9 21.2 %collective-permute-start = (bf16[2,1,128,512]{3,2,1,0:T(8,128)(2,1)S(1)}, bf16[2,1,128,512]{3,2,1,0:T(8,128)(2,1)S(1)}, u32[]{:S(2)}, u32[]{:S(2)}) collective-permute-start(bf16[2,1,128,512]{3,2,1,0:T(8,128)(2,1)S(1)} %get-tuple-element.13), channel_id=1, source_target_pairs={{0,8},{8,16},{16,24},{24,0},{1,9},{9,17},{17,25},{25,1},{2,10},{10... | collective-permute-start | bytes 786440 | tf_op jit(solution)/shard_map/ppermute | solution.py:176
  61.2 75.1 %all-to-all-start.1 = ((bf16[64,2,32,128]{3,2,1,0:T(8,128)(2,1)}), bf16[64,2,32,128]{3,2,1,0:T(8,128)(2,1)S(1)}, u32[]{:S(2)}, u32[]{:S(2)}) async-start(bf16[64,2,32,128]{3,2,1,0:T(8,128)(2,1)} %bitcast.7), calls=%async_computation.1 | async-start | bytes 2097152 | tf_op jit(solution)/shard_map/all_to_all | solution.py:172
  76.2 30.1 %collective-permute-start.5 = (bf16[4,4,2,2,16,512]{5,4,3,2,1,0:T(8,128)(2,1)S(1)}, bf16[4,4,2,2,16,512]{5,4,3,2,1,0:T(8,128)(2,1)S(1)}, u32[]{:S(2)}, u32[]{:S(2)}) collective-permute-start(bf16[4,4,2,2,16,512]{5,4,3,2,1,0:T(8,128)(2,1)S(1)} %bitcast.12), channel_id=1, source_target_pairs={{0,24},{8,0},{16,8},{24,16},{1,25},{9,1},{17,9},{25,17},{2,26},{10... | collective-permute-start | bytes 3145736 | tf_op jit(solution)/shard_map/ppermute | solution.py:176
  80.8 27.3 %collective-permute-start.4 = (bf16[4,4,2,2,16,512]{5,4,3,2,1,0:T(8,128)(2,1)S(1)}, bf16[4,4,2,2,16,512]{5,4,3,2,1,0:T(8,128)(2,1)S(1)}, u32[]{:S(2)}, u32[]{:S(2)}) collective-permute-start(bf16[4,4,2,2,16,512]{5,4,3,2,1,0:T(8,128)(2,1)S(1)} %bitcast.13), channel_id=1, source_target_pairs={{0,8},{8,16},{16,24},{24,0},{1,9},{9,17},{17,25},{25,1},{2,10},{10... | collective-permute-start | bytes 3145736 | tf_op jit(solution)/shard_map/ppermute | solution.py:176
  108.1 1.0 copy-start
  136.2 1.0 copy-start.5
  139.7 51.3 %all-to-all-start.2 = ((bf16[16,4,2,32,128]{4,3,2,1,0:T(8,128)(2,1)}), bf16[16,4,2,32,128]{4,3,2,1,0:T(8,128)(2,1)S(1)}, u32[]{:S(2)}, u32[]{:S(2)}) async-start(bf16[16,4,2,32,128]{4,3,2,1,0:T(8,128)(2,1)} %bitcast.8), calls=%async_computation.2 | async-start | bytes 2097152 | tf_op jit(solution)/shard_map/all_to_all | solution.py:172
  143.8 27.9 %collective-permute-start.6 = (bf16[4,4,2,2,16,512]{5,4,3,2,1,0:T(8,128)(2,1)S(1)}, bf16[4,4,2,2,16,512]{5,4,3,2,1,0:T(8,128)(2,1)S(1)}, u32[]{:S(2)}, u32[]{:S(2)}) collective-permute-start(bf16[4,4,2,2,16,512]{5,4,3,2,1,0:T(8,128)(2,1)S(1)} %bitcast.14), channel_id=1, source_target_pairs={{0,16},{8,24},{16,0},{24,8},{1,17},{9,25},{17,1},{25,9},{2,18},{10... | collective-permute-start | bytes 3145736 | tf_op jit(solution)/shard_map/ppermute | solution.py:176
  171.7 1.0 copy-start.2
  190.9 1.2 copy-start.1
  192.2 1.2 copy-start.3

commit v4 on v3

--- a/solution.py
+++ b/solution.py
@@ -9,7 +9,7 @@
 
 XS, ZH, ZQ = 4, 2, 4
 KG, KL = 16, 4
-VMEM = pltpu.CompilerParams(vmem_limit_bytes=48 << 20)
+VMEM = pltpu.CompilerParams(vmem_limit_bytes=24 << 20)
 
 
 def pairs_kernel(place_ref, *refs):
@@ -117,19 +117,21 @@
     )(x, coulomb)
 
 
-def apply_kernel(place_ref, kernel_ref, *refs):
-    rights, out_ref = refs[:XS], refs[XS]
+def apply_kernel(sizes, place_ref, kernel_ref, *refs):
+    out_ref = refs[-1]
     mu, orbitals = out_ref.shape[2:]
     tn = (((0,), (0,)), ((), ()))
 
-    def product(right_ref):
+    def product(pieces):
         total = None
         for side in range(2):
             at = (place_ref[0] + side) % ZH
             k_re = kernel_ref[:, at, :, 0, 0].reshape(-1, mu)
             k_im = kernel_ref[:, at, :, 0, 1].reshape(-1, mu)
-            b_re = right_ref[:, :, 0, side].reshape(-1, orbitals)
-            b_im = right_ref[:, :, 1, side].reshape(-1, orbitals)
+            b_re, b_im = (
+                jnp.concatenate([piece[:, :, part, side].reshape(-1, orbitals) for piece in pieces], 0)
+                for part in range(2)
+            )
             first = jnp.concatenate([k_re, k_im], 1)
             second = jnp.concatenate([-k_im, k_re], 1)
             term = lax.dot_general(first, b_re, tn, preferred_element_type=jnp.float32) + lax.dot_general(
@@ -140,14 +142,16 @@
         out_ref[1, 0] = total[mu:]
 
     for d in range(XS):
-        pl.when(pl.program_id(0) == d)(functools.partial(product, rights[d]))
+        begin = sum(sizes[:d])
+        pl.when(pl.program_id(0) == d)(functools.partial(product, refs[begin : begin + sizes[d]]))
 
 
 def apply(place, kernel, rights):
     xs, zhs, pairs, kl, _, rows, mu = kernel.shape
-    orbitals = rights[0].shape[-1]
+    flat = [piece for pieces in rights for piece in pieces]
+    orbitals = flat[0].shape[-1]
     return pl.pallas_call(
-        apply_kernel,
+        functools.partial(apply_kernel, [len(pieces) for pieces in rights]),
         grid_spec=pltpu.PrefetchScalarGridSpec(
             num_scalar_prefetch=1,
             grid=(XS,),
@@ -156,7 +160,7 @@
                     (xs, zhs, pairs, 1, 2, rows, mu), lambda d, place: (0, 0, 0, (place[1] + XS - d) % XS, 0, 0, 0)
                 )
             ]
-            + [pl.BlockSpec(rights[0].shape, lambda d, place: (0,) * 6)] * XS,
+            + [pl.BlockSpec(piece.shape, lambda d, place: (0,) * 6) for piece in flat],
             out_specs=pl.BlockSpec((2, 1, mu, orbitals), lambda d, place: (0, (place[1] + XS - d) % XS, 0, 0)),
         ),
         out_shape=jax.ShapeDtypeStruct((2, kl, mu, orbitals), jnp.float32),
@@ -165,7 +169,7 @@
             flops=8 * kl * xs * zhs * pairs * rows * mu * orbitals, bytes_accessed=7 << 20, transcendentals=0
         ),
         name="apply",
-    )(place, kernel, *rights)
+    )(place, kernel, *flat)
 
 
 def swap(blocks, axes):
@@ -190,9 +194,10 @@
         block = lax.dynamic_slice_in_dim(left, (x + d) % XS, 1, 1)
         lefts.append(shift(block, d))
     pairs = make_pairs(place, lefts, mine)
-    rights = [mine] + [shift(mine, d) for d in range(1, XS)]
     columns = swap(pairs.reshape(KG * XS, parts, 2 * nus, mu), ("kg", "x"))
-    columns, rights[1], rights[3] = lax.optimization_barrier((columns, rights[1], rights[3]))
+    low, high = mine[: XS // 2], mine[XS // 2 :]
+    columns, up, down = lax.optimization_barrier((columns, shift(low, 1), shift(high, XS - 1)))
+    rights = [[mine], [up, shift(high, 1)], [shift(up, 1), shift(down, XS - 1)], [shift(low, XS - 1), down]]
     kernel = swap(spectral(columns, coulomb).reshape(KG, KL, parts, 2 * nus, mu), "kg")
     return apply(place, kernel.reshape(XS, ZH, ZQ // 2, KL, parts, 2 * nus, mu), rights)
 

time: 198 us -> 190 us (0.960)
  waiting for transfers between devices: 124 us -> 105 us
  starting transfers between devices: 55.9 us -> 65.2 us
    ppermute x6 -> x9, waiting for transfers between devices: 69.1 us -> 50.1 us  [shift(): return lax.ppermute(block, 'x', [(i, (i + d) % XS) for i in range(XS)])]
    ppermute x6 -> x9, starting transfers between devices: 18.5 us -> 27.5 us  [shift(): return lax.ppermute(block, 'x', [(i, (i + d) % XS) for i in range(XS)])]
    unnamed x12 -> x20, local copies, waits for them, and re-layouts: 5.46 us -> 5.54 us
  transfers between devices with their start and end apart: 10 -> 13, of which waited for: 9 -> 10; matrix products, arithmetic and copies ran while one was open for 0% -> 0% of each run, Pallas kernels for 0% -> 0%
where the time goes in v4:
time: 190 us; the launch traced here: 189 us
  waiting for transfers between devices  105 us (55%)
  starting transfers between devices  65.2 us (34%)
  Pallas kernels  10.2 us (5%)
  local copies, waits for them, and re-layouts  7.49 us (4%)
    ppermute x9, waiting for transfers between devices, shift(): return lax.ppermute(block, 'x', [(i, (i + d) % XS) for i in range(XS)])  50.1 us
    all_to_all x3, waiting for transfers between devices, swap(): return lax.all_to_all(blocks, axes, split_axis=0, concat_axis=0, tiled=True)  45.6 us
    all_to_all x3, starting transfers between devices, swap(): return lax.all_to_all(blocks, axes, split_axis=0, concat_axis=0, tiled=True)  28.9 us
    ppermute x9, starting transfers between devices, shift(): return lax.ppermute(block, 'x', [(i, (i + d) % XS) for i in range(XS)])  27.5 us
    ppermute x1, waiting for transfers between devices, on_device(): sides = jnp.stack([right, lax.ppermute(right, 'zh', [(0, 1), (1, 0)])], 2)  9.08 us
    ppermute x1, starting transfers between devices, on_device(): sides = jnp.stack([right, lax.ppermute(right, 'zh', [(0, 1), (1, 0)])], 2)  8.8 us
    unnamed x20, local copies, waits for them, and re-layouts  5.54 us
    pallas_call x1, Pallas kernels, apply(): pl.pallas_call(functools.partial(apply_kernel, [len(pieces) for pieces in...  4.74 us
  transfers between devices with their start and end apart: 13, of which 10 were waited for; matrix products, arithmetic and copies ran while one was open for 0% of the time, Pallas kernels for 0%

profile of v4, /device:TPU:33, one launch (start us, length us, event | category | flops | bytes accessed | tf_op | source)
XLA Modules:
  0.0 188.9 jit_solution(16183097280779712474)
XLA Ops:
  0.0 8.8 %collective-permute-start.3 = (bf16[2,4,16,512]{3,2,1,0:T(8,128)(2,1)}, bf16[2,4,16,512]{3,2,1,0:T(8,128)(2,1)S(1)}, u32[]{:S(2)}, u32[]{:S(2)}) collective-permute-start(bf16[2,4,16,512]{3,2,1,0:T(8,128)(2,1)} %param.4), channel_id=1, source_target_pairs={{0,4},{4,0},{1,5},{5,1},{2,6},{6,2},{3,7},{7,3},{8,12},{12,8},{9,1... | collective-permute-start | bytes 393224 | tf_op jit(solution)/shard_map/ppermute | solution.py:188
  8.8 9.1 %collective-permute-done.3 = bf16[2,4,16,512]{3,2,1,0:T(8,128)(2,1)S(1)} collective-permute-done((bf16[2,4,16,512]{3,2,1,0:T(8,128)(2,1)}, bf16[2,4,16,512]{3,2,1,0:T(8,128)(2,1)S(1)}, u32[]{:S(2)}, u32[]{:S(2)}) %collective-permute-start.3) | collective-permute-done | bytes 131104 | tf_op jit(solution)/shard_map/ppermute | solution.py:188
  17.9 0.9 maximum_bitcast_fusion
  18.8 0.0 copy-start
  18.9 1.1 broadcast_in_dim.2
  20.0 9.4 %all-to-all-start = ((bf16[16,2,2,16,512]{4,3,2,1,0:T(8,128)(2,1)}), bf16[16,2,2,16,512]{4,3,2,1,0:T(8,128)(2,1)S(1)}, u32[]{:S(2)}, u32[]{:S(2)}) async-start(bf16[16,2,2,16,512]{4,3,2,1,0:T(8,128)(2,1)} %bitcast.5), calls=%async_computation | async-start | bytes 2097152 | tf_op jit(solution)/shard_map/all_to_all | solution.py:176
  29.4 0.0 copy-done
  29.4 0.8 constant_dynamic-slice_fusion
  30.1 4.3 %collective-permute-start.2 = (bf16[2,1,128,512]{3,2,1,0:T(8,128)(2,1)}, bf16[2,1,128,512]{3,2,1,0:T(8,128)(2,1)S(1)}, u32[]{:S(2)}, u32[]{:S(2)}) collective-permute-start(bf16[2,1,128,512]{3,2,1,0:T(8,128)(2,1)} %get-tuple-element.13), channel_id=1, source_target_pairs={{0,24},{8,0},{16,8},{24,16},{1,25},{9,1},{17,9},{25,17},{2,26},{10... | collective-permute-start | bytes 786440 | tf_op jit(solution)/shard_map/ppermute | solution.py:180
  34.4 2.5 %collective-permute-start.1 = (bf16[2,1,128,512]{3,2,1,0:T(8,128)(2,1)S(1)}, bf16[2,1,128,512]{3,2,1,0:T(8,128)(2,1)S(1)}, u32[]{:S(2)}, u32[]{:S(2)}) collective-permute-start(bf16[2,1,128,512]{3,2,1,0:T(8,128)(2,1)S(1)} %get-tuple-element.14), channel_id=1, source_target_pairs={{0,16},{8,24},{16,0},{24,8},{1,17},{9,25},{17,1},{25,9},{2,18},{10... | collective-permute-start | bytes 786440 | tf_op jit(solution)/shard_map/ppermute | solution.py:180
  36.9 2.5 %collective-permute-start = (bf16[2,1,128,512]{3,2,1,0:T(8,128)(2,1)S(1)}, bf16[2,1,128,512]{3,2,1,0:T(8,128)(2,1)S(1)}, u32[]{:S(2)}, u32[]{:S(2)}) collective-permute-start(bf16[2,1,128,512]{3,2,1,0:T(8,128)(2,1)S(1)} %get-tuple-element.15), channel_id=1, source_target_pairs={{0,8},{8,16},{16,24},{24,0},{1,9},{9,17},{17,25},{25,1},{2,10},{10... | collective-permute-start | bytes 786440 | tf_op jit(solution)/shard_map/ppermute | solution.py:180
  39.4 0.1 pad_add_fusion.place_ref
  39.5 3.6 %collective-permute-done.2.refs_3_ = bf16[2,1,128,512]{3,2,1,0:T(8,128)(2,1)S(1)} collective-permute-done((bf16[2,1,128,512]{3,2,1,0:T(8,128)(2,1)}, bf16[2,1,128,512]{3,2,1,0:T(8,128)(2,1)S(1)}, u32[]{:S(2)}, u32[]{:S(2)}) %collective-permute-start.2) | collective-permute-done | bytes 262176 | tf_op jit(solution)/shard_map/ppermute | solution.py:180
  43.1 4.4 %collective-permute-done.1.refs_2_ = bf16[2,1,128,512]{3,2,1,0:T(8,128)(2,1)S(1)} collective-permute-done((bf16[2,1,128,512]{3,2,1,0:T(8,128)(2,1)S(1)}, bf16[2,1,128,512]{3,2,1,0:T(8,128)(2,1)S(1)}, u32[]{:S(2)}, u32[]{:S(2)}) %collective-permute-start.1) | collective-permute-done | bytes 262176 | tf_op jit(solution)/shard_map/ppermute | solution.py:180
  47.5 10.6 %collective-permute-done.refs_1_ = bf16[2,1,128,512]{3,2,1,0:T(8,128)(2,1)S(1)} collective-permute-done((bf16[2,1,128,512]{3,2,1,0:T(8,128)(2,1)S(1)}, bf16[2,1,128,512]{3,2,1,0:T(8,128)(2,1)S(1)}, u32[]{:S(2)}, u32[]{:S(2)}) %collective-permute-start) | collective-permute-done | bytes 262176 | tf_op jit(solution)/shard_map/ppermute | solution.py:180
  58.1 0.0 all-to-all-done
  58.1 3.1 %pairs.1 = bf16[4,2,2,4,2,32,128]{6,5,4,3,2,1,0:T(8,128)(2,1)} custom-call(s32[2]{0:T(128)S(1)} %pad_add_fusion.place_ref, bf16[2,4,128,512]{3,2,1,0:T(8,128)(2,1)S(1)} %copy-done, bf16[2,1,128,512]{3,2,1,0:T(8,128)(2,1)S(1)} %collective-permute-done.refs_1_, bf16[2,1,128,512]{3,2,1,0:T(8,128)(2,1)S(1)} %collective-permute-done.1.refs_2_, ...), custom_call_target="tpu_custom_call" | custom-call | flops 1073741824 | bytes 3145728 | tf_op jit(solution)/shard_map/pairs/pallas_call | solution.py:41
  61.2 0.0 copy-start.1
  61.2 15.2 %all-to-all-start.1 = ((bf16[64,2,32,128]{3,2,1,0:T(8,128)(2,1)}), bf16[64,2,32,128]{3,2,1,0:T(8,128)(2,1)S(1)}, u32[]{:S(2)}, u32[]{:S(2)}) async-start(bf16[64,2,32,128]{3,2,1,0:T(8,128)(2,1)} %bitcast.7), calls=%async_computation.1 | async-start | bytes 2097152 | tf_op jit(solution)/shard_map/all_to_all | solution.py:176
  76.4 0.1 fusion
  76.5 0.0 copy-start.8
  76.5 0.0 copy-start.9
  76.5 3.3 %collective-permute-start.4 = (bf16[2,4,2,2,16,512]{5,4,3,2,1,0:T(8,128)(2,1)S(1)}, bf16[2,4,2,2,16,512]{5,4,3,2,1,0:T(8,128)(2,1)S(1)}, u32[]{:S(2)}, u32[]{:S(2)}) collective-permute-start(bf16[2,4,2,2,16,512]{5,4,3,2,1,0:T(8,128)(2,1)S(1)} %bitcast.18), channel_id=1, source_target_pairs={{0,8},{8,16},{16,24},{24,0},{1,9},{9,17},{17,25},{25,1},{2,10},{10... | collective-permute-start | bytes 1572872 | tf_op jit(solution)/shard_map/ppermute | solution.py:180
  79.8 3.2 %collective-permute-start.5 = (bf16[2,4,2,2,16,512]{5,4,3,2,1,0:T(8,128)(2,1)S(1)}, bf16[2,4,2,2,16,512]{5,4,3,2,1,0:T(8,128)(2,1)}, u32[]{:S(2)}, u32[]{:S(2)}) collective-permute-start(bf16[2,4,2,2,16,512]{5,4,3,2,1,0:T(8,128)(2,1)S(1)} %bitcast.16), channel_id=1, source_target_pairs={{0,24},{8,0},{16,8},{24,16},{1,25},{9,1},{17,9},{25,17},{2,26},{10... | collective-permute-start | bytes 1572872 | tf_op jit(solution)/shard_map/ppermute | solution.py:180
  83.0 13.7 %collective-permute-done.4.refs_1_ = bf16[2,4,2,2,16,512]{5,4,3,2,1,0:T(8,128)(2,1)S(1)} collective-permute-done((bf16[2,4,2,2,16,512]{5,4,3,2,1,0:T(8,128)(2,1)S(1)}, bf16[2,4,2,2,16,512]{5,4,3,2,1,0:T(8,128)(2,1)S(1)}, u32[]{:S(2)}, u32[]{:S(2)}) %collective-permute-start.4) | collective-permute-done | bytes 524320 | tf_op jit(solution)/shard_map/ppermute | solution.py:180
  96.7 0.0 copy-done.8
  96.7 0.0 copy-done.9
  96.7 0.0 collective-permute-done.5.refs_6_
  96.7 39.7 %all-to-all-done.1.x_ref = bf16[64,2,32,128]{3,2,1,0:T(8,128)(2,1)S(1)} async-done(((bf16[64,2,32,128]{3,2,1,0:T(8,128)(2,1)}), bf16[64,2,32,128]{3,2,1,0:T(8,128)(2,1)S(1)}, u32[]{:S(2)}, u32[]{:S(2)}) %all-to-all-start.1) | async-done | bytes 1048608 | tf_op jit(solution)/shard_map/all_to_all | solution.py:176
  136.4 0.0 copy-done.1
  136.4 2.4 %spectral.1 = bf16[64,2,32,128]{3,2,1,0:T(8,128)(2,1)} custom-call(bf16[64,2,32,128]{3,2,1,0:T(8,128)(2,1)S(1)} %all-to-all-done.1.x_ref, bf16[64,32,128]{2,1,0:T(8,128)(2,1)S(1)} %copy-done.1), custom_call_target="tpu_custom_call" | custom-call | flops 8388608 | bytes 2621440 | tf_op jit(solution)/shard_map/spectral/pallas_call | solution.py:107
  138.8 4.3 %all-to-all-start.2 = ((bf16[16,4,2,32,128]{4,3,2,1,0:T(8,128)(2,1)}), bf16[16,4,2,32,128]{4,3,2,1,0:T(8,128)(2,1)S(1)}, u32[]{:S(2)}, u32[]{:S(2)}) async-start(bf16[16,4,2,32,128]{4,3,2,1,0:T(8,128)(2,1)} %bitcast.10), calls=%async_computation.2 | async-start | bytes 2097152 | tf_op jit(solution)/shard_map/all_to_all | solution.py:176
  143.1 2.9 %collective-permute-start.9 = (bf16[2,4,2,2,16,512]{5,4,3,2,1,0:T(8,128)(2,1)}, bf16[2,4,2,2,16,512]{5,4,3,2,1,0:T(8,128)(2,1)S(1)}, u32[]{:S(2)}, u32[]{:S(2)}) collective-permute-start(bf16[2,4,2,2,16,512]{5,4,3,2,1,0:T(8,128)(2,1)} %bitcast.19), channel_id=1, source_target_pairs={{0,24},{8,0},{16,8},{24,16},{1,25},{9,1},{17,9},{25,17},{2,26},{10... | collective-permute-start | bytes 1572872 | tf_op jit(solution)/shard_map/ppermute | solution.py:180
  146.0 2.4 %collective-permute-start.6 = (bf16[2,4,2,2,16,512]{5,4,3,2,1,0:T(8,128)(2,1)}, bf16[2,4,2,2,16,512]{5,4,3,2,1,0:T(8,128)(2,1)S(1)}, u32[]{:S(2)}, u32[]{:S(2)}) collective-permute-start(bf16[2,4,2,2,16,512]{5,4,3,2,1,0:T(8,128)(2,1)} %bitcast.17), channel_id=1, source_target_pairs={{0,8},{8,16},{16,24},{24,0},{1,9},{9,17},{17,25},{25,1},{2,10},{10... | collective-permute-start | bytes 1572872 | tf_op jit(solution)/shard_map/ppermute | solution.py:180
  148.4 2.3 %collective-permute-start.7 = (bf16[2,4,2,2,16,512]{5,4,3,2,1,0:T(8,128)(2,1)S(1)}, bf16[2,4,2,2,16,512]{5,4,3,2,1,0:T(8,128)(2,1)S(1)}, u32[]{:S(2)}, u32[]{:S(2)}) collective-permute-start(bf16[2,4,2,2,16,512]{5,4,3,2,1,0:T(8,128)(2,1)S(1)} %collective-permute-done.4.refs_1_), channel_id=1, source_target_pairs={{0,8},{8,16},{16,24},{24,0},{1,9},{9,17},{17,25},{25,1},{2,10},{10... | collective-permute-start | bytes 1572872 | tf_op jit(solution)/shard_map/ppermute | solution.py:180
  150.7 4.2 %collective-permute-start.8 = (bf16[2,4,2,2,16,512]{5,4,3,2,1,0:T(8,128)(2,1)}, bf16[2,4,2,2,16,512]{5,4,3,2,1,0:T(8,128)(2,1)S(1)}, u32[]{:S(2)}, u32[]{:S(2)}) collective-permute-start(bf16[2,4,2,2,16,512]{5,4,3,2,1,0:T(8,128)(2,1)} %collective-permute-done.5.refs_6_), channel_id=1, source_target_pairs={{0,24},{8,0},{16,8},{24,16},{1,25},{9,1},{17,9},{25,17},{2,26},{10... | collective-permute-start | bytes 1572872 | tf_op jit(solution)/shard_map/ppermute | solution.py:180
  154.9 3.6 %collective-permute-done.9.refs_5_ = bf16[2,4,2,2,16,512]{5,4,3,2,1,0:T(8,128)(2,1)S(1)} collective-permute-done((bf16[2,4,2,2,16,512]{5,4,3,2,1,0:T(8,128)(2,1)}, bf16[2,4,2,2,16,512]{5,4,3,2,1,0:T(8,128)(2,1)S(1)}, u32[]{:S(2)}, u32[]{:S(2)}) %collective-permute-start.9) | collective-permute-done | bytes 524320 | tf_op jit(solution)/shard_map/ppermute | solution.py:180
  158.5 3.8 %collective-permute-done.6.refs_2_ = bf16[2,4,2,2,16,512]{5,4,3,2,1,0:T(8,128)(2,1)S(1)} collective-permute-done((bf16[2,4,2,2,16,512]{5,4,3,2,1,0:T(8,128)(2,1)}, bf16[2,4,2,2,16,512]{5,4,3,2,1,0:T(8,128)(2,1)S(1)}, u32[]{:S(2)}, u32[]{:S(2)}) %collective-permute-start.6) | collective-permute-done | bytes 524320 | tf_op jit(solution)/shard_map/ppermute | solution.py:180
  162.3 0.8 copy-done.2
  163.1 10.4 %collective-permute-done.7.refs_3_ = bf16[2,4,2,2,16,512]{5,4,3,2,1,0:T(8,128)(2,1)S(1)} collective-permute-done((bf16[2,4,2,2,16,512]{5,4,3,2,1,0:T(8,128)(2,1)S(1)}, bf16[2,4,2,2,16,512]{5,4,3,2,1,0:T(8,128)(2,1)S(1)}, u32[]{:S(2)}, u32[]{:S(2)}) %collective-permute-start.7) | collective-permute-done | bytes 524320 | tf_op jit(solution)/shard_map/ppermute | solution.py:180
  173.5 0.8 copy-done.4
  174.3 0.0 collective-permute-done.8.refs_4_
  174.3 0.8 copy-done.6
  175.1 5.9 %all-to-all-done.2 = bf16[16,4,2,32,128]{4,3,2,1,0:T(8,128)(2,1)S(1)} async-done(((bf16[16,4,2,32,128]{4,3,2,1,0:T(8,128)(2,1)}), bf16[16,4,2,32,128]{4,3,2,1,0:T(8,128)(2,1)S(1)}, u32[]{:S(2)}, u32[]{:S(2)}) %all-to-all-start.2) | async-done | bytes 1048608 | tf_op jit(solution)/shard_map/all_to_all | solution.py:176
  181.1 1.0 copy-done.3
  182.1 1.0 copy-done.5
  183.1 1.0 copy-done.7
  184.2 4.7 %apply.1 = f32[2,4,128,512]{3,2,1,0:T(8,128)} custom-call(s32[2]{0:T(128)S(1)} %pad_add_fusion.place_ref, bf16[4,2,2,4,2,32,128]{6,5,4,3,2,1,0:T(8,128)(2,1)S(1)} %bitcast.15, bf16[4,4,2,2,16,512]{5,4,3,2,1,0:T(8,128)(2,1)S(1)} %bitcast.14, bf16[2,4,2,2,16,512]{5,4,3,2,1,0:T(8,128)(2,1)S(1)} %collective-permute-done.4.refs_1_, ...), custom_call_target="tpu_custom_call" | custom-call | flops 1073741824 | bytes 7340032 | tf_op jit(solution)/shard_map/apply/pallas_call | solution.py:153
  (7 shorter events, 0.0 us)
Async XLA Ops:
  0.0 17.9 %collective-permute-start.3 = (bf16[2,4,16,512]{3,2,1,0:T(8,128)(2,1)}, bf16[2,4,16,512]{3,2,1,0:T(8,128)(2,1)S(1)}, u32[]{:S(2)}, u32[]{:S(2)}) collective-permute-start(bf16[2,4,16,512]{3,2,1,0:T(8,128)(2,1)} %param.4), channel_id=1, source_target_pairs={{0,4},{4,0},{1,5},{5,1},{2,6},{6,2},{3,7},{7,3},{8,12},{12,8},{9,1... | collective-permute-start | bytes 393224 | tf_op jit(solution)/shard_map/ppermute | solution.py:188
  18.8 10.6 %copy-start = (bf16[2,4,128,512]{3,2,1,0:T(8,128)(2,1)S(1)}, bf16[2,4,128,512]{3,2,1,0:T(8,128)(2,1)}, u32[]{:S(2)}) copy-start(bf16[2,4,128,512]{3,2,1,0:T(8,128)(2,1)} %refs_0_.1) | copy-start | bytes 3145732
  20.0 38.2 %all-to-all-start = ((bf16[16,2,2,16,512]{4,3,2,1,0:T(8,128)(2,1)}), bf16[16,2,2,16,512]{4,3,2,1,0:T(8,128)(2,1)S(1)}, u32[]{:S(2)}, u32[]{:S(2)}) async-start(bf16[16,2,2,16,512]{4,3,2,1,0:T(8,128)(2,1)} %bitcast.5), calls=%async_computation | async-start | bytes 2097152 | tf_op jit(solution)/shard_map/all_to_all | solution.py:176
  30.1 13.0 %collective-permute-start.2 = (bf16[2,1,128,512]{3,2,1,0:T(8,128)(2,1)}, bf16[2,1,128,512]{3,2,1,0:T(8,128)(2,1)S(1)}, u32[]{:S(2)}, u32[]{:S(2)}) collective-permute-start(bf16[2,1,128,512]{3,2,1,0:T(8,128)(2,1)} %get-tuple-element.13), channel_id=1, source_target_pairs={{0,24},{8,0},{16,8},{24,16},{1,25},{9,1},{17,9},{25,17},{2,26},{10... | collective-permute-start | bytes 786440 | tf_op jit(solution)/shard_map/ppermute | solution.py:180
  34.4 13.1 %collective-permute-start.1 = (bf16[2,1,128,512]{3,2,1,0:T(8,128)(2,1)S(1)}, bf16[2,1,128,512]{3,2,1,0:T(8,128)(2,1)S(1)}, u32[]{:S(2)}, u32[]{:S(2)}) collective-permute-start(bf16[2,1,128,512]{3,2,1,0:T(8,128)(2,1)S(1)} %get-tuple-element.14), channel_id=1, source_target_pairs={{0,16},{8,24},{16,0},{24,8},{1,17},{9,25},{17,1},{25,9},{2,18},{10... | collective-permute-start | bytes 786440 | tf_op jit(solution)/shard_map/ppermute | solution.py:180
  36.9 21.2 %collective-permute-start = (bf16[2,1,128,512]{3,2,1,0:T(8,128)(2,1)S(1)}, bf16[2,1,128,512]{3,2,1,0:T(8,128)(2,1)S(1)}, u32[]{:S(2)}, u32[]{:S(2)}) collective-permute-start(bf16[2,1,128,512]{3,2,1,0:T(8,128)(2,1)S(1)} %get-tuple-element.15), channel_id=1, source_target_pairs={{0,8},{8,16},{16,24},{24,0},{1,9},{9,17},{17,25},{25,1},{2,10},{10... | collective-permute-start | bytes 786440 | tf_op jit(solution)/shard_map/ppermute | solution.py:180
  61.2 75.2 %copy-start.1 = (bf16[64,32,128]{2,1,0:T(8,128)(2,1)S(1)}, bf16[64,32,128]{2,1,0:T(8,128)(2,1)}, u32[]{:S(2)}) copy-start(bf16[64,32,128]{2,1,0:T(8,128)(2,1)} %c_ref.1) | copy-start | bytes 1572868
  61.2 75.2 %all-to-all-start.1 = ((bf16[64,2,32,128]{3,2,1,0:T(8,128)(2,1)}), bf16[64,2,32,128]{3,2,1,0:T(8,128)(2,1)S(1)}, u32[]{:S(2)}, u32[]{:S(2)}) async-start(bf16[64,2,32,128]{3,2,1,0:T(8,128)(2,1)} %bitcast.7), calls=%async_computation.1 | async-start | bytes 2097152 | tf_op jit(solution)/shard_map/all_to_all | solution.py:176
  76.5 20.2 %copy-start.8 = (bf16[8,2,2,16,512]{4,3,2,1,0:T(8,128)(2,1)}, bf16[8,2,2,16,512]{4,3,2,1,0:T(8,128)(2,1)S(1)}, u32[]{:S(2)}) copy-start(bf16[8,2,2,16,512]{4,3,2,1,0:T(8,128)(2,1)S(1)} %get-tuple-element.11) | copy-start | bytes 1572868
  76.5 20.2 %copy-start.9 = (bf16[8,2,2,16,512]{4,3,2,1,0:T(8,128)(2,1)}, bf16[8,2,2,16,512]{4,3,2,1,0:T(8,128)(2,1)S(1)}, u32[]{:S(2)}) copy-start(bf16[8,2,2,16,512]{4,3,2,1,0:T(8,128)(2,1)S(1)} %get-tuple-element.12) | copy-start | bytes 1572868
  76.5 20.2 %collective-permute-start.4 = (bf16[2,4,2,2,16,512]{5,4,3,2,1,0:T(8,128)(2,1)S(1)}, bf16[2,4,2,2,16,512]{5,4,3,2,1,0:T(8,128)(2,1)S(1)}, u32[]{:S(2)}, u32[]{:S(2)}) collective-permute-start(bf16[2,4,2,2,16,512]{5,4,3,2,1,0:T(8,128)(2,1)S(1)} %bitcast.18), channel_id=1, source_target_pairs={{0,8},{8,16},{16,24},{24,0},{1,9},{9,17},{17,25},{25,1},{2,10},{10... | collective-permute-start | bytes 1572872 | tf_op jit(solution)/shard_map/ppermute | solution.py:180
  79.8 16.9 %collective-permute-start.5 = (bf16[2,4,2,2,16,512]{5,4,3,2,1,0:T(8,128)(2,1)S(1)}, bf16[2,4,2,2,16,512]{5,4,3,2,1,0:T(8,128)(2,1)}, u32[]{:S(2)}, u32[]{:S(2)}) collective-permute-start(bf16[2,4,2,2,16,512]{5,4,3,2,1,0:T(8,128)(2,1)S(1)} %bitcast.16), channel_id=1, source_target_pairs={{0,24},{8,0},{16,8},{24,16},{1,25},{9,1},{17,9},{25,17},{2,26},{10... | collective-permute-start | bytes 1572872 | tf_op jit(solution)/shard_map/ppermute | solution.py:180
  138.8 42.2 %all-to-all-start.2 = ((bf16[16,4,2,32,128]{4,3,2,1,0:T(8,128)(2,1)}), bf16[16,4,2,32,128]{4,3,2,1,0:T(8,128)(2,1)S(1)}, u32[]{:S(2)}, u32[]{:S(2)}) async-start(bf16[16,4,2,32,128]{4,3,2,1,0:T(8,128)(2,1)} %bitcast.10), calls=%async_computation.2 | async-start | bytes 2097152 | tf_op jit(solution)/shard_map/all_to_all | solution.py:176
  143.1 15.4 %collective-permute-start.9 = (bf16[2,4,2,2,16,512]{5,4,3,2,1,0:T(8,128)(2,1)}, bf16[2,4,2,2,16,512]{5,4,3,2,1,0:T(8,128)(2,1)S(1)}, u32[]{:S(2)}, u32[]{:S(2)}) collective-permute-start(bf16[2,4,2,2,16,512]{5,4,3,2,1,0:T(8,128)(2,1)} %bitcast.19), channel_id=1, source_target_pairs={{0,24},{8,0},{16,8},{24,16},{1,25},{9,1},{17,9},{25,17},{2,26},{10... | collective-permute-start | bytes 1572872 | tf_op jit(solution)/shard_map/ppermute | solution.py:180
  146.0 16.3 %collective-permute-start.6 = (bf16[2,4,2,2,16,512]{5,4,3,2,1,0:T(8,128)(2,1)}, bf16[2,4,2,2,16,512]{5,4,3,2,1,0:T(8,128)(2,1)S(1)}, u32[]{:S(2)}, u32[]{:S(2)}) collective-permute-start(bf16[2,4,2,2,16,512]{5,4,3,2,1,0:T(8,128)(2,1)} %bitcast.17), channel_id=1, source_target_pairs={{0,8},{8,16},{16,24},{24,0},{1,9},{9,17},{17,25},{25,1},{2,10},{10... | collective-permute-start | bytes 1572872 | tf_op jit(solution)/shard_map/ppermute | solution.py:180
  148.4 25.1 %collective-permute-start.7 = (bf16[2,4,2,2,16,512]{5,4,3,2,1,0:T(8,128)(2,1)S(1)}, bf16[2,4,2,2,16,512]{5,4,3,2,1,0:T(8,128)(2,1)S(1)}, u32[]{:S(2)}, u32[]{:S(2)}) collective-permute-start(bf16[2,4,2,2,16,512]{5,4,3,2,1,0:T(8,128)(2,1)S(1)} %collective-permute-done.4.refs_1_), channel_id=1, source_target_pairs={{0,8},{8,16},{16,24},{24,0},{1,9},{9,17},{17,25},{25,1},{2,10},{10... | collective-permute-start | bytes 1572872 | tf_op jit(solution)/shard_map/ppermute | solution.py:180
  150.7 23.7 %collective-permute-start.8 = (bf16[2,4,2,2,16,512]{5,4,3,2,1,0:T(8,128)(2,1)}, bf16[2,4,2,2,16,512]{5,4,3,2,1,0:T(8,128)(2,1)S(1)}, u32[]{:S(2)}, u32[]{:S(2)}) collective-permute-start(bf16[2,4,2,2,16,512]{5,4,3,2,1,0:T(8,128)(2,1)} %collective-permute-done.5.refs_6_), channel_id=1, source_target_pairs={{0,24},{8,0},{16,8},{24,16},{1,25},{9,1},{17,9},{25,17},{2,26},{10... | collective-permute-start | bytes 1572872 | tf_op jit(solution)/shard_map/ppermute | solution.py:180
  162.3 0.8 copy-start.2
  173.5 0.8 copy-start.4
  174.3 0.8 copy-start.6
  181.1 1.0 copy-start.3
  182.1 1.0 copy-start.5
  183.1 1.0 copy-start.7

commit v5 on v3

--- a/solution.py
+++ b/solution.py
@@ -9,7 +9,7 @@
 
 XS, ZH, ZQ = 4, 2, 4
 KG, KL = 16, 4
-VMEM = pltpu.CompilerParams(vmem_limit_bytes=48 << 20)
+VMEM = pltpu.CompilerParams(vmem_limit_bytes=24 << 20)
 
 
 def pairs_kernel(place_ref, *refs):
@@ -117,19 +117,37 @@
     )(x, coulomb)
 
 
-def apply_kernel(place_ref, kernel_ref, *refs):
-    rights, out_ref = refs[:XS], refs[XS]
+def apply_kernel(plan, place_ref, kernel_ref, *refs):
+    out_ref, right_ref, sems = refs[-3:]
     mu, orbitals = out_ref.shape[2:]
     tn = (((0,), (0,)), ((), ()))
-
-    def product(right_ref):
+    copies = [[] for _ in plan]
+    n = 0
+    for d, pieces in enumerate(plan):
+        at = 0
+        for array, begin, length in pieces:
+            source = refs[array].at[pl.ds(begin, length)]
+            copies[d].append(pltpu.make_async_copy(source, right_ref.at[d, pl.ds(at, length)], sems.at[n]))
+            at += length
+            n += 1
+
+    @pl.when(pl.program_id(0) == 0)
+    def _():
+        for copy in copies[0] + copies[1]:
+            copy.start()
+
+    def step(d):
+        for copy in copies[d + 2] if d + 2 < XS else []:
+            copy.start()
+        for copy in copies[d]:
+            copy.wait()
         total = None
         for side in range(2):
             at = (place_ref[0] + side) % ZH
             k_re = kernel_ref[:, at, :, 0, 0].reshape(-1, mu)
             k_im = kernel_ref[:, at, :, 0, 1].reshape(-1, mu)
-            b_re = right_ref[:, :, 0, side].reshape(-1, orbitals)
-            b_im = right_ref[:, :, 1, side].reshape(-1, orbitals)
+            b_re = right_ref[d, :, :, 0, side].reshape(-1, orbitals)
+            b_im = right_ref[d, :, :, 1, side].reshape(-1, orbitals)
             first = jnp.concatenate([k_re, k_im], 1)
             second = jnp.concatenate([-k_im, k_re], 1)
             term = lax.dot_general(first, b_re, tn, preferred_element_type=jnp.float32) + lax.dot_general(
@@ -140,14 +158,14 @@
         out_ref[1, 0] = total[mu:]
 
     for d in range(XS):
-        pl.when(pl.program_id(0) == d)(functools.partial(product, rights[d]))
-
-
-def apply(place, kernel, rights):
+        pl.when(pl.program_id(0) == d)(functools.partial(step, d))
+
+
+def apply(place, kernel, arrays, plan):
     xs, zhs, pairs, kl, _, rows, mu = kernel.shape
-    orbitals = rights[0].shape[-1]
+    orbitals = arrays[0].shape[-1]
     return pl.pallas_call(
-        apply_kernel,
+        functools.partial(apply_kernel, plan),
         grid_spec=pltpu.PrefetchScalarGridSpec(
             num_scalar_prefetch=1,
             grid=(XS,),
@@ -156,8 +174,12 @@
                     (xs, zhs, pairs, 1, 2, rows, mu), lambda d, place: (0, 0, 0, (place[1] + XS - d) % XS, 0, 0, 0)
                 )
             ]
-            + [pl.BlockSpec(rights[0].shape, lambda d, place: (0,) * 6)] * XS,
+            + [pl.BlockSpec(memory_space=pl.ANY)] * len(arrays),
             out_specs=pl.BlockSpec((2, 1, mu, orbitals), lambda d, place: (0, (place[1] + XS - d) % XS, 0, 0)),
+            scratch_shapes=[
+                pltpu.VMEM((XS, XS, *arrays[0].shape[1:]), jnp.bfloat16),
+                pltpu.SemaphoreType.DMA((sum(map(len, plan)),)),
+            ],
         ),
         out_shape=jax.ShapeDtypeStruct((2, kl, mu, orbitals), jnp.float32),
         compiler_params=VMEM,
@@ -165,7 +187,7 @@
             flops=8 * kl * xs * zhs * pairs * rows * mu * orbitals, bytes_accessed=7 << 20, transcendentals=0
         ),
         name="apply",
-    )(place, kernel, *rights)
+    )(place, kernel, *arrays)
 
 
 def swap(blocks, axes):
@@ -190,11 +212,20 @@
         block = lax.dynamic_slice_in_dim(left, (x + d) % XS, 1, 1)
         lefts.append(shift(block, d))
     pairs = make_pairs(place, lefts, mine)
-    rights = [mine] + [shift(mine, d) for d in range(1, XS)]
     columns = swap(pairs.reshape(KG * XS, parts, 2 * nus, mu), ("kg", "x"))
-    columns, rights[1], rights[3] = lax.optimization_barrier((columns, rights[1], rights[3]))
-    kernel = swap(spectral(columns, coulomb).reshape(KG, KL, parts, 2 * nus, mu), "kg")
-    return apply(place, kernel.reshape(XS, ZH, ZQ // 2, KL, parts, 2 * nus, mu), rights)
+    low, high = mine[: XS // 2], mine[XS // 2 :]
+    spatial = spectral(columns, coulomb)
+    spatial, up, down = lax.optimization_barrier((spatial, shift(low, 1), shift(high, XS - 1)))
+    late = jnp.concatenate([shift(high, 1), shift(up, 1), shift(down, XS - 1), shift(low, XS - 1)])
+    half = XS // 2
+    plan = [
+        [(0, 0, XS)],
+        [(1, 0, half), (3, 0, half)],
+        [(3, half, XS)],
+        [(3, half + XS, half), (2, 0, half)],
+    ]
+    kernel = swap(spatial.reshape(KG, KL, parts, 2 * nus, mu), "kg")
+    return apply(place, kernel.reshape(XS, ZH, ZQ // 2, KL, parts, 2 * nus, mu), [mine, up, down, late], plan)
 
 
 def solution(mesh):

time: 198 us -> 187 us (0.944)
  waiting for transfers between devices: 124 us -> 104 us
  starting transfers between devices: 55.9 us -> 65.8 us
  local copies, waits for them, and re-layouts: 7.33 us -> 3.99 us
    ppermute x6 -> x9, waiting for transfers between devices: 69.1 us -> 37.3 us  [shift(): return lax.ppermute(block, 'x', [(i, (i + d) % XS) for i in range(XS)])]
    all_to_all x3, waiting for transfers between devices: 45.5 us -> 57.9 us  [swap(): return lax.all_to_all(blocks, axes, split_axis=0, concat_axis=0, tiled=True)]
    ppermute x6 -> x9, starting transfers between devices: 18.5 us -> 27.5 us  [shift(): return lax.ppermute(block, 'x', [(i, (i + d) % XS) for i in range(XS)])]
    unnamed x12 -> x8, local copies, waits for them, and re-layouts: 5.46 us -> 1.06 us
  transfers between devices with their start and end apart: 10 -> 13, of which waited for: 9 -> 9; matrix products, arithmetic and copies ran while one was open for 0% -> 1% of each run, Pallas kernels for 0% -> 1%
where the time goes in v5:
time: 187 us; the launch traced here: 186 us
  waiting for transfers between devices  104 us (56%)
  starting transfers between devices  65.8 us (35%)
  Pallas kernels  10.7 us (6%)
  local copies, waits for them, and re-layouts  3.99 us (2%)
    all_to_all x3, waiting for transfers between devices, swap(): return lax.all_to_all(blocks, axes, split_axis=0, concat_axis=0, tiled=True)  57.9 us
    ppermute x9, waiting for transfers between devices, shift(): return lax.ppermute(block, 'x', [(i, (i + d) % XS) for i in range(XS)])  37.3 us
    all_to_all x3, starting transfers between devices, swap(): return lax.all_to_all(blocks, axes, split_axis=0, concat_axis=0, tiled=True)  29.5 us
    ppermute x9, starting transfers between devices, shift(): return lax.ppermute(block, 'x', [(i, (i + d) % XS) for i in range(XS)])  27.5 us
    ppermute x1, waiting for transfers between devices, on_device(): sides = jnp.stack([right, lax.ppermute(right, 'zh', [(0, 1), (1, 0)])], 2)  9.08 us
    ppermute x1, starting transfers between devices, on_device(): sides = jnp.stack([right, lax.ppermute(right, 'zh', [(0, 1), (1, 0)])], 2)  8.8 us
    pallas_call x1, Pallas kernels, apply(): pl.pallas_call(functools.partial(apply_kernel, plan), grid_spec=pltpu.Pre...  5.33 us
  transfers between devices with their start and end apart: 13, of which 9 were waited for; matrix products, arithmetic and copies ran while one was open for 1% of the time, Pallas kernels for 1%

profile of v5, /device:TPU:33, one launch (start us, length us, event | category | flops | bytes accessed | tf_op | source)
XLA Modules:
  0.0 186.2 jit_solution(7430462941964696763)
XLA Ops:
  0.0 8.8 %collective-permute-start.3 = (bf16[2,4,16,512]{3,2,1,0:T(8,128)(2,1)}, bf16[2,4,16,512]{3,2,1,0:T(8,128)(2,1)S(1)}, u32[]{:S(2)}, u32[]{:S(2)}) collective-permute-start(bf16[2,4,16,512]{3,2,1,0:T(8,128)(2,1)} %param.4), channel_id=1, source_target_pairs={{0,4},{4,0},{1,5},{5,1},{2,6},{6,2},{3,7},{7,3},{8,12},{12,8},{9,1... | collective-permute-start | bytes 393224 | tf_op jit(solution)/shard_map/ppermute | solution.py:206
  8.8 9.1 %collective-permute-done.3 = bf16[2,4,16,512]{3,2,1,0:T(8,128)(2,1)S(1)} collective-permute-done((bf16[2,4,16,512]{3,2,1,0:T(8,128)(2,1)}, bf16[2,4,16,512]{3,2,1,0:T(8,128)(2,1)S(1)}, u32[]{:S(2)}, u32[]{:S(2)}) %collective-permute-start.3) | collective-permute-done | bytes 131104 | tf_op jit(solution)/shard_map/ppermute | solution.py:206
  17.9 0.9 maximum_bitcast_fusion
  18.8 0.0 copy-start
  18.9 1.1 broadcast_in_dim.2
  20.0 9.4 %all-to-all-start = ((bf16[16,2,2,16,512]{4,3,2,1,0:T(8,128)(2,1)}), bf16[16,2,2,16,512]{4,3,2,1,0:T(8,128)(2,1)S(1)}, u32[]{:S(2)}, u32[]{:S(2)}) async-start(bf16[16,2,2,16,512]{4,3,2,1,0:T(8,128)(2,1)} %bitcast.5), calls=%async_computation | async-start | bytes 2097152 | tf_op jit(solution)/shard_map/all_to_all | solution.py:194
  29.4 0.0 copy-done
  29.4 0.8 constant_dynamic-slice_fusion
  30.1 4.3 %collective-permute-start.2 = (bf16[2,1,128,512]{3,2,1,0:T(8,128)(2,1)}, bf16[2,1,128,512]{3,2,1,0:T(8,128)(2,1)S(1)}, u32[]{:S(2)}, u32[]{:S(2)}) collective-permute-start(bf16[2,1,128,512]{3,2,1,0:T(8,128)(2,1)} %get-tuple-element.13), channel_id=1, source_target_pairs={{0,24},{8,0},{16,8},{24,16},{1,25},{9,1},{17,9},{25,17},{2,26},{10... | collective-permute-start | bytes 786440 | tf_op jit(solution)/shard_map/ppermute | solution.py:198
  34.5 2.5 %collective-permute-start.1 = (bf16[2,1,128,512]{3,2,1,0:T(8,128)(2,1)S(1)}, bf16[2,1,128,512]{3,2,1,0:T(8,128)(2,1)S(1)}, u32[]{:S(2)}, u32[]{:S(2)}) collective-permute-start(bf16[2,1,128,512]{3,2,1,0:T(8,128)(2,1)S(1)} %get-tuple-element.14), channel_id=1, source_target_pairs={{0,16},{8,24},{16,0},{24,8},{1,17},{9,25},{17,1},{25,9},{2,18},{10... | collective-permute-start | bytes 786440 | tf_op jit(solution)/shard_map/ppermute | solution.py:198
  36.9 2.5 %collective-permute-start = (bf16[2,1,128,512]{3,2,1,0:T(8,128)(2,1)S(1)}, bf16[2,1,128,512]{3,2,1,0:T(8,128)(2,1)S(1)}, u32[]{:S(2)}, u32[]{:S(2)}) collective-permute-start(bf16[2,1,128,512]{3,2,1,0:T(8,128)(2,1)S(1)} %get-tuple-element.15), channel_id=1, source_target_pairs={{0,8},{8,16},{16,24},{24,0},{1,9},{9,17},{17,25},{25,1},{2,10},{10... | collective-permute-start | bytes 786440 | tf_op jit(solution)/shard_map/ppermute | solution.py:198
  39.4 0.1 pad_add_fusion.place_ref
  39.5 3.6 %collective-permute-done.2.refs_3_ = bf16[2,1,128,512]{3,2,1,0:T(8,128)(2,1)S(1)} collective-permute-done((bf16[2,1,128,512]{3,2,1,0:T(8,128)(2,1)}, bf16[2,1,128,512]{3,2,1,0:T(8,128)(2,1)S(1)}, u32[]{:S(2)}, u32[]{:S(2)}) %collective-permute-start.2) | collective-permute-done | bytes 262176 | tf_op jit(solution)/shard_map/ppermute | solution.py:198
  43.1 4.4 %collective-permute-done.1.refs_2_ = bf16[2,1,128,512]{3,2,1,0:T(8,128)(2,1)S(1)} collective-permute-done((bf16[2,1,128,512]{3,2,1,0:T(8,128)(2,1)S(1)}, bf16[2,1,128,512]{3,2,1,0:T(8,128)(2,1)S(1)}, u32[]{:S(2)}, u32[]{:S(2)}) %collective-permute-start.1) | collective-permute-done | bytes 262176 | tf_op jit(solution)/shard_map/ppermute | solution.py:198
  47.5 10.6 %collective-permute-done.refs_1_ = bf16[2,1,128,512]{3,2,1,0:T(8,128)(2,1)S(1)} collective-permute-done((bf16[2,1,128,512]{3,2,1,0:T(8,128)(2,1)S(1)}, bf16[2,1,128,512]{3,2,1,0:T(8,128)(2,1)S(1)}, u32[]{:S(2)}, u32[]{:S(2)}) %collective-permute-start) | collective-permute-done | bytes 262176 | tf_op jit(solution)/shard_map/ppermute | solution.py:198
  58.1 0.0 all-to-all-done
  58.1 3.0 %pairs.1 = bf16[4,2,2,4,2,32,128]{6,5,4,3,2,1,0:T(8,128)(2,1)} custom-call(s32[2]{0:T(128)S(1)} %pad_add_fusion.place_ref, bf16[2,4,128,512]{3,2,1,0:T(8,128)(2,1)S(1)} %copy-done, bf16[2,1,128,512]{3,2,1,0:T(8,128)(2,1)S(1)} %collective-permute-done.refs_1_, bf16[2,1,128,512]{3,2,1,0:T(8,128)(2,1)S(1)} %collective-permute-done.1.refs_2_, ...), custom_call_target="tpu_custom_call" | custom-call | flops 1073741824 | bytes 3145728 | tf_op jit(solution)/shard_map/pairs/pallas_call | solution.py:41
  61.2 0.0 copy-start.1
  61.2 15.2 %all-to-all-start.1 = ((bf16[64,2,32,128]{3,2,1,0:T(8,128)(2,1)}), bf16[64,2,32,128]{3,2,1,0:T(8,128)(2,1)S(1)}, u32[]{:S(2)}, u32[]{:S(2)}) async-start(bf16[64,2,32,128]{3,2,1,0:T(8,128)(2,1)} %bitcast.7), calls=%async_computation.1 | async-start | bytes 2097152 | tf_op jit(solution)/shard_map/all_to_all | solution.py:194
  76.4 1.1 fusion
  77.4 3.3 %collective-permute-start.4 = (bf16[2,4,2,2,16,512]{5,4,3,2,1,0:T(8,128)(2,1)}, bf16[2,4,2,2,16,512]{5,4,3,2,1,0:T(8,128)(2,1)S(1)}, u32[]{:S(2)}, u32[]{:S(2)}) collective-permute-start(bf16[2,4,2,2,16,512]{5,4,3,2,1,0:T(8,128)(2,1)} %bitcast.8), channel_id=1, source_target_pairs={{0,8},{8,16},{16,24},{24,0},{1,9},{9,17},{17,25},{25,1},{2,10},{10... | collective-permute-start | bytes 1572872 | tf_op jit(solution)/shard_map/ppermute | solution.py:198
  80.7 3.2 %collective-permute-start.5 = (bf16[2,4,2,2,16,512]{5,4,3,2,1,0:T(8,128)(2,1)}, bf16[2,4,2,2,16,512]{5,4,3,2,1,0:T(8,128)(2,1)}, u32[]{:S(2)}, u32[]{:S(2)}) collective-permute-start(bf16[2,4,2,2,16,512]{5,4,3,2,1,0:T(8,128)(2,1)} %bitcast.9), channel_id=1, source_target_pairs={{0,24},{8,0},{16,8},{24,16},{1,25},{9,1},{17,9},{25,17},{2,26},{10... | collective-permute-start | bytes 1572872 | tf_op jit(solution)/shard_map/ppermute | solution.py:198
  83.9 52.6 %all-to-all-done.1.x_ref = bf16[64,2,32,128]{3,2,1,0:T(8,128)(2,1)S(1)} async-done(((bf16[64,2,32,128]{3,2,1,0:T(8,128)(2,1)}), bf16[64,2,32,128]{3,2,1,0:T(8,128)(2,1)S(1)}, u32[]{:S(2)}, u32[]{:S(2)}) %all-to-all-start.1) | async-done | bytes 1048608 | tf_op jit(solution)/shard_map/all_to_all | solution.py:194
  136.5 0.0 copy-done.1
  136.5 2.4 %spectral.1 = bf16[64,2,32,128]{3,2,1,0:T(8,128)(2,1)} custom-call(bf16[64,2,32,128]{3,2,1,0:T(8,128)(2,1)S(1)} %all-to-all-done.1.x_ref, bf16[64,32,128]{2,1,0:T(8,128)(2,1)S(1)} %copy-done.1), custom_call_target="tpu_custom_call" | custom-call | flops 8388608 | bytes 2621440 | tf_op jit(solution)/shard_map/spectral/pallas_call | solution.py:107
  138.9 0.0 collective-permute-done.4.refs_1_
  138.9 0.0 copy-start.2
  138.9 0.0 collective-permute-done.5.refs_2_
  138.9 4.9 %all-to-all-start.2 = ((bf16[16,4,2,32,128]{4,3,2,1,0:T(8,128)(2,1)}), bf16[16,4,2,32,128]{4,3,2,1,0:T(8,128)(2,1)}, u32[]{:S(2)}, u32[]{:S(2)}) async-start(bf16[16,4,2,32,128]{4,3,2,1,0:T(8,128)(2,1)} %bitcast.10), calls=%async_computation.2 | async-start | bytes 2097152 | tf_op jit(solution)/shard_map/all_to_all | solution.py:194
  143.8 2.9 %collective-permute-start.9 = (bf16[2,4,2,2,16,512]{5,4,3,2,1,0:T(8,128)(2,1)}, bf16[2,4,2,2,16,512]{5,4,3,2,1,0:T(8,128)(2,1)S(1)}, u32[]{:S(2)}, u32[]{:S(2)}) collective-permute-start(bf16[2,4,2,2,16,512]{5,4,3,2,1,0:T(8,128)(2,1)} %bitcast.8), channel_id=1, source_target_pairs={{0,24},{8,0},{16,8},{24,16},{1,25},{9,1},{17,9},{25,17},{2,26},{10... | collective-permute-start | bytes 1572872 | tf_op jit(solution)/shard_map/ppermute | solution.py:198
  146.6 2.4 %collective-permute-start.6 = (bf16[2,4,2,2,16,512]{5,4,3,2,1,0:T(8,128)(2,1)}, bf16[2,4,2,2,16,512]{5,4,3,2,1,0:T(8,128)(2,1)S(1)}, u32[]{:S(2)}, u32[]{:S(2)}) collective-permute-start(bf16[2,4,2,2,16,512]{5,4,3,2,1,0:T(8,128)(2,1)} %bitcast.9), channel_id=1, source_target_pairs={{0,8},{8,16},{16,24},{24,0},{1,9},{9,17},{17,25},{25,1},{2,10},{10... | collective-permute-start | bytes 1572872 | tf_op jit(solution)/shard_map/ppermute | solution.py:198
  149.1 2.3 %collective-permute-start.7 = (bf16[2,4,2,2,16,512]{5,4,3,2,1,0:T(8,128)(2,1)S(1)}, bf16[2,4,2,2,16,512]{5,4,3,2,1,0:T(8,128)(2,1)S(1)}, u32[]{:S(2)}, u32[]{:S(2)}) collective-permute-start(bf16[2,4,2,2,16,512]{5,4,3,2,1,0:T(8,128)(2,1)S(1)} %collective-permute-done.4.refs_1_), channel_id=1, source_target_pairs={{0,8},{8,16},{16,24},{24,0},{1,9},{9,17},{17,25},{25,1},{2,10},{10... | collective-permute-start | bytes 1572872 | tf_op jit(solution)/shard_map/ppermute | solution.py:198
  151.4 4.2 %collective-permute-start.8 = (bf16[2,4,2,2,16,512]{5,4,3,2,1,0:T(8,128)(2,1)}, bf16[2,4,2,2,16,512]{5,4,3,2,1,0:T(8,128)(2,1)S(1)}, u32[]{:S(2)}, u32[]{:S(2)}) collective-permute-start(bf16[2,4,2,2,16,512]{5,4,3,2,1,0:T(8,128)(2,1)} %collective-permute-done.5.refs_2_), channel_id=1, source_target_pairs={{0,24},{8,0},{16,8},{24,16},{1,25},{9,1},{17,9},{25,17},{2,26},{10... | collective-permute-start | bytes 1572872 | tf_op jit(solution)/shard_map/ppermute | solution.py:198
  155.6 3.6 %collective-permute-done.9 = bf16[2,4,2,2,16,512]{5,4,3,2,1,0:T(8,128)(2,1)S(1)} collective-permute-done((bf16[2,4,2,2,16,512]{5,4,3,2,1,0:T(8,128)(2,1)}, bf16[2,4,2,2,16,512]{5,4,3,2,1,0:T(8,128)(2,1)S(1)}, u32[]{:S(2)}, u32[]{:S(2)}) %collective-permute-start.9) | collective-permute-done | bytes 524320 | tf_op jit(solution)/shard_map/ppermute | solution.py:198
  159.2 3.8 %collective-permute-done.6 = bf16[2,4,2,2,16,512]{5,4,3,2,1,0:T(8,128)(2,1)S(1)} collective-permute-done((bf16[2,4,2,2,16,512]{5,4,3,2,1,0:T(8,128)(2,1)}, bf16[2,4,2,2,16,512]{5,4,3,2,1,0:T(8,128)(2,1)S(1)}, u32[]{:S(2)}, u32[]{:S(2)}) %collective-permute-start.6) | collective-permute-done | bytes 524320 | tf_op jit(solution)/shard_map/ppermute | solution.py:198
  163.0 11.2 %collective-permute-done.7 = bf16[2,4,2,2,16,512]{5,4,3,2,1,0:T(8,128)(2,1)S(1)} collective-permute-done((bf16[2,4,2,2,16,512]{5,4,3,2,1,0:T(8,128)(2,1)S(1)}, bf16[2,4,2,2,16,512]{5,4,3,2,1,0:T(8,128)(2,1)S(1)}, u32[]{:S(2)}, u32[]{:S(2)}) %collective-permute-start.7) | collective-permute-done | bytes 524320 | tf_op jit(solution)/shard_map/ppermute | solution.py:198
  174.2 0.0 copy-done.2
  174.2 0.0 collective-permute-done.8
  174.2 0.3 pad_maximum_fusion.refs_3_
  174.5 5.3 %all-to-all-done.2 = bf16[16,4,2,32,128]{4,3,2,1,0:T(8,128)(2,1)} async-done(((bf16[16,4,2,32,128]{4,3,2,1,0:T(8,128)(2,1)}), bf16[16,4,2,32,128]{4,3,2,1,0:T(8,128)(2,1)}, u32[]{:S(2)}, u32[]{:S(2)}) %all-to-all-start.2) | async-done | bytes 1048608 | tf_op jit(solution)/shard_map/all_to_all | solution.py:194
  179.8 0.0 copy-start.3
  179.8 1.0 copy-done.3
  180.8 5.3 %apply.1 = f32[2,4,128,512]{3,2,1,0:T(8,128)} custom-call(s32[2]{0:T(128)S(1)} %pad_add_fusion.place_ref, bf16[4,2,2,4,2,32,128]{6,5,4,3,2,1,0:T(8,128)(2,1)} %bitcast.11.kernel_ref, bf16[4,4,2,2,16,512]{5,4,3,2,1,0:T(8,128)(2,1)S(1)} %bitcast.14, bf16[2,4,2,2,16,512]{5,4,3,2,1,0:T(8,128)(2,1)S(1)} %copy-done.3, ...), custom_call_target="tpu_custom_call" | custom-call | flops 1073741824 | bytes 7340032 | tf_op jit(solution)/shard_map/apply/pallas_call | solution.py:167
  (1 shorter events, 0.0 us)
Async XLA Ops:
  0.0 17.9 %collective-permute-start.3 = (bf16[2,4,16,512]{3,2,1,0:T(8,128)(2,1)}, bf16[2,4,16,512]{3,2,1,0:T(8,128)(2,1)S(1)}, u32[]{:S(2)}, u32[]{:S(2)}) collective-permute-start(bf16[2,4,16,512]{3,2,1,0:T(8,128)(2,1)} %param.4), channel_id=1, source_target_pairs={{0,4},{4,0},{1,5},{5,1},{2,6},{6,2},{3,7},{7,3},{8,12},{12,8},{9,1... | collective-permute-start | bytes 393224 | tf_op jit(solution)/shard_map/ppermute | solution.py:206
  18.8 10.6 %copy-start = (bf16[2,4,128,512]{3,2,1,0:T(8,128)(2,1)S(1)}, bf16[2,4,128,512]{3,2,1,0:T(8,128)(2,1)}, u32[]{:S(2)}) copy-start(bf16[2,4,128,512]{3,2,1,0:T(8,128)(2,1)} %refs_0_.1) | copy-start | bytes 3145732
  20.0 38.2 %all-to-all-start = ((bf16[16,2,2,16,512]{4,3,2,1,0:T(8,128)(2,1)}), bf16[16,2,2,16,512]{4,3,2,1,0:T(8,128)(2,1)S(1)}, u32[]{:S(2)}, u32[]{:S(2)}) async-start(bf16[16,2,2,16,512]{4,3,2,1,0:T(8,128)(2,1)} %bitcast.5), calls=%async_computation | async-start | bytes 2097152 | tf_op jit(solution)/shard_map/all_to_all | solution.py:194
  30.1 13.0 %collective-permute-start.2 = (bf16[2,1,128,512]{3,2,1,0:T(8,128)(2,1)}, bf16[2,1,128,512]{3,2,1,0:T(8,128)(2,1)S(1)}, u32[]{:S(2)}, u32[]{:S(2)}) collective-permute-start(bf16[2,1,128,512]{3,2,1,0:T(8,128)(2,1)} %get-tuple-element.13), channel_id=1, source_target_pairs={{0,24},{8,0},{16,8},{24,16},{1,25},{9,1},{17,9},{25,17},{2,26},{10... | collective-permute-start | bytes 786440 | tf_op jit(solution)/shard_map/ppermute | solution.py:198
  34.5 13.1 %collective-permute-start.1 = (bf16[2,1,128,512]{3,2,1,0:T(8,128)(2,1)S(1)}, bf16[2,1,128,512]{3,2,1,0:T(8,128)(2,1)S(1)}, u32[]{:S(2)}, u32[]{:S(2)}) collective-permute-start(bf16[2,1,128,512]{3,2,1,0:T(8,128)(2,1)S(1)} %get-tuple-element.14), channel_id=1, source_target_pairs={{0,16},{8,24},{16,0},{24,8},{1,17},{9,25},{17,1},{25,9},{2,18},{10... | collective-permute-start | bytes 786440 | tf_op jit(solution)/shard_map/ppermute | solution.py:198
  36.9 21.2 %collective-permute-start = (bf16[2,1,128,512]{3,2,1,0:T(8,128)(2,1)S(1)}, bf16[2,1,128,512]{3,2,1,0:T(8,128)(2,1)S(1)}, u32[]{:S(2)}, u32[]{:S(2)}) collective-permute-start(bf16[2,1,128,512]{3,2,1,0:T(8,128)(2,1)S(1)} %get-tuple-element.15), channel_id=1, source_target_pairs={{0,8},{8,16},{16,24},{24,0},{1,9},{9,17},{17,25},{25,1},{2,10},{10... | collective-permute-start | bytes 786440 | tf_op jit(solution)/shard_map/ppermute | solution.py:198
  61.2 75.3 %copy-start.1 = (bf16[64,32,128]{2,1,0:T(8,128)(2,1)S(1)}, bf16[64,32,128]{2,1,0:T(8,128)(2,1)}, u32[]{:S(2)}) copy-start(bf16[64,32,128]{2,1,0:T(8,128)(2,1)} %c_ref.1) | copy-start | bytes 1572868
  61.2 75.3 %all-to-all-start.1 = ((bf16[64,2,32,128]{3,2,1,0:T(8,128)(2,1)}), bf16[64,2,32,128]{3,2,1,0:T(8,128)(2,1)S(1)}, u32[]{:S(2)}, u32[]{:S(2)}) async-start(bf16[64,2,32,128]{3,2,1,0:T(8,128)(2,1)} %bitcast.7), calls=%async_computation.1 | async-start | bytes 2097152 | tf_op jit(solution)/shard_map/all_to_all | solution.py:194
  77.4 61.4 %collective-permute-start.4 = (bf16[2,4,2,2,16,512]{5,4,3,2,1,0:T(8,128)(2,1)}, bf16[2,4,2,2,16,512]{5,4,3,2,1,0:T(8,128)(2,1)S(1)}, u32[]{:S(2)}, u32[]{:S(2)}) collective-permute-start(bf16[2,4,2,2,16,512]{5,4,3,2,1,0:T(8,128)(2,1)} %bitcast.8), channel_id=1, source_target_pairs={{0,8},{8,16},{16,24},{24,0},{1,9},{9,17},{17,25},{25,1},{2,10},{10... | collective-permute-start | bytes 1572872 | tf_op jit(solution)/shard_map/ppermute | solution.py:198
  80.7 58.2 %collective-permute-start.5 = (bf16[2,4,2,2,16,512]{5,4,3,2,1,0:T(8,128)(2,1)}, bf16[2,4,2,2,16,512]{5,4,3,2,1,0:T(8,128)(2,1)}, u32[]{:S(2)}, u32[]{:S(2)}) collective-permute-start(bf16[2,4,2,2,16,512]{5,4,3,2,1,0:T(8,128)(2,1)} %bitcast.9), channel_id=1, source_target_pairs={{0,24},{8,0},{16,8},{24,16},{1,25},{9,1},{17,9},{25,17},{2,26},{10... | collective-permute-start | bytes 1572872 | tf_op jit(solution)/shard_map/ppermute | solution.py:198
  138.9 35.3 %copy-start.2 = (bf16[2,4,2,2,16,512]{5,4,3,2,1,0:T(8,128)(2,1)}, bf16[2,4,2,2,16,512]{5,4,3,2,1,0:T(8,128)(2,1)S(1)}, u32[]{:S(2)}) copy-start(bf16[2,4,2,2,16,512]{5,4,3,2,1,0:T(8,128)(2,1)S(1)} %collective-permute-done.4.refs_1_) | copy-start | bytes 1572868
  138.9 40.9 %all-to-all-start.2 = ((bf16[16,4,2,32,128]{4,3,2,1,0:T(8,128)(2,1)}), bf16[16,4,2,32,128]{4,3,2,1,0:T(8,128)(2,1)}, u32[]{:S(2)}, u32[]{:S(2)}) async-start(bf16[16,4,2,32,128]{4,3,2,1,0:T(8,128)(2,1)} %bitcast.10), calls=%async_computation.2 | async-start | bytes 2097152 | tf_op jit(solution)/shard_map/all_to_all | solution.py:194
  143.8 15.4 %collective-permute-start.9 = (bf16[2,4,2,2,16,512]{5,4,3,2,1,0:T(8,128)(2,1)}, bf16[2,4,2,2,16,512]{5,4,3,2,1,0:T(8,128)(2,1)S(1)}, u32[]{:S(2)}, u32[]{:S(2)}) collective-permute-start(bf16[2,4,2,2,16,512]{5,4,3,2,1,0:T(8,128)(2,1)} %bitcast.8), channel_id=1, source_target_pairs={{0,24},{8,0},{16,8},{24,16},{1,25},{9,1},{17,9},{25,17},{2,26},{10... | collective-permute-start | bytes 1572872 | tf_op jit(solution)/shard_map/ppermute | solution.py:198
  146.6 16.3 %collective-permute-start.6 = (bf16[2,4,2,2,16,512]{5,4,3,2,1,0:T(8,128)(2,1)}, bf16[2,4,2,2,16,512]{5,4,3,2,1,0:T(8,128)(2,1)S(1)}, u32[]{:S(2)}, u32[]{:S(2)}) collective-permute-start(bf16[2,4,2,2,16,512]{5,4,3,2,1,0:T(8,128)(2,1)} %bitcast.9), channel_id=1, source_target_pairs={{0,8},{8,16},{16,24},{24,0},{1,9},{9,17},{17,25},{25,1},{2,10},{10... | collective-permute-start | bytes 1572872 | tf_op jit(solution)/shard_map/ppermute | solution.py:198
  149.1 25.1 %collective-permute-start.7 = (bf16[2,4,2,2,16,512]{5,4,3,2,1,0:T(8,128)(2,1)S(1)}, bf16[2,4,2,2,16,512]{5,4,3,2,1,0:T(8,128)(2,1)S(1)}, u32[]{:S(2)}, u32[]{:S(2)}) collective-permute-start(bf16[2,4,2,2,16,512]{5,4,3,2,1,0:T(8,128)(2,1)S(1)} %collective-permute-done.4.refs_1_), channel_id=1, source_target_pairs={{0,8},{8,16},{16,24},{24,0},{1,9},{9,17},{17,25},{25,1},{2,10},{10... | collective-permute-start | bytes 1572872 | tf_op jit(solution)/shard_map/ppermute | solution.py:198
  151.4 22.8 %collective-permute-start.8 = (bf16[2,4,2,2,16,512]{5,4,3,2,1,0:T(8,128)(2,1)}, bf16[2,4,2,2,16,512]{5,4,3,2,1,0:T(8,128)(2,1)S(1)}, u32[]{:S(2)}, u32[]{:S(2)}) collective-permute-start(bf16[2,4,2,2,16,512]{5,4,3,2,1,0:T(8,128)(2,1)} %collective-permute-done.5.refs_2_), channel_id=1, source_target_pairs={{0,24},{8,0},{16,8},{24,16},{1,25},{9,1},{17,9},{25,17},{2,26},{10... | collective-permute-start | bytes 1572872 | tf_op jit(solution)/shard_map/ppermute | solution.py:198
  179.8 1.0 copy-start.3

commit v6 on v5

--- a/solution.py
+++ b/solution.py
@@ -10,6 +10,30 @@
 XS, ZH, ZQ = 4, 2, 4
 KG, KL = 16, 4
 VMEM = pltpu.CompilerParams(vmem_limit_bytes=24 << 20)
+
+
+def send_kernel(right_ref, *refs):
+    out_ref = refs[-1]
+    for part in range(2):
+        block = right_ref[part]
+        for zq in range(ZQ):
+            out_ref[:, zq, part, 0] = block
+
+
+def make_send(right, side, base=None):
+    parts, kl, nus, orbitals = right.shape
+    more = [] if base is None else [base]
+    return pl.pallas_call(
+        send_kernel,
+        grid=(1,),
+        in_specs=[pl.BlockSpec(right.shape, lambda n: (0, 0, 0, 0))] + [pl.BlockSpec(memory_space=pl.ANY)] * len(more),
+        out_specs=pl.BlockSpec((kl, ZQ, parts, 1, nus, orbitals), lambda n: (0, 0, 0, side, 0, 0)),
+        out_shape=jax.ShapeDtypeStruct((kl, ZQ, parts, 2, nus, orbitals), right.dtype),
+        input_output_aliases={1: 0} if more else {},
+        compiler_params=VMEM,
+        cost_estimate=pl.CostEstimate(flops=0, bytes_accessed=5 << 17, transcendentals=0),
+        name="send",
+    )(right, *more)
 
 
 def pairs_kernel(place_ref, *refs):
@@ -203,8 +227,8 @@
     mu = left.shape[2]
     x = lax.axis_index("x")
     place = jnp.stack([lax.axis_index("zh"), x]).astype(jnp.int32)
-    sides = jnp.stack([right, lax.ppermute(right, "zh", [(0, 1), (1, 0)])], 2)
-    sides = jnp.broadcast_to(sides.transpose(1, 0, 2, 3, 4)[:, None], (kl, ZQ, parts, 2, nus, orbitals))
+    other = lax.ppermute(right, "zh", [(0, 1), (1, 0)])
+    sides = make_send(other, 1, make_send(right, 0))
     mine = swap(sides.reshape(kl * ZQ, parts, 2, nus, orbitals), ("x", "zq"))
     mine = mine.reshape(XS, ZQ, parts, 2, nus, orbitals)
     lefts = [left]

time: 187 us -> 186 us (level)
  waiting for transfers between devices: 104 us -> 102 us
where the time goes in v6:
time: 186 us; the launch traced here: 185 us
  waiting for transfers between devices  102 us (55%)
  starting transfers between devices  65.8 us (35%)
  Pallas kernels  12.4 us (7%)
  local copies, waits for them, and re-layouts  3.77 us (2%)
    all_to_all x3, waiting for transfers between devices, swap(): return lax.all_to_all(blocks, axes, split_axis=0, concat_axis=0, tiled=True)  57.9 us
    ppermute x9, waiting for transfers between devices, shift(): return lax.ppermute(block, 'x', [(i, (i + d) % XS) for i in range(XS)])  37.3 us
    all_to_all x3, starting transfers between devices, swap(): return lax.all_to_all(blocks, axes, split_axis=0, concat_axis=0, tiled=True)  29.5 us
    ppermute x9, starting transfers between devices, shift(): return lax.ppermute(block, 'x', [(i, (i + d) % XS) for i in range(XS)])  27.5 us
    ppermute x1, starting transfers between devices, on_device(): other = lax.ppermute(right, 'zh', [(0, 1), (1, 0)])  8.8 us
    ppermute x1, waiting for transfers between devices, on_device(): other = lax.ppermute(right, 'zh', [(0, 1), (1, 0)])  7.33 us
    pallas_call x1, Pallas kernels, apply(): pl.pallas_call(functools.partial(apply_kernel, plan), grid_spec=pltpu.Pre...  5.33 us
  transfers between devices with their start and end apart: 13, of which 9 were waited for; matrix products, arithmetic and copies ran while one was open for 1% of the time, Pallas kernels for 1%

profile of v6, /device:TPU:33, one launch (start us, length us, event | category | flops | bytes accessed | tf_op | source)
XLA Modules:
  0.0 184.9 jit_solution(9341362853100435935)
XLA Ops:
  0.0 8.8 %collective-permute-start.3 = (bf16[2,4,16,512]{3,2,1,0:T(8,128)(2,1)}, bf16[2,4,16,512]{3,2,1,0:T(8,128)(2,1)S(1)}, u32[]{:S(2)}, u32[]{:S(2)}) collective-permute-start(bf16[2,4,16,512]{3,2,1,0:T(8,128)(2,1)} %right_ref.1), channel_id=1, source_target_pairs={{0,4},{4,0},{1,5},{5,1},{2,6},{6,2},{3,7},{7,3},{8,12},{12,8},{9,1... | collective-permute-start | bytes 393224 | tf_op jit(solution)/shard_map/ppermute | solution.py:230
  8.8 0.0 copy-start.4
  8.8 0.9 copy-done.4
  9.7 0.8 send.2.refs_0_
  10.6 0.0 copy-start
  10.6 7.3 %collective-permute-done.3.right_ref = bf16[2,4,16,512]{3,2,1,0:T(8,128)(2,1)S(1)} collective-permute-done((bf16[2,4,16,512]{3,2,1,0:T(8,128)(2,1)}, bf16[2,4,16,512]{3,2,1,0:T(8,128)(2,1)S(1)}, u32[]{:S(2)}, u32[]{:S(2)}) %collective-permute-start.3) | collective-permute-done | bytes 131104 | tf_op jit(solution)/shard_map/ppermute | solution.py:230
  17.9 0.8 send.3
  18.7 9.4 %all-to-all-start = ((bf16[16,2,2,16,512]{4,3,2,1,0:T(8,128)(2,1)}), bf16[16,2,2,16,512]{4,3,2,1,0:T(8,128)(2,1)S(1)}, u32[]{:S(2)}, u32[]{:S(2)}) async-start(bf16[16,2,2,16,512]{4,3,2,1,0:T(8,128)(2,1)} %bitcast.2), calls=%async_computation | async-start | bytes 2097152 | tf_op jit(solution)/shard_map/all_to_all | solution.py:218
  28.1 0.0 copy-done
  28.1 0.8 constant_dynamic-slice_fusion
  28.9 4.3 %collective-permute-start.2 = (bf16[2,1,128,512]{3,2,1,0:T(8,128)(2,1)}, bf16[2,1,128,512]{3,2,1,0:T(8,128)(2,1)S(1)}, u32[]{:S(2)}, u32[]{:S(2)}) collective-permute-start(bf16[2,1,128,512]{3,2,1,0:T(8,128)(2,1)} %get-tuple-element.13), channel_id=1, source_target_pairs={{0,24},{8,0},{16,8},{24,16},{1,25},{9,1},{17,9},{25,17},{2,26},{10... | collective-permute-start | bytes 786440 | tf_op jit(solution)/shard_map/ppermute | solution.py:222
  33.2 2.5 %collective-permute-start.1 = (bf16[2,1,128,512]{3,2,1,0:T(8,128)(2,1)S(1)}, bf16[2,1,128,512]{3,2,1,0:T(8,128)(2,1)S(1)}, u32[]{:S(2)}, u32[]{:S(2)}) collective-permute-start(bf16[2,1,128,512]{3,2,1,0:T(8,128)(2,1)S(1)} %get-tuple-element.14), channel_id=1, source_target_pairs={{0,16},{8,24},{16,0},{24,8},{1,17},{9,25},{17,1},{25,9},{2,18},{10... | collective-permute-start | bytes 786440 | tf_op jit(solution)/shard_map/ppermute | solution.py:222
  35.7 2.5 %collective-permute-start = (bf16[2,1,128,512]{3,2,1,0:T(8,128)(2,1)S(1)}, bf16[2,1,128,512]{3,2,1,0:T(8,128)(2,1)S(1)}, u32[]{:S(2)}, u32[]{:S(2)}) collective-permute-start(bf16[2,1,128,512]{3,2,1,0:T(8,128)(2,1)S(1)} %get-tuple-element.15), channel_id=1, source_target_pairs={{0,8},{8,16},{16,24},{24,0},{1,9},{9,17},{17,25},{25,1},{2,10},{10... | collective-permute-start | bytes 786440 | tf_op jit(solution)/shard_map/ppermute | solution.py:222
  38.2 0.1 pad_add_fusion.place_ref
  38.3 3.6 %collective-permute-done.2.refs_3_ = bf16[2,1,128,512]{3,2,1,0:T(8,128)(2,1)S(1)} collective-permute-done((bf16[2,1,128,512]{3,2,1,0:T(8,128)(2,1)}, bf16[2,1,128,512]{3,2,1,0:T(8,128)(2,1)S(1)}, u32[]{:S(2)}, u32[]{:S(2)}) %collective-permute-start.2) | collective-permute-done | bytes 262176 | tf_op jit(solution)/shard_map/ppermute | solution.py:222
  41.9 4.4 %collective-permute-done.1.refs_2_ = bf16[2,1,128,512]{3,2,1,0:T(8,128)(2,1)S(1)} collective-permute-done((bf16[2,1,128,512]{3,2,1,0:T(8,128)(2,1)S(1)}, bf16[2,1,128,512]{3,2,1,0:T(8,128)(2,1)S(1)}, u32[]{:S(2)}, u32[]{:S(2)}) %collective-permute-start.1) | collective-permute-done | bytes 262176 | tf_op jit(solution)/shard_map/ppermute | solution.py:222
  46.3 10.6 %collective-permute-done.refs_1_ = bf16[2,1,128,512]{3,2,1,0:T(8,128)(2,1)S(1)} collective-permute-done((bf16[2,1,128,512]{3,2,1,0:T(8,128)(2,1)S(1)}, bf16[2,1,128,512]{3,2,1,0:T(8,128)(2,1)S(1)}, u32[]{:S(2)}, u32[]{:S(2)}) %collective-permute-start) | collective-permute-done | bytes 262176 | tf_op jit(solution)/shard_map/ppermute | solution.py:222
  56.9 0.0 all-to-all-done
  56.9 3.0 %pairs.1 = bf16[4,2,2,4,2,32,128]{6,5,4,3,2,1,0:T(8,128)(2,1)} custom-call(s32[2]{0:T(128)S(1)} %pad_add_fusion.place_ref, bf16[2,4,128,512]{3,2,1,0:T(8,128)(2,1)S(1)} %copy-done, bf16[2,1,128,512]{3,2,1,0:T(8,128)(2,1)S(1)} %collective-permute-done.refs_1_, bf16[2,1,128,512]{3,2,1,0:T(8,128)(2,1)S(1)} %collective-permute-done.1.refs_2_, ...), custom_call_target="tpu_custom_call" | custom-call | flops 1073741824 | bytes 3145728 | tf_op jit(solution)/shard_map/pairs/pallas_call | solution.py:65
  59.9 0.0 copy-start.1
  59.9 15.2 %all-to-all-start.1 = ((bf16[64,2,32,128]{3,2,1,0:T(8,128)(2,1)}), bf16[64,2,32,128]{3,2,1,0:T(8,128)(2,1)S(1)}, u32[]{:S(2)}, u32[]{:S(2)}) async-start(bf16[64,2,32,128]{3,2,1,0:T(8,128)(2,1)} %bitcast.4), calls=%async_computation.1 | async-start | bytes 2097152 | tf_op jit(solution)/shard_map/all_to_all | solution.py:218
  75.1 1.1 fusion
  76.2 3.3 %collective-permute-start.4 = (bf16[2,4,2,2,16,512]{5,4,3,2,1,0:T(8,128)(2,1)}, bf16[2,4,2,2,16,512]{5,4,3,2,1,0:T(8,128)(2,1)S(1)}, u32[]{:S(2)}, u32[]{:S(2)}) collective-permute-start(bf16[2,4,2,2,16,512]{5,4,3,2,1,0:T(8,128)(2,1)} %bitcast.5), channel_id=1, source_target_pairs={{0,8},{8,16},{16,24},{24,0},{1,9},{9,17},{17,25},{25,1},{2,10},{10... | collective-permute-start | bytes 1572872 | tf_op jit(solution)/shard_map/ppermute | solution.py:222
  79.5 3.2 %collective-permute-start.5 = (bf16[2,4,2,2,16,512]{5,4,3,2,1,0:T(8,128)(2,1)}, bf16[2,4,2,2,16,512]{5,4,3,2,1,0:T(8,128)(2,1)}, u32[]{:S(2)}, u32[]{:S(2)}) collective-permute-start(bf16[2,4,2,2,16,512]{5,4,3,2,1,0:T(8,128)(2,1)} %bitcast.6), channel_id=1, source_target_pairs={{0,24},{8,0},{16,8},{24,16},{1,25},{9,1},{17,9},{25,17},{2,26},{10... | collective-permute-start | bytes 1572872 | tf_op jit(solution)/shard_map/ppermute | solution.py:222
  82.7 52.6 %all-to-all-done.1.x_ref = bf16[64,2,32,128]{3,2,1,0:T(8,128)(2,1)S(1)} async-done(((bf16[64,2,32,128]{3,2,1,0:T(8,128)(2,1)}), bf16[64,2,32,128]{3,2,1,0:T(8,128)(2,1)S(1)}, u32[]{:S(2)}, u32[]{:S(2)}) %all-to-all-start.1) | async-done | bytes 1048608 | tf_op jit(solution)/shard_map/all_to_all | solution.py:218
  135.3 0.0 copy-done.1
  135.3 2.4 %spectral.1 = bf16[64,2,32,128]{3,2,1,0:T(8,128)(2,1)} custom-call(bf16[64,2,32,128]{3,2,1,0:T(8,128)(2,1)S(1)} %all-to-all-done.1.x_ref, bf16[64,32,128]{2,1,0:T(8,128)(2,1)S(1)} %copy-done.1), custom_call_target="tpu_custom_call" | custom-call | flops 8388608 | bytes 2621440 | tf_op jit(solution)/shard_map/spectral/pallas_call | solution.py:131
  137.6 0.0 collective-permute-done.4.refs_1_
  137.6 0.0 copy-start.2
  137.6 0.0 collective-permute-done.5.refs_2_
  137.6 4.9 %all-to-all-start.2 = ((bf16[16,4,2,32,128]{4,3,2,1,0:T(8,128)(2,1)}), bf16[16,4,2,32,128]{4,3,2,1,0:T(8,128)(2,1)}, u32[]{:S(2)}, u32[]{:S(2)}) async-start(bf16[16,4,2,32,128]{4,3,2,1,0:T(8,128)(2,1)} %bitcast.7), calls=%async_computation.2 | async-start | bytes 2097152 | tf_op jit(solution)/shard_map/all_to_all | solution.py:218
  142.5 2.9 %collective-permute-start.9 = (bf16[2,4,2,2,16,512]{5,4,3,2,1,0:T(8,128)(2,1)}, bf16[2,4,2,2,16,512]{5,4,3,2,1,0:T(8,128)(2,1)S(1)}, u32[]{:S(2)}, u32[]{:S(2)}) collective-permute-start(bf16[2,4,2,2,16,512]{5,4,3,2,1,0:T(8,128)(2,1)} %bitcast.5), channel_id=1, source_target_pairs={{0,24},{8,0},{16,8},{24,16},{1,25},{9,1},{17,9},{25,17},{2,26},{10... | collective-permute-start | bytes 1572872 | tf_op jit(solution)/shard_map/ppermute | solution.py:222
  145.4 2.4 %collective-permute-start.6 = (bf16[2,4,2,2,16,512]{5,4,3,2,1,0:T(8,128)(2,1)}, bf16[2,4,2,2,16,512]{5,4,3,2,1,0:T(8,128)(2,1)S(1)}, u32[]{:S(2)}, u32[]{:S(2)}) collective-permute-start(bf16[2,4,2,2,16,512]{5,4,3,2,1,0:T(8,128)(2,1)} %bitcast.6), channel_id=1, source_target_pairs={{0,8},{8,16},{16,24},{24,0},{1,9},{9,17},{17,25},{25,1},{2,10},{10... | collective-permute-start | bytes 1572872 | tf_op jit(solution)/shard_map/ppermute | solution.py:222
  147.8 2.3 %collective-permute-start.7 = (bf16[2,4,2,2,16,512]{5,4,3,2,1,0:T(8,128)(2,1)S(1)}, bf16[2,4,2,2,16,512]{5,4,3,2,1,0:T(8,128)(2,1)S(1)}, u32[]{:S(2)}, u32[]{:S(2)}) collective-permute-start(bf16[2,4,2,2,16,512]{5,4,3,2,1,0:T(8,128)(2,1)S(1)} %collective-permute-done.4.refs_1_), channel_id=1, source_target_pairs={{0,8},{8,16},{16,24},{24,0},{1,9},{9,17},{17,25},{25,1},{2,10},{10... | collective-permute-start | bytes 1572872 | tf_op jit(solution)/shard_map/ppermute | solution.py:222
  150.1 4.2 %collective-permute-start.8 = (bf16[2,4,2,2,16,512]{5,4,3,2,1,0:T(8,128)(2,1)}, bf16[2,4,2,2,16,512]{5,4,3,2,1,0:T(8,128)(2,1)S(1)}, u32[]{:S(2)}, u32[]{:S(2)}) collective-permute-start(bf16[2,4,2,2,16,512]{5,4,3,2,1,0:T(8,128)(2,1)} %collective-permute-done.5.refs_2_), channel_id=1, source_target_pairs={{0,24},{8,0},{16,8},{24,16},{1,25},{9,1},{17,9},{25,17},{2,26},{10... | collective-permute-start | bytes 1572872 | tf_op jit(solution)/shard_map/ppermute | solution.py:222
  154.3 3.6 %collective-permute-done.9 = bf16[2,4,2,2,16,512]{5,4,3,2,1,0:T(8,128)(2,1)S(1)} collective-permute-done((bf16[2,4,2,2,16,512]{5,4,3,2,1,0:T(8,128)(2,1)}, bf16[2,4,2,2,16,512]{5,4,3,2,1,0:T(8,128)(2,1)S(1)}, u32[]{:S(2)}, u32[]{:S(2)}) %collective-permute-start.9) | collective-permute-done | bytes 524320 | tf_op jit(solution)/shard_map/ppermute | solution.py:222
  158.0 3.8 %collective-permute-done.6 = bf16[2,4,2,2,16,512]{5,4,3,2,1,0:T(8,128)(2,1)S(1)} collective-permute-done((bf16[2,4,2,2,16,512]{5,4,3,2,1,0:T(8,128)(2,1)}, bf16[2,4,2,2,16,512]{5,4,3,2,1,0:T(8,128)(2,1)S(1)}, u32[]{:S(2)}, u32[]{:S(2)}) %collective-permute-start.6) | collective-permute-done | bytes 524320 | tf_op jit(solution)/shard_map/ppermute | solution.py:222
  161.7 11.2 %collective-permute-done.7 = bf16[2,4,2,2,16,512]{5,4,3,2,1,0:T(8,128)(2,1)S(1)} collective-permute-done((bf16[2,4,2,2,16,512]{5,4,3,2,1,0:T(8,128)(2,1)S(1)}, bf16[2,4,2,2,16,512]{5,4,3,2,1,0:T(8,128)(2,1)S(1)}, u32[]{:S(2)}, u32[]{:S(2)}) %collective-permute-start.7) | collective-permute-done | bytes 524320 | tf_op jit(solution)/shard_map/ppermute | solution.py:222
  173.0 0.0 copy-done.2
  173.0 0.0 collective-permute-done.8
  173.0 0.3 pad_maximum_fusion.refs_3_
  173.2 5.3 %all-to-all-done.2 = bf16[16,4,2,32,128]{4,3,2,1,0:T(8,128)(2,1)} async-done(((bf16[16,4,2,32,128]{4,3,2,1,0:T(8,128)(2,1)}), bf16[16,4,2,32,128]{4,3,2,1,0:T(8,128)(2,1)}, u32[]{:S(2)}, u32[]{:S(2)}) %all-to-all-start.2) | async-done | bytes 1048608 | tf_op jit(solution)/shard_map/all_to_all | solution.py:218
  178.5 0.0 copy-start.3
  178.6 1.0 copy-done.3
  179.6 5.3 %apply.1 = f32[2,4,128,512]{3,2,1,0:T(8,128)} custom-call(s32[2]{0:T(128)S(1)} %pad_add_fusion.place_ref, bf16[4,2,2,4,2,32,128]{6,5,4,3,2,1,0:T(8,128)(2,1)} %bitcast.8.kernel_ref, bf16[4,4,2,2,16,512]{5,4,3,2,1,0:T(8,128)(2,1)S(1)} %bitcast.10, bf16[2,4,2,2,16,512]{5,4,3,2,1,0:T(8,128)(2,1)S(1)} %copy-done.3, ...), custom_call_target="tpu_custom_call" | custom-call | flops 1073741824 | bytes 7340032 | tf_op jit(solution)/shard_map/apply/pallas_call | solution.py:191
Async XLA Ops:
  0.0 17.9 %collective-permute-start.3 = (bf16[2,4,16,512]{3,2,1,0:T(8,128)(2,1)}, bf16[2,4,16,512]{3,2,1,0:T(8,128)(2,1)S(1)}, u32[]{:S(2)}, u32[]{:S(2)}) collective-permute-start(bf16[2,4,16,512]{3,2,1,0:T(8,128)(2,1)} %right_ref.1), channel_id=1, source_target_pairs={{0,4},{4,0},{1,5},{5,1},{2,6},{6,2},{3,7},{7,3},{8,12},{12,8},{9,1... | collective-permute-start | bytes 393224 | tf_op jit(solution)/shard_map/ppermute | solution.py:230
  8.8 0.9 copy-start.4
  10.6 17.6 %copy-start = (bf16[2,4,128,512]{3,2,1,0:T(8,128)(2,1)S(1)}, bf16[2,4,128,512]{3,2,1,0:T(8,128)(2,1)}, u32[]{:S(2)}) copy-start(bf16[2,4,128,512]{3,2,1,0:T(8,128)(2,1)} %refs_0_.1) | copy-start | bytes 3145732
  18.7 38.2 %all-to-all-start = ((bf16[16,2,2,16,512]{4,3,2,1,0:T(8,128)(2,1)}), bf16[16,2,2,16,512]{4,3,2,1,0:T(8,128)(2,1)S(1)}, u32[]{:S(2)}, u32[]{:S(2)}) async-start(bf16[16,2,2,16,512]{4,3,2,1,0:T(8,128)(2,1)} %bitcast.2), calls=%async_computation | async-start | bytes 2097152 | tf_op jit(solution)/shard_map/all_to_all | solution.py:218
  28.9 13.0 %collective-permute-start.2 = (bf16[2,1,128,512]{3,2,1,0:T(8,128)(2,1)}, bf16[2,1,128,512]{3,2,1,0:T(8,128)(2,1)S(1)}, u32[]{:S(2)}, u32[]{:S(2)}) collective-permute-start(bf16[2,1,128,512]{3,2,1,0:T(8,128)(2,1)} %get-tuple-element.13), channel_id=1, source_target_pairs={{0,24},{8,0},{16,8},{24,16},{1,25},{9,1},{17,9},{25,17},{2,26},{10... | collective-permute-start | bytes 786440 | tf_op jit(solution)/shard_map/ppermute | solution.py:222
  33.2 13.1 %collective-permute-start.1 = (bf16[2,1,128,512]{3,2,1,0:T(8,128)(2,1)S(1)}, bf16[2,1,128,512]{3,2,1,0:T(8,128)(2,1)S(1)}, u32[]{:S(2)}, u32[]{:S(2)}) collective-permute-start(bf16[2,1,128,512]{3,2,1,0:T(8,128)(2,1)S(1)} %get-tuple-element.14), channel_id=1, source_target_pairs={{0,16},{8,24},{16,0},{24,8},{1,17},{9,25},{17,1},{25,9},{2,18},{10... | collective-permute-start | bytes 786440 | tf_op jit(solution)/shard_map/ppermute | solution.py:222
  35.7 21.2 %collective-permute-start = (bf16[2,1,128,512]{3,2,1,0:T(8,128)(2,1)S(1)}, bf16[2,1,128,512]{3,2,1,0:T(8,128)(2,1)S(1)}, u32[]{:S(2)}, u32[]{:S(2)}) collective-permute-start(bf16[2,1,128,512]{3,2,1,0:T(8,128)(2,1)S(1)} %get-tuple-element.15), channel_id=1, source_target_pairs={{0,8},{8,16},{16,24},{24,0},{1,9},{9,17},{17,25},{25,1},{2,10},{10... | collective-permute-start | bytes 786440 | tf_op jit(solution)/shard_map/ppermute | solution.py:222
  59.9 75.3 %copy-start.1 = (bf16[64,32,128]{2,1,0:T(8,128)(2,1)S(1)}, bf16[64,32,128]{2,1,0:T(8,128)(2,1)}, u32[]{:S(2)}) copy-start(bf16[64,32,128]{2,1,0:T(8,128)(2,1)} %c_ref.1) | copy-start | bytes 1572868
  59.9 75.3 %all-to-all-start.1 = ((bf16[64,2,32,128]{3,2,1,0:T(8,128)(2,1)}), bf16[64,2,32,128]{3,2,1,0:T(8,128)(2,1)S(1)}, u32[]{:S(2)}, u32[]{:S(2)}) async-start(bf16[64,2,32,128]{3,2,1,0:T(8,128)(2,1)} %bitcast.4), calls=%async_computation.1 | async-start | bytes 2097152 | tf_op jit(solution)/shard_map/all_to_all | solution.py:218
  76.2 61.4 %collective-permute-start.4 = (bf16[2,4,2,2,16,512]{5,4,3,2,1,0:T(8,128)(2,1)}, bf16[2,4,2,2,16,512]{5,4,3,2,1,0:T(8,128)(2,1)S(1)}, u32[]{:S(2)}, u32[]{:S(2)}) collective-permute-start(bf16[2,4,2,2,16,512]{5,4,3,2,1,0:T(8,128)(2,1)} %bitcast.5), channel_id=1, source_target_pairs={{0,8},{8,16},{16,24},{24,0},{1,9},{9,17},{17,25},{25,1},{2,10},{10... | collective-permute-start | bytes 1572872 | tf_op jit(solution)/shard_map/ppermute | solution.py:222
  79.5 58.2 %collective-permute-start.5 = (bf16[2,4,2,2,16,512]{5,4,3,2,1,0:T(8,128)(2,1)}, bf16[2,4,2,2,16,512]{5,4,3,2,1,0:T(8,128)(2,1)}, u32[]{:S(2)}, u32[]{:S(2)}) collective-permute-start(bf16[2,4,2,2,16,512]{5,4,3,2,1,0:T(8,128)(2,1)} %bitcast.6), channel_id=1, source_target_pairs={{0,24},{8,0},{16,8},{24,16},{1,25},{9,1},{17,9},{25,17},{2,26},{10... | collective-permute-start | bytes 1572872 | tf_op jit(solution)/shard_map/ppermute | solution.py:222
  137.6 35.3 %copy-start.2 = (bf16[2,4,2,2,16,512]{5,4,3,2,1,0:T(8,128)(2,1)}, bf16[2,4,2,2,16,512]{5,4,3,2,1,0:T(8,128)(2,1)S(1)}, u32[]{:S(2)}) copy-start(bf16[2,4,2,2,16,512]{5,4,3,2,1,0:T(8,128)(2,1)S(1)} %collective-permute-done.4.refs_1_) | copy-start | bytes 1572868
  137.6 40.9 %all-to-all-start.2 = ((bf16[16,4,2,32,128]{4,3,2,1,0:T(8,128)(2,1)}), bf16[16,4,2,32,128]{4,3,2,1,0:T(8,128)(2,1)}, u32[]{:S(2)}, u32[]{:S(2)}) async-start(bf16[16,4,2,32,128]{4,3,2,1,0:T(8,128)(2,1)} %bitcast.7), calls=%async_computation.2 | async-start | bytes 2097152 | tf_op jit(solution)/shard_map/all_to_all | solution.py:218
  142.5 15.4 %collective-permute-start.9 = (bf16[2,4,2,2,16,512]{5,4,3,2,1,0:T(8,128)(2,1)}, bf16[2,4,2,2,16,512]{5,4,3,2,1,0:T(8,128)(2,1)S(1)}, u32[]{:S(2)}, u32[]{:S(2)}) collective-permute-start(bf16[2,4,2,2,16,512]{5,4,3,2,1,0:T(8,128)(2,1)} %bitcast.5), channel_id=1, source_target_pairs={{0,24},{8,0},{16,8},{24,16},{1,25},{9,1},{17,9},{25,17},{2,26},{10... | collective-permute-start | bytes 1572872 | tf_op jit(solution)/shard_map/ppermute | solution.py:222
  145.4 16.3 %collective-permute-start.6 = (bf16[2,4,2,2,16,512]{5,4,3,2,1,0:T(8,128)(2,1)}, bf16[2,4,2,2,16,512]{5,4,3,2,1,0:T(8,128)(2,1)S(1)}, u32[]{:S(2)}, u32[]{:S(2)}) collective-permute-start(bf16[2,4,2,2,16,512]{5,4,3,2,1,0:T(8,128)(2,1)} %bitcast.6), channel_id=1, source_target_pairs={{0,8},{8,16},{16,24},{24,0},{1,9},{9,17},{17,25},{25,1},{2,10},{10... | collective-permute-start | bytes 1572872 | tf_op jit(solution)/shard_map/ppermute | solution.py:222
  147.8 25.1 %collective-permute-start.7 = (bf16[2,4,2,2,16,512]{5,4,3,2,1,0:T(8,128)(2,1)S(1)}, bf16[2,4,2,2,16,512]{5,4,3,2,1,0:T(8,128)(2,1)S(1)}, u32[]{:S(2)}, u32[]{:S(2)}) collective-permute-start(bf16[2,4,2,2,16,512]{5,4,3,2,1,0:T(8,128)(2,1)S(1)} %collective-permute-done.4.refs_1_), channel_id=1, source_target_pairs={{0,8},{8,16},{16,24},{24,0},{1,9},{9,17},{17,25},{25,1},{2,10},{10... | collective-permute-start | bytes 1572872 | tf_op jit(solution)/shard_map/ppermute | solution.py:222
  150.1 22.8 %collective-permute-start.8 = (bf16[2,4,2,2,16,512]{5,4,3,2,1,0:T(8,128)(2,1)}, bf16[2,4,2,2,16,512]{5,4,3,2,1,0:T(8,128)(2,1)S(1)}, u32[]{:S(2)}, u32[]{:S(2)}) collective-permute-start(bf16[2,4,2,2,16,512]{5,4,3,2,1,0:T(8,128)(2,1)} %collective-permute-done.5.refs_2_), channel_id=1, source_target_pairs={{0,24},{8,0},{16,8},{24,16},{1,25},{9,1},{17,9},{25,17},{2,26},{10... | collective-permute-start | bytes 1572872 | tf_op jit(solution)/shard_map/ppermute | solution.py:222
  178.5 1.0 copy-start.3

commit v7 on v6

--- a/solution.py
+++ b/solution.py
@@ -37,43 +37,48 @@
 
 
 def pairs_kernel(place_ref, *refs):
-    lefts, right_ref, out_ref = refs[:XS], refs[XS], refs[-1]
+    lefts, (right_ref, out_ref, done_ref, sems) = refs[:XS], refs[XS:]
     mu, orbitals = lefts[0].shape[2:]
     nt = (((1,), (1,)), ((), ()))
-    b_re = right_ref[:, :, 0, 0].reshape(-1, orbitals)
-    b_im = right_ref[:, :, 1, 0].reshape(-1, orbitals)
-    shape = (XS, ZQ // 2, out_ref.shape[5], mu)
-    for d, left_ref in enumerate(lefts):
-        a_re, a_im = left_ref[0, 0], left_ref[1, 0]
-        first = jnp.concatenate([a_re, a_im], 0)
-        second = jnp.concatenate([a_im, -a_re], 0)
-        both = lax.dot_general(b_re, first, nt, preferred_element_type=jnp.float32) + lax.dot_general(
-            b_im, second, nt, preferred_element_type=jnp.float32
+    shape = (XS, ZQ // 2, done_ref.shape[5], mu)
+    copies = []
+    for side in range(2):
+        b_re = right_ref[:, :, 0, side].reshape(-1, orbitals)
+        b_im = right_ref[:, :, 1, side].reshape(-1, orbitals)
+        for d, left_ref in enumerate(lefts):
+            a_re, a_im = left_ref[0, 0], left_ref[1, 0]
+            first = jnp.concatenate([a_re, a_im], 0)
+            second = jnp.concatenate([a_im, -a_re], 0)
+            both = lax.dot_general(b_re, first, nt, preferred_element_type=jnp.float32) + lax.dot_general(
+                b_im, second, nt, preferred_element_type=jnp.float32
+            )
+            both = both.astype(jnp.bfloat16)
+            at = (place_ref[1] + XS - d) % XS
+            done_ref[side, :, :, at, 0] = both[:, :mu].reshape(shape)
+            done_ref[side, :, :, at, 1] = both[:, mu:].reshape(shape)
+        copies.append(
+            pltpu.make_async_copy(done_ref.at[side], out_ref.at[:, (place_ref[0] + side) % ZH], sems.at[side])
         )
-        both = both.astype(jnp.bfloat16)
-        at = (place_ref[1] + XS - d) % XS
-        out_ref[:, 0, :, at, 0] = both[:, :mu].reshape(shape)
-        out_ref[:, 0, :, at, 1] = both[:, mu:].reshape(shape)
+        copies[-1].start()
+    for copy in copies:
+        copy.wait()
 
 
 def make_pairs(place, lefts, right):
     _, _, mu, orbitals = lefts[0].shape
     nus = right.shape[4]
-    one = (2, 1, mu, orbitals)
-    left_specs = [pl.BlockSpec(one, lambda side, place: (0, place[1], 0, 0))]
-    left_specs += [pl.BlockSpec(one, lambda side, place: (0, 0, 0, 0))] * (XS - 1)
+    half = (XS, ZQ // 2, XS, 2, 2 * nus, mu)
     return pl.pallas_call(
         pairs_kernel,
         grid_spec=pltpu.PrefetchScalarGridSpec(
             num_scalar_prefetch=1,
-            grid=(2,),
-            in_specs=left_specs
-            + [pl.BlockSpec((XS, ZQ, 2, 1, nus, orbitals), lambda side, place: (0, 0, 0, side, 0, 0))],
-            out_specs=pl.BlockSpec(
-                (XS, 1, ZQ // 2, XS, 2, 2 * nus, mu), lambda side, place: (0, (place[0] + side) % ZH, 0, 0, 0, 0, 0)
-            ),
-        ),
-        out_shape=jax.ShapeDtypeStruct((XS, ZH, ZQ // 2, XS, 2, 2 * nus, mu), jnp.bfloat16),
+            grid=(1,),
+            in_specs=[pl.BlockSpec((2, 1, mu, orbitals), lambda n, place: (0, place[1], 0, 0))]
+            + [pl.BlockSpec(memory_space=pltpu.VMEM)] * XS,
+            out_specs=pl.BlockSpec(memory_space=pl.ANY),
+            scratch_shapes=[pltpu.VMEM((2, *half), jnp.bfloat16), pltpu.SemaphoreType.DMA((2,))],
+        ),
+        out_shape=jax.ShapeDtypeStruct((XS, ZH, *half[1:]), jnp.bfloat16),
         compiler_params=VMEM,
         cost_estimate=pl.CostEstimate(
             flops=16 * XS * XS * ZQ * nus * mu * orbitals, bytes_accessed=3 << 20, transcendentals=0
@@ -142,34 +147,34 @@
 
 
 def apply_kernel(plan, place_ref, kernel_ref, *refs):
-    out_ref, right_ref, sems = refs[-3:]
+    out_ref, blocks_ref, right_ref, done_ref, in_sems, out_sems = refs[-6:]
     mu, orbitals = out_ref.shape[2:]
     tn = (((0,), (0,)), ((), ()))
-    copies = [[] for _ in plan]
+    gets, puts = [], []
     n = 0
     for d, pieces in enumerate(plan):
+        k = (place_ref[1] + XS - d) % XS
+        gets.append([pltpu.make_async_copy(kernel_ref.at[:, :, :, k], blocks_ref.at[d], in_sems.at[n])])
+        n += 1
         at = 0
         for array, begin, length in pieces:
             source = refs[array].at[pl.ds(begin, length)]
-            copies[d].append(pltpu.make_async_copy(source, right_ref.at[d, pl.ds(at, length)], sems.at[n]))
+            gets[d].append(pltpu.make_async_copy(source, right_ref.at[d, pl.ds(at, length)], in_sems.at[n]))
             at += length
             n += 1
-
-    @pl.when(pl.program_id(0) == 0)
-    def _():
-        for copy in copies[0] + copies[1]:
+        puts.append(pltpu.make_async_copy(done_ref.at[d], out_ref.at[:, k], out_sems.at[d]))
+    for copy in gets[0] + gets[1]:
+        copy.start()
+    for d in range(XS):
+        for copy in gets[d + 2] if d + 2 < XS else []:
             copy.start()
-
-    def step(d):
-        for copy in copies[d + 2] if d + 2 < XS else []:
-            copy.start()
-        for copy in copies[d]:
+        for copy in gets[d]:
             copy.wait()
         total = None
         for side in range(2):
             at = (place_ref[0] + side) % ZH
-            k_re = kernel_ref[:, at, :, 0, 0].reshape(-1, mu)
-            k_im = kernel_ref[:, at, :, 0, 1].reshape(-1, mu)
+            k_re = blocks_ref[d, :, at, :, 0].reshape(-1, mu)
+            k_im = blocks_ref[d, :, at, :, 1].reshape(-1, mu)
             b_re = right_ref[d, :, :, 0, side].reshape(-1, orbitals)
             b_im = right_ref[d, :, :, 1, side].reshape(-1, orbitals)
             first = jnp.concatenate([k_re, k_im], 1)
@@ -178,11 +183,11 @@
                 second, b_im, tn, preferred_element_type=jnp.float32
             )
             total = term if total is None else total + term
-        out_ref[0, 0] = total[:mu]
-        out_ref[1, 0] = total[mu:]
-
-    for d in range(XS):
-        pl.when(pl.program_id(0) == d)(functools.partial(step, d))
+        done_ref[d, 0] = total[:mu]
+        done_ref[d, 1] = total[mu:]
+        puts[d].start()
+    for copy in puts:
+        copy.wait()
 
 
 def apply(place, kernel, arrays, plan):
@@ -192,17 +197,15 @@
         functools.partial(apply_kernel, plan),
         grid_spec=pltpu.PrefetchScalarGridSpec(
             num_scalar_prefetch=1,
-            grid=(XS,),
-            in_specs=[
-                pl.BlockSpec(
-                    (xs, zhs, pairs, 1, 2, rows, mu), lambda d, place: (0, 0, 0, (place[1] + XS - d) % XS, 0, 0, 0)
-                )
-            ]
-            + [pl.BlockSpec(memory_space=pl.ANY)] * len(arrays),
-            out_specs=pl.BlockSpec((2, 1, mu, orbitals), lambda d, place: (0, (place[1] + XS - d) % XS, 0, 0)),
+            grid=(1,),
+            in_specs=[pl.BlockSpec(memory_space=pl.ANY)] * (1 + len(arrays)),
+            out_specs=pl.BlockSpec(memory_space=pl.ANY),
             scratch_shapes=[
+                pltpu.VMEM((XS, xs, zhs, pairs, 2, rows, mu), jnp.bfloat16),
                 pltpu.VMEM((XS, XS, *arrays[0].shape[1:]), jnp.bfloat16),
-                pltpu.SemaphoreType.DMA((sum(map(len, plan)),)),
+                pltpu.VMEM((XS, 2, mu, orbitals), jnp.float32),
+                pltpu.SemaphoreType.DMA((XS + sum(map(len, plan)),)),
+                pltpu.SemaphoreType.DMA((XS,)),
             ],
         ),
         out_shape=jax.ShapeDtypeStruct((2, kl, mu, orbitals), jnp.float32),

time: 186 us -> 185 us (level)
  no operation moved by 1% of the time
where the time goes in v7:
time: 185 us; the launch traced here: 184 us
  waiting for transfers between devices  102 us (55%)
  starting transfers between devices  65.8 us (36%)
  Pallas kernels  11.3 us (6%)
  local copies, waits for them, and re-layouts  3.78 us (2%)
    all_to_all x3, waiting for transfers between devices, swap(): return lax.all_to_all(blocks, axes, split_axis=0, concat_axis=0, tiled=True)  57.9 us
    ppermute x9, waiting for transfers between devices, shift(): return lax.ppermute(block, 'x', [(i, (i + d) % XS) for i in range(XS)])  37.3 us
    all_to_all x3, starting transfers between devices, swap(): return lax.all_to_all(blocks, axes, split_axis=0, concat_axis=0, tiled=True)  29.5 us
    ppermute x9, starting transfers between devices, shift(): return lax.ppermute(block, 'x', [(i, (i + d) % XS) for i in range(XS)])  27.5 us
    ppermute x1, starting transfers between devices, on_device(): other = lax.ppermute(right, 'zh', [(0, 1), (1, 0)])  8.8 us
    ppermute x1, waiting for transfers between devices, on_device(): other = lax.ppermute(right, 'zh', [(0, 1), (1, 0)])  7.33 us
    pallas_call x1, Pallas kernels, apply(): pl.pallas_call(functools.partial(apply_kernel, plan), grid_spec=pltpu.Pre...  4.62 us
  transfers between devices with their start and end apart: 13, of which 9 were waited for; matrix products, arithmetic and copies ran while one was open for 1% of the time, Pallas kernels for 1%

profile of v7, /device:TPU:33, one launch (start us, length us, event | category | flops | bytes accessed | tf_op | source)
XLA Modules:
  0.0 183.9 jit_solution(18306185778123285045)
XLA Ops:
  0.0 8.8 %collective-permute-start.3 = (bf16[2,4,16,512]{3,2,1,0:T(8,128)(2,1)}, bf16[2,4,16,512]{3,2,1,0:T(8,128)(2,1)S(1)}, u32[]{:S(2)}, u32[]{:S(2)}) collective-permute-start(bf16[2,4,16,512]{3,2,1,0:T(8,128)(2,1)} %right_ref.1), channel_id=1, source_target_pairs={{0,4},{4,0},{1,5},{5,1},{2,6},{6,2},{3,7},{7,3},{8,12},{12,8},{9,1... | collective-permute-start | bytes 393224 | tf_op jit(solution)/shard_map/ppermute | solution.py:233
  8.8 0.0 copy-start.4
  8.8 0.9 copy-done.4
  9.7 0.8 send.2.refs_0_
  10.6 0.0 copy-start
  10.6 7.3 %collective-permute-done.3.right_ref = bf16[2,4,16,512]{3,2,1,0:T(8,128)(2,1)S(1)} collective-permute-done((bf16[2,4,16,512]{3,2,1,0:T(8,128)(2,1)}, bf16[2,4,16,512]{3,2,1,0:T(8,128)(2,1)S(1)}, u32[]{:S(2)}, u32[]{:S(2)}) %collective-permute-start.3) | collective-permute-done | bytes 131104 | tf_op jit(solution)/shard_map/ppermute | solution.py:233
  17.9 0.8 send.3
  18.7 9.4 %all-to-all-start = ((bf16[16,2,2,16,512]{4,3,2,1,0:T(8,128)(2,1)}), bf16[16,2,2,16,512]{4,3,2,1,0:T(8,128)(2,1)S(1)}, u32[]{:S(2)}, u32[]{:S(2)}) async-start(bf16[16,2,2,16,512]{4,3,2,1,0:T(8,128)(2,1)} %bitcast.2), calls=%async_computation | async-start | bytes 2097152 | tf_op jit(solution)/shard_map/all_to_all | solution.py:221
  28.1 0.0 copy-done
  28.1 0.8 constant_dynamic-slice_fusion
  28.9 4.3 %collective-permute-start.2 = (bf16[2,1,128,512]{3,2,1,0:T(8,128)(2,1)}, bf16[2,1,128,512]{3,2,1,0:T(8,128)(2,1)S(1)}, u32[]{:S(2)}, u32[]{:S(2)}) collective-permute-start(bf16[2,1,128,512]{3,2,1,0:T(8,128)(2,1)} %get-tuple-element.13), channel_id=1, source_target_pairs={{0,24},{8,0},{16,8},{24,16},{1,25},{9,1},{17,9},{25,17},{2,26},{10... | collective-permute-start | bytes 786440 | tf_op jit(solution)/shard_map/ppermute | solution.py:225
  33.2 2.5 %collective-permute-start.1 = (bf16[2,1,128,512]{3,2,1,0:T(8,128)(2,1)S(1)}, bf16[2,1,128,512]{3,2,1,0:T(8,128)(2,1)S(1)}, u32[]{:S(2)}, u32[]{:S(2)}) collective-permute-start(bf16[2,1,128,512]{3,2,1,0:T(8,128)(2,1)S(1)} %get-tuple-element.14), channel_id=1, source_target_pairs={{0,16},{8,24},{16,0},{24,8},{1,17},{9,25},{17,1},{25,9},{2,18},{10... | collective-permute-start | bytes 786440 | tf_op jit(solution)/shard_map/ppermute | solution.py:225
  35.7 2.5 %collective-permute-start = (bf16[2,1,128,512]{3,2,1,0:T(8,128)(2,1)S(1)}, bf16[2,1,128,512]{3,2,1,0:T(8,128)(2,1)S(1)}, u32[]{:S(2)}, u32[]{:S(2)}) collective-permute-start(bf16[2,1,128,512]{3,2,1,0:T(8,128)(2,1)S(1)} %get-tuple-element.15), channel_id=1, source_target_pairs={{0,8},{8,16},{16,24},{24,0},{1,9},{9,17},{17,25},{25,1},{2,10},{10... | collective-permute-start | bytes 786440 | tf_op jit(solution)/shard_map/ppermute | solution.py:225
  38.2 0.1 pad_add_fusion.place_ref
  38.3 3.6 %collective-permute-done.2.refs_3_ = bf16[2,1,128,512]{3,2,1,0:T(8,128)(2,1)S(1)} collective-permute-done((bf16[2,1,128,512]{3,2,1,0:T(8,128)(2,1)}, bf16[2,1,128,512]{3,2,1,0:T(8,128)(2,1)S(1)}, u32[]{:S(2)}, u32[]{:S(2)}) %collective-permute-start.2) | collective-permute-done | bytes 262176 | tf_op jit(solution)/shard_map/ppermute | solution.py:225
  41.9 4.4 %collective-permute-done.1.refs_2_ = bf16[2,1,128,512]{3,2,1,0:T(8,128)(2,1)S(1)} collective-permute-done((bf16[2,1,128,512]{3,2,1,0:T(8,128)(2,1)S(1)}, bf16[2,1,128,512]{3,2,1,0:T(8,128)(2,1)S(1)}, u32[]{:S(2)}, u32[]{:S(2)}) %collective-permute-start.1) | collective-permute-done | bytes 262176 | tf_op jit(solution)/shard_map/ppermute | solution.py:225
  46.3 10.6 %collective-permute-done.refs_1_ = bf16[2,1,128,512]{3,2,1,0:T(8,128)(2,1)S(1)} collective-permute-done((bf16[2,1,128,512]{3,2,1,0:T(8,128)(2,1)S(1)}, bf16[2,1,128,512]{3,2,1,0:T(8,128)(2,1)S(1)}, u32[]{:S(2)}, u32[]{:S(2)}) %collective-permute-start) | collective-permute-done | bytes 262176 | tf_op jit(solution)/shard_map/ppermute | solution.py:225
  56.9 0.0 all-to-all-done
  56.9 2.6 %pairs.1 = bf16[4,2,2,4,2,32,128]{6,5,4,3,2,1,0:T(8,128)(2,1)} custom-call(s32[2]{0:T(128)S(1)} %pad_add_fusion.place_ref, bf16[2,4,128,512]{3,2,1,0:T(8,128)(2,1)S(1)} %copy-done, bf16[2,1,128,512]{3,2,1,0:T(8,128)(2,1)S(1)} %collective-permute-done.refs_1_, bf16[2,1,128,512]{3,2,1,0:T(8,128)(2,1)S(1)} %collective-permute-done.1.refs_2_, ...), custom_call_target="tpu_custom_call" | custom-call | flops 1073741824 | bytes 3145728 | tf_op jit(solution)/shard_map/pairs/pallas_call | solution.py:71
  59.6 0.0 copy-start.1
  59.6 15.2 %all-to-all-start.1 = ((bf16[64,2,32,128]{3,2,1,0:T(8,128)(2,1)}), bf16[64,2,32,128]{3,2,1,0:T(8,128)(2,1)S(1)}, u32[]{:S(2)}, u32[]{:S(2)}) async-start(bf16[64,2,32,128]{3,2,1,0:T(8,128)(2,1)} %bitcast.4), calls=%async_computation.1 | async-start | bytes 2097152 | tf_op jit(solution)/shard_map/all_to_all | solution.py:221
  74.8 1.1 fusion
  75.9 3.3 %collective-permute-start.4 = (bf16[2,4,2,2,16,512]{5,4,3,2,1,0:T(8,128)(2,1)}, bf16[2,4,2,2,16,512]{5,4,3,2,1,0:T(8,128)(2,1)S(1)}, u32[]{:S(2)}, u32[]{:S(2)}) collective-permute-start(bf16[2,4,2,2,16,512]{5,4,3,2,1,0:T(8,128)(2,1)} %bitcast.5), channel_id=1, source_target_pairs={{0,8},{8,16},{16,24},{24,0},{1,9},{9,17},{17,25},{25,1},{2,10},{10... | collective-permute-start | bytes 1572872 | tf_op jit(solution)/shard_map/ppermute | solution.py:225
  79.1 3.2 %collective-permute-start.5 = (bf16[2,4,2,2,16,512]{5,4,3,2,1,0:T(8,128)(2,1)}, bf16[2,4,2,2,16,512]{5,4,3,2,1,0:T(8,128)(2,1)}, u32[]{:S(2)}, u32[]{:S(2)}) collective-permute-start(bf16[2,4,2,2,16,512]{5,4,3,2,1,0:T(8,128)(2,1)} %bitcast.6), channel_id=1, source_target_pairs={{0,24},{8,0},{16,8},{24,16},{1,25},{9,1},{17,9},{25,17},{2,26},{10... | collective-permute-start | bytes 1572872 | tf_op jit(solution)/shard_map/ppermute | solution.py:225
  82.4 52.6 %all-to-all-done.1.x_ref = bf16[64,2,32,128]{3,2,1,0:T(8,128)(2,1)S(1)} async-done(((bf16[64,2,32,128]{3,2,1,0:T(8,128)(2,1)}), bf16[64,2,32,128]{3,2,1,0:T(8,128)(2,1)S(1)}, u32[]{:S(2)}, u32[]{:S(2)}) %all-to-all-start.1) | async-done | bytes 1048608 | tf_op jit(solution)/shard_map/all_to_all | solution.py:221
  134.9 0.0 copy-done.1
  134.9 2.4 %spectral.1 = bf16[64,2,32,128]{3,2,1,0:T(8,128)(2,1)} custom-call(bf16[64,2,32,128]{3,2,1,0:T(8,128)(2,1)S(1)} %all-to-all-done.1.x_ref, bf16[64,32,128]{2,1,0:T(8,128)(2,1)S(1)} %copy-done.1), custom_call_target="tpu_custom_call" | custom-call | flops 8388608 | bytes 2621440 | tf_op jit(solution)/shard_map/spectral/pallas_call | solution.py:136
  137.3 0.0 collective-permute-done.4.refs_1_
  137.3 0.0 copy-start.2
  137.3 0.0 collective-permute-done.5.refs_2_
  137.3 4.9 %all-to-all-start.2 = ((bf16[16,4,2,32,128]{4,3,2,1,0:T(8,128)(2,1)}), bf16[16,4,2,32,128]{4,3,2,1,0:T(8,128)(2,1)}, u32[]{:S(2)}, u32[]{:S(2)}) async-start(bf16[16,4,2,32,128]{4,3,2,1,0:T(8,128)(2,1)} %bitcast.7), calls=%async_computation.2 | async-start | bytes 2097152 | tf_op jit(solution)/shard_map/all_to_all | solution.py:221
  142.2 2.9 %collective-permute-start.9 = (bf16[2,4,2,2,16,512]{5,4,3,2,1,0:T(8,128)(2,1)}, bf16[2,4,2,2,16,512]{5,4,3,2,1,0:T(8,128)(2,1)S(1)}, u32[]{:S(2)}, u32[]{:S(2)}) collective-permute-start(bf16[2,4,2,2,16,512]{5,4,3,2,1,0:T(8,128)(2,1)} %bitcast.5), channel_id=1, source_target_pairs={{0,24},{8,0},{16,8},{24,16},{1,25},{9,1},{17,9},{25,17},{2,26},{10... | collective-permute-start | bytes 1572872 | tf_op jit(solution)/shard_map/ppermute | solution.py:225
  145.1 2.4 %collective-permute-start.6 = (bf16[2,4,2,2,16,512]{5,4,3,2,1,0:T(8,128)(2,1)}, bf16[2,4,2,2,16,512]{5,4,3,2,1,0:T(8,128)(2,1)S(1)}, u32[]{:S(2)}, u32[]{:S(2)}) collective-permute-start(bf16[2,4,2,2,16,512]{5,4,3,2,1,0:T(8,128)(2,1)} %bitcast.6), channel_id=1, source_target_pairs={{0,8},{8,16},{16,24},{24,0},{1,9},{9,17},{17,25},{25,1},{2,10},{10... | collective-permute-start | bytes 1572872 | tf_op jit(solution)/shard_map/ppermute | solution.py:225
  147.5 2.3 %collective-permute-start.7 = (bf16[2,4,2,2,16,512]{5,4,3,2,1,0:T(8,128)(2,1)S(1)}, bf16[2,4,2,2,16,512]{5,4,3,2,1,0:T(8,128)(2,1)S(1)}, u32[]{:S(2)}, u32[]{:S(2)}) collective-permute-start(bf16[2,4,2,2,16,512]{5,4,3,2,1,0:T(8,128)(2,1)S(1)} %collective-permute-done.4.refs_1_), channel_id=1, source_target_pairs={{0,8},{8,16},{16,24},{24,0},{1,9},{9,17},{17,25},{25,1},{2,10},{10... | collective-permute-start | bytes 1572872 | tf_op jit(solution)/shard_map/ppermute | solution.py:225
  149.8 4.2 %collective-permute-start.8 = (bf16[2,4,2,2,16,512]{5,4,3,2,1,0:T(8,128)(2,1)}, bf16[2,4,2,2,16,512]{5,4,3,2,1,0:T(8,128)(2,1)S(1)}, u32[]{:S(2)}, u32[]{:S(2)}) collective-permute-start(bf16[2,4,2,2,16,512]{5,4,3,2,1,0:T(8,128)(2,1)} %collective-permute-done.5.refs_2_), channel_id=1, source_target_pairs={{0,24},{8,0},{16,8},{24,16},{1,25},{9,1},{17,9},{25,17},{2,26},{10... | collective-permute-start | bytes 1572872 | tf_op jit(solution)/shard_map/ppermute | solution.py:225
  154.0 3.6 %collective-permute-done.9 = bf16[2,4,2,2,16,512]{5,4,3,2,1,0:T(8,128)(2,1)S(1)} collective-permute-done((bf16[2,4,2,2,16,512]{5,4,3,2,1,0:T(8,128)(2,1)}, bf16[2,4,2,2,16,512]{5,4,3,2,1,0:T(8,128)(2,1)S(1)}, u32[]{:S(2)}, u32[]{:S(2)}) %collective-permute-start.9) | collective-permute-done | bytes 524320 | tf_op jit(solution)/shard_map/ppermute | solution.py:225
  157.6 3.8 %collective-permute-done.6 = bf16[2,4,2,2,16,512]{5,4,3,2,1,0:T(8,128)(2,1)S(1)} collective-permute-done((bf16[2,4,2,2,16,512]{5,4,3,2,1,0:T(8,128)(2,1)}, bf16[2,4,2,2,16,512]{5,4,3,2,1,0:T(8,128)(2,1)S(1)}, u32[]{:S(2)}, u32[]{:S(2)}) %collective-permute-start.6) | collective-permute-done | bytes 524320 | tf_op jit(solution)/shard_map/ppermute | solution.py:225
  161.4 11.2 %collective-permute-done.7 = bf16[2,4,2,2,16,512]{5,4,3,2,1,0:T(8,128)(2,1)S(1)} collective-permute-done((bf16[2,4,2,2,16,512]{5,4,3,2,1,0:T(8,128)(2,1)S(1)}, bf16[2,4,2,2,16,512]{5,4,3,2,1,0:T(8,128)(2,1)S(1)}, u32[]{:S(2)}, u32[]{:S(2)}) %collective-permute-start.7) | collective-permute-done | bytes 524320 | tf_op jit(solution)/shard_map/ppermute | solution.py:225
  172.6 0.0 copy-done.2
  172.6 0.0 collective-permute-done.8
  172.6 0.3 pad_maximum_fusion.refs_3_
  172.9 5.3 %all-to-all-done.2 = bf16[16,4,2,32,128]{4,3,2,1,0:T(8,128)(2,1)} async-done(((bf16[16,4,2,32,128]{4,3,2,1,0:T(8,128)(2,1)}), bf16[16,4,2,32,128]{4,3,2,1,0:T(8,128)(2,1)}, u32[]{:S(2)}, u32[]{:S(2)}) %all-to-all-start.2) | async-done | bytes 1048608 | tf_op jit(solution)/shard_map/all_to_all | solution.py:221
  178.2 0.0 copy-start.3
  178.2 1.0 copy-done.3
  179.2 4.6 %apply.1 = f32[2,4,128,512]{3,2,1,0:T(8,128)} custom-call(s32[2]{0:T(128)S(1)} %pad_add_fusion.place_ref, bf16[4,2,2,4,2,32,128]{6,5,4,3,2,1,0:T(8,128)(2,1)} %bitcast.8.kernel_ref, bf16[4,4,2,2,16,512]{5,4,3,2,1,0:T(8,128)(2,1)S(1)} %bitcast.10, bf16[2,4,2,2,16,512]{5,4,3,2,1,0:T(8,128)(2,1)S(1)} %copy-done.3, ...), custom_call_target="tpu_custom_call" | custom-call | flops 1073741824 | bytes 7340032 | tf_op jit(solution)/shard_map/apply/pallas_call | solution.py:196
Async XLA Ops:
  0.0 17.9 %collective-permute-start.3 = (bf16[2,4,16,512]{3,2,1,0:T(8,128)(2,1)}, bf16[2,4,16,512]{3,2,1,0:T(8,128)(2,1)S(1)}, u32[]{:S(2)}, u32[]{:S(2)}) collective-permute-start(bf16[2,4,16,512]{3,2,1,0:T(8,128)(2,1)} %right_ref.1), channel_id=1, source_target_pairs={{0,4},{4,0},{1,5},{5,1},{2,6},{6,2},{3,7},{7,3},{8,12},{12,8},{9,1... | collective-permute-start | bytes 393224 | tf_op jit(solution)/shard_map/ppermute | solution.py:233
  8.8 0.9 copy-start.4
  10.6 17.6 %copy-start = (bf16[2,4,128,512]{3,2,1,0:T(8,128)(2,1)S(1)}, bf16[2,4,128,512]{3,2,1,0:T(8,128)(2,1)}, u32[]{:S(2)}) copy-start(bf16[2,4,128,512]{3,2,1,0:T(8,128)(2,1)} %refs_0_.1) | copy-start | bytes 3145732
  18.7 38.2 %all-to-all-start = ((bf16[16,2,2,16,512]{4,3,2,1,0:T(8,128)(2,1)}), bf16[16,2,2,16,512]{4,3,2,1,0:T(8,128)(2,1)S(1)}, u32[]{:S(2)}, u32[]{:S(2)}) async-start(bf16[16,2,2,16,512]{4,3,2,1,0:T(8,128)(2,1)} %bitcast.2), calls=%async_computation | async-start | bytes 2097152 | tf_op jit(solution)/shard_map/all_to_all | solution.py:221
  28.9 13.0 %collective-permute-start.2 = (bf16[2,1,128,512]{3,2,1,0:T(8,128)(2,1)}, bf16[2,1,128,512]{3,2,1,0:T(8,128)(2,1)S(1)}, u32[]{:S(2)}, u32[]{:S(2)}) collective-permute-start(bf16[2,1,128,512]{3,2,1,0:T(8,128)(2,1)} %get-tuple-element.13), channel_id=1, source_target_pairs={{0,24},{8,0},{16,8},{24,16},{1,25},{9,1},{17,9},{25,17},{2,26},{10... | collective-permute-start | bytes 786440 | tf_op jit(solution)/shard_map/ppermute | solution.py:225
  33.2 13.1 %collective-permute-start.1 = (bf16[2,1,128,512]{3,2,1,0:T(8,128)(2,1)S(1)}, bf16[2,1,128,512]{3,2,1,0:T(8,128)(2,1)S(1)}, u32[]{:S(2)}, u32[]{:S(2)}) collective-permute-start(bf16[2,1,128,512]{3,2,1,0:T(8,128)(2,1)S(1)} %get-tuple-element.14), channel_id=1, source_target_pairs={{0,16},{8,24},{16,0},{24,8},{1,17},{9,25},{17,1},{25,9},{2,18},{10... | collective-permute-start | bytes 786440 | tf_op jit(solution)/shard_map/ppermute | solution.py:225
  35.7 21.2 %collective-permute-start = (bf16[2,1,128,512]{3,2,1,0:T(8,128)(2,1)S(1)}, bf16[2,1,128,512]{3,2,1,0:T(8,128)(2,1)S(1)}, u32[]{:S(2)}, u32[]{:S(2)}) collective-permute-start(bf16[2,1,128,512]{3,2,1,0:T(8,128)(2,1)S(1)} %get-tuple-element.15), channel_id=1, source_target_pairs={{0,8},{8,16},{16,24},{24,0},{1,9},{9,17},{17,25},{25,1},{2,10},{10... | collective-permute-start | bytes 786440 | tf_op jit(solution)/shard_map/ppermute | solution.py:225
  59.6 75.4 %copy-start.1 = (bf16[64,32,128]{2,1,0:T(8,128)(2,1)S(1)}, bf16[64,32,128]{2,1,0:T(8,128)(2,1)}, u32[]{:S(2)}) copy-start(bf16[64,32,128]{2,1,0:T(8,128)(2,1)} %c_ref.1) | copy-start | bytes 1572868
  59.6 75.3 %all-to-all-start.1 = ((bf16[64,2,32,128]{3,2,1,0:T(8,128)(2,1)}), bf16[64,2,32,128]{3,2,1,0:T(8,128)(2,1)S(1)}, u32[]{:S(2)}, u32[]{:S(2)}) async-start(bf16[64,2,32,128]{3,2,1,0:T(8,128)(2,1)} %bitcast.4), calls=%async_computation.1 | async-start | bytes 2097152 | tf_op jit(solution)/shard_map/all_to_all | solution.py:221
  75.9 61.4 %collective-permute-start.4 = (bf16[2,4,2,2,16,512]{5,4,3,2,1,0:T(8,128)(2,1)}, bf16[2,4,2,2,16,512]{5,4,3,2,1,0:T(8,128)(2,1)S(1)}, u32[]{:S(2)}, u32[]{:S(2)}) collective-permute-start(bf16[2,4,2,2,16,512]{5,4,3,2,1,0:T(8,128)(2,1)} %bitcast.5), channel_id=1, source_target_pairs={{0,8},{8,16},{16,24},{24,0},{1,9},{9,17},{17,25},{25,1},{2,10},{10... | collective-permute-start | bytes 1572872 | tf_op jit(solution)/shard_map/ppermute | solution.py:225
  79.1 58.2 %collective-permute-start.5 = (bf16[2,4,2,2,16,512]{5,4,3,2,1,0:T(8,128)(2,1)}, bf16[2,4,2,2,16,512]{5,4,3,2,1,0:T(8,128)(2,1)}, u32[]{:S(2)}, u32[]{:S(2)}) collective-permute-start(bf16[2,4,2,2,16,512]{5,4,3,2,1,0:T(8,128)(2,1)} %bitcast.6), channel_id=1, source_target_pairs={{0,24},{8,0},{16,8},{24,16},{1,25},{9,1},{17,9},{25,17},{2,26},{10... | collective-permute-start | bytes 1572872 | tf_op jit(solution)/shard_map/ppermute | solution.py:225
  137.3 35.3 %copy-start.2 = (bf16[2,4,2,2,16,512]{5,4,3,2,1,0:T(8,128)(2,1)}, bf16[2,4,2,2,16,512]{5,4,3,2,1,0:T(8,128)(2,1)S(1)}, u32[]{:S(2)}) copy-start(bf16[2,4,2,2,16,512]{5,4,3,2,1,0:T(8,128)(2,1)S(1)} %collective-permute-done.4.refs_1_) | copy-start | bytes 1572868
  137.3 40.9 %all-to-all-start.2 = ((bf16[16,4,2,32,128]{4,3,2,1,0:T(8,128)(2,1)}), bf16[16,4,2,32,128]{4,3,2,1,0:T(8,128)(2,1)}, u32[]{:S(2)}, u32[]{:S(2)}) async-start(bf16[16,4,2,32,128]{4,3,2,1,0:T(8,128)(2,1)} %bitcast.7), calls=%async_computation.2 | async-start | bytes 2097152 | tf_op jit(solution)/shard_map/all_to_all | solution.py:221
  142.2 15.4 %collective-permute-start.9 = (bf16[2,4,2,2,16,512]{5,4,3,2,1,0:T(8,128)(2,1)}, bf16[2,4,2,2,16,512]{5,4,3,2,1,0:T(8,128)(2,1)S(1)}, u32[]{:S(2)}, u32[]{:S(2)}) collective-permute-start(bf16[2,4,2,2,16,512]{5,4,3,2,1,0:T(8,128)(2,1)} %bitcast.5), channel_id=1, source_target_pairs={{0,24},{8,0},{16,8},{24,16},{1,25},{9,1},{17,9},{25,17},{2,26},{10... | collective-permute-start | bytes 1572872 | tf_op jit(solution)/shard_map/ppermute | solution.py:225
  145.1 16.3 %collective-permute-start.6 = (bf16[2,4,2,2,16,512]{5,4,3,2,1,0:T(8,128)(2,1)}, bf16[2,4,2,2,16,512]{5,4,3,2,1,0:T(8,128)(2,1)S(1)}, u32[]{:S(2)}, u32[]{:S(2)}) collective-permute-start(bf16[2,4,2,2,16,512]{5,4,3,2,1,0:T(8,128)(2,1)} %bitcast.6), channel_id=1, source_target_pairs={{0,8},{8,16},{16,24},{24,0},{1,9},{9,17},{17,25},{25,1},{2,10},{10... | collective-permute-start | bytes 1572872 | tf_op jit(solution)/shard_map/ppermute | solution.py:225
  147.5 25.1 %collective-permute-start.7 = (bf16[2,4,2,2,16,512]{5,4,3,2,1,0:T(8,128)(2,1)S(1)}, bf16[2,4,2,2,16,512]{5,4,3,2,1,0:T(8,128)(2,1)S(1)}, u32[]{:S(2)}, u32[]{:S(2)}) collective-permute-start(bf16[2,4,2,2,16,512]{5,4,3,2,1,0:T(8,128)(2,1)S(1)} %collective-permute-done.4.refs_1_), channel_id=1, source_target_pairs={{0,8},{8,16},{16,24},{24,0},{1,9},{9,17},{17,25},{25,1},{2,10},{10... | collective-permute-start | bytes 1572872 | tf_op jit(solution)/shard_map/ppermute | solution.py:225
  149.8 22.8 %collective-permute-start.8 = (bf16[2,4,2,2,16,512]{5,4,3,2,1,0:T(8,128)(2,1)}, bf16[2,4,2,2,16,512]{5,4,3,2,1,0:T(8,128)(2,1)S(1)}, u32[]{:S(2)}, u32[]{:S(2)}) collective-permute-start(bf16[2,4,2,2,16,512]{5,4,3,2,1,0:T(8,128)(2,1)} %collective-permute-done.5.refs_2_), channel_id=1, source_target_pairs={{0,24},{8,0},{16,8},{24,16},{1,25},{9,1},{17,9},{25,17},{2,26},{10... | collective-permute-start | bytes 1572872 | tf_op jit(solution)/shard_map/ppermute | solution.py:225
  178.2 1.0 copy-start.3

commit v8 on v7

--- a/solution.py
+++ b/solution.py
@@ -105,41 +105,51 @@
     return out
 
 
-def spectral_kernel(x_ref, c_ref, out_ref, work_ref):
-    for top in range(4):
-        values = [
-            tuple(x_ref[16 * top + low, part].astype(jnp.float32) for part in range(2)) for low in range(16)
-        ]
-        for low, (re, im) in enumerate(dft16(values, -1)):
-            work_ref[0, 16 * top + low] = re
-            work_ref[1, 16 * top + low] = im
-    for low in range(16):
-        values = [(work_ref[0, 16 * top + low], work_ref[1, 16 * top + low]) for top in range(4)]
-        weighted = []
-        for top, (re, im) in enumerate(dft4(values, -1)):
-            c = c_ref[16 * top + low].astype(jnp.float32)
-            weighted.append(tuple((c * part).astype(jnp.bfloat16).astype(jnp.float32) for part in (re, im)))
-        for top, (re, im) in enumerate(dft4(weighted, 1)):
-            work_ref[0, 16 * top + low] = re
-            work_ref[1, 16 * top + low] = im
-    for top in range(4):
-        values = [(work_ref[0, 16 * top + low], work_ref[1, 16 * top + low]) for low in range(16)]
-        for low, parts in enumerate(dft16(values, 1)):
-            for part in range(2):
-                out_ref[16 * top + low, part] = (parts[part] * (1.0 / 64.0)).astype(jnp.bfloat16)
+def spectral_kernel(x_ref, c_ref, out_ref, work_ref, done_ref, sems):
+    rows = work_ref.shape[2]
+    copies = []
+    for n in range(done_ref.shape[0]):
+        at = slice(n * rows, (n + 1) * rows)
+        for top in range(4):
+            values = [
+                tuple(x_ref[16 * top + low, part, at].astype(jnp.float32) for part in range(2)) for low in range(16)
+            ]
+            for low, (re, im) in enumerate(dft16(values, -1)):
+                work_ref[0, 16 * top + low] = re
+                work_ref[1, 16 * top + low] = im
+        for low in range(16):
+            values = [(work_ref[0, 16 * top + low], work_ref[1, 16 * top + low]) for top in range(4)]
+            weighted = []
+            for top, (re, im) in enumerate(dft4(values, -1)):
+                c = c_ref[16 * top + low, at].astype(jnp.float32)
+                weighted.append(tuple((c * part).astype(jnp.bfloat16).astype(jnp.float32) for part in (re, im)))
+            for top, (re, im) in enumerate(dft4(weighted, 1)):
+                work_ref[0, 16 * top + low] = re
+                work_ref[1, 16 * top + low] = im
+        for top in range(4):
+            values = [(work_ref[0, 16 * top + low], work_ref[1, 16 * top + low]) for low in range(16)]
+            for low, parts in enumerate(dft16(values, 1)):
+                for part in range(2):
+                    done_ref[n, 16 * top + low, part] = (parts[part] * (1.0 / 64.0)).astype(jnp.bfloat16)
+        copies.append(pltpu.make_async_copy(done_ref.at[n], out_ref.at[:, :, pl.ds(n * rows, rows)], sems.at[n]))
+        copies[-1].start()
+    for copy in copies:
+        copy.wait()
 
 
 def spectral(x, coulomb):
     count, _, nus, mu = x.shape
     rows = 16
-    block = pl.BlockSpec((count, 2, rows, mu), lambda n: (0, 0, n, 0))
     return pl.pallas_call(
         spectral_kernel,
-        grid=(nus // rows,),
-        in_specs=[block, pl.BlockSpec((count, rows, mu), lambda n: (0, n, 0))],
-        out_specs=block,
+        in_specs=[pl.BlockSpec(memory_space=pltpu.VMEM)] * 2,
+        out_specs=pl.BlockSpec(memory_space=pl.ANY),
         out_shape=jax.ShapeDtypeStruct(x.shape, jnp.bfloat16),
-        scratch_shapes=[pltpu.VMEM((2, count, rows, mu), jnp.float32)],
+        scratch_shapes=[
+            pltpu.VMEM((2, count, rows, mu), jnp.float32),
+            pltpu.VMEM((nus // rows, count, 2, rows, mu), jnp.bfloat16),
+            pltpu.SemaphoreType.DMA((nus // rows,)),
+        ],
         compiler_params=VMEM,
         cost_estimate=pl.CostEstimate(flops=32 * count * nus * mu, bytes_accessed=5 << 19, transcendentals=0),
         name="spectral",
@@ -244,15 +254,16 @@
     spatial = spectral(columns, coulomb)
     spatial, up, down = lax.optimization_barrier((spatial, shift(low, 1), shift(high, XS - 1)))
     late = jnp.concatenate([shift(high, 1), shift(up, 1), shift(down, XS - 1), shift(low, XS - 1)])
+    early = jnp.concatenate([up, down])
     half = XS // 2
     plan = [
         [(0, 0, XS)],
-        [(1, 0, half), (3, 0, half)],
-        [(3, half, XS)],
-        [(3, half + XS, half), (2, 0, half)],
+        [(1, 0, half), (2, 0, half)],
+        [(2, half, XS)],
+        [(2, half + XS, half), (1, half, half)],
     ]
     kernel = swap(spatial.reshape(KG, KL, parts, 2 * nus, mu), "kg")
-    return apply(place, kernel.reshape(XS, ZH, ZQ // 2, KL, parts, 2 * nus, mu), [mine, up, down, late], plan)
+    return apply(place, kernel.reshape(XS, ZH, ZQ // 2, KL, parts, 2 * nus, mu), [mine, early, late], plan)
 
 
 def solution(mesh):

time: 185 us -> 185 us (level)
  other arithmetic: 0.34 us -> 2.61 us
  waiting for transfers between devices: 102 us -> 100 us
    ppermute x9, waiting for transfers between devices: 37.3 us -> 34.8 us  [shift(): return lax.ppermute(block, 'x', [(i, (i + d) % XS) for i in range(XS)])]
    concatenate x0 -> x1, other arithmetic: none -> 2.27 us  [on_device(): early = jnp.concatenate([up, down])]
  transfers between devices with their start and end apart: 13 -> 13, of which waited for: 9 -> 9; matrix products, arithmetic and copies ran while one was open for 1% -> 2% of each run, Pallas kernels for 1% -> 1%
where the time goes in v8:
time: 185 us; the launch traced here: 184 us
  waiting for transfers between devices  100 us (54%)
  starting transfers between devices  65.8 us (36%)
  Pallas kernels  10.9 us (6%)
  local copies, waits for them, and re-layouts  3.79 us (2%)
  other arithmetic  2.61 us (1%)
    all_to_all x3, waiting for transfers between devices, swap(): return lax.all_to_all(blocks, axes, split_axis=0, concat_axis=0, tiled=True)  58.4 us
    ppermute x9, waiting for transfers between devices, shift(): return lax.ppermute(block, 'x', [(i, (i + d) % XS) for i in range(XS)])  34.8 us
    all_to_all x3, starting transfers between devices, swap(): return lax.all_to_all(blocks, axes, split_axis=0, concat_axis=0, tiled=True)  29.5 us
    ppermute x9, starting transfers between devices, shift(): return lax.ppermute(block, 'x', [(i, (i + d) % XS) for i in range(XS)])  27.5 us
    ppermute x1, starting transfers between devices, on_device(): other = lax.ppermute(right, 'zh', [(0, 1), (1, 0)])  8.8 us
    ppermute x1, waiting for transfers between devices, on_device(): other = lax.ppermute(right, 'zh', [(0, 1), (1, 0)])  7.33 us
    pallas_call x1, Pallas kernels, apply(): pl.pallas_call(functools.partial(apply_kernel, plan), grid_spec=pltpu.Pre...  4.37 us
  transfers between devices with their start and end apart: 13, of which 9 were waited for; matrix products, arithmetic and copies ran while one was open for 2% of the time, Pallas kernels for 1%

profile of v8, /device:TPU:33, one launch (start us, length us, event | category | flops | bytes accessed | tf_op | source)
XLA Modules:
  0.0 183.8 jit_solution(10690857982588073447)
XLA Ops:
  0.0 8.8 %collective-permute-start.3 = (bf16[2,4,16,512]{3,2,1,0:T(8,128)(2,1)}, bf16[2,4,16,512]{3,2,1,0:T(8,128)(2,1)S(1)}, u32[]{:S(2)}, u32[]{:S(2)}) collective-permute-start(bf16[2,4,16,512]{3,2,1,0:T(8,128)(2,1)} %right_ref.1), channel_id=1, source_target_pairs={{0,4},{4,0},{1,5},{5,1},{2,6},{6,2},{3,7},{7,3},{8,12},{12,8},{9,1... | collective-permute-start | bytes 393224 | tf_op jit(solution)/shard_map/ppermute | solution.py:243
  8.8 0.0 copy-start.3
  8.8 0.9 copy-done.3
  9.7 0.8 send.2.refs_0_
  10.6 0.0 copy-start.1
  10.6 7.3 %collective-permute-done.3.right_ref = bf16[2,4,16,512]{3,2,1,0:T(8,128)(2,1)S(1)} collective-permute-done((bf16[2,4,16,512]{3,2,1,0:T(8,128)(2,1)}, bf16[2,4,16,512]{3,2,1,0:T(8,128)(2,1)S(1)}, u32[]{:S(2)}, u32[]{:S(2)}) %collective-permute-start.3) | collective-permute-done | bytes 131104 | tf_op jit(solution)/shard_map/ppermute | solution.py:243
  17.9 0.8 send.3
  18.7 9.4 %all-to-all-start = ((bf16[16,2,2,16,512]{4,3,2,1,0:T(8,128)(2,1)}), bf16[16,2,2,16,512]{4,3,2,1,0:T(8,128)(2,1)S(1)}, u32[]{:S(2)}, u32[]{:S(2)}) async-start(bf16[16,2,2,16,512]{4,3,2,1,0:T(8,128)(2,1)} %bitcast.2), calls=%async_computation | async-start | bytes 2097152 | tf_op jit(solution)/shard_map/all_to_all | solution.py:231
  28.1 0.0 copy-done.1
  28.1 0.8 constant_dynamic-slice_fusion
  28.9 4.3 %collective-permute-start.2 = (bf16[2,1,128,512]{3,2,1,0:T(8,128)(2,1)}, bf16[2,1,128,512]{3,2,1,0:T(8,128)(2,1)S(1)}, u32[]{:S(2)}, u32[]{:S(2)}) collective-permute-start(bf16[2,1,128,512]{3,2,1,0:T(8,128)(2,1)} %get-tuple-element.13), channel_id=1, source_target_pairs={{0,24},{8,0},{16,8},{24,16},{1,25},{9,1},{17,9},{25,17},{2,26},{10... | collective-permute-start | bytes 786440 | tf_op jit(solution)/shard_map/ppermute | solution.py:235
  33.2 2.5 %collective-permute-start.1 = (bf16[2,1,128,512]{3,2,1,0:T(8,128)(2,1)S(1)}, bf16[2,1,128,512]{3,2,1,0:T(8,128)(2,1)S(1)}, u32[]{:S(2)}, u32[]{:S(2)}) collective-permute-start(bf16[2,1,128,512]{3,2,1,0:T(8,128)(2,1)S(1)} %get-tuple-element.14), channel_id=1, source_target_pairs={{0,16},{8,24},{16,0},{24,8},{1,17},{9,25},{17,1},{25,9},{2,18},{10... | collective-permute-start | bytes 786440 | tf_op jit(solution)/shard_map/ppermute | solution.py:235
  35.7 2.5 %collective-permute-start = (bf16[2,1,128,512]{3,2,1,0:T(8,128)(2,1)S(1)}, bf16[2,1,128,512]{3,2,1,0:T(8,128)(2,1)S(1)}, u32[]{:S(2)}, u32[]{:S(2)}) collective-permute-start(bf16[2,1,128,512]{3,2,1,0:T(8,128)(2,1)S(1)} %get-tuple-element.15), channel_id=1, source_target_pairs={{0,8},{8,16},{16,24},{24,0},{1,9},{9,17},{17,25},{25,1},{2,10},{10... | collective-permute-start | bytes 786440 | tf_op jit(solution)/shard_map/ppermute | solution.py:235
  38.2 0.1 pad_add_fusion.place_ref
  38.3 3.6 %collective-permute-done.2.refs_3_ = bf16[2,1,128,512]{3,2,1,0:T(8,128)(2,1)S(1)} collective-permute-done((bf16[2,1,128,512]{3,2,1,0:T(8,128)(2,1)}, bf16[2,1,128,512]{3,2,1,0:T(8,128)(2,1)S(1)}, u32[]{:S(2)}, u32[]{:S(2)}) %collective-permute-start.2) | collective-permute-done | bytes 262176 | tf_op jit(solution)/shard_map/ppermute | solution.py:235
  41.9 4.4 %collective-permute-done.1.refs_2_ = bf16[2,1,128,512]{3,2,1,0:T(8,128)(2,1)S(1)} collective-permute-done((bf16[2,1,128,512]{3,2,1,0:T(8,128)(2,1)S(1)}, bf16[2,1,128,512]{3,2,1,0:T(8,128)(2,1)S(1)}, u32[]{:S(2)}, u32[]{:S(2)}) %collective-permute-start.1) | collective-permute-done | bytes 262176 | tf_op jit(solution)/shard_map/ppermute | solution.py:235
  46.3 10.6 %collective-permute-done.refs_1_ = bf16[2,1,128,512]{3,2,1,0:T(8,128)(2,1)S(1)} collective-permute-done((bf16[2,1,128,512]{3,2,1,0:T(8,128)(2,1)S(1)}, bf16[2,1,128,512]{3,2,1,0:T(8,128)(2,1)S(1)}, u32[]{:S(2)}, u32[]{:S(2)}) %collective-permute-start) | collective-permute-done | bytes 262176 | tf_op jit(solution)/shard_map/ppermute | solution.py:235
  56.9 0.0 all-to-all-done
  56.9 2.6 %pairs.1 = bf16[4,2,2,4,2,32,128]{6,5,4,3,2,1,0:T(8,128)(2,1)} custom-call(s32[2]{0:T(128)S(1)} %pad_add_fusion.place_ref, bf16[2,4,128,512]{3,2,1,0:T(8,128)(2,1)S(1)} %copy-done.1, bf16[2,1,128,512]{3,2,1,0:T(8,128)(2,1)S(1)} %collective-permute-done.refs_1_, bf16[2,1,128,512]{3,2,1,0:T(8,128)(2,1)S(1)} %collective-permute-done.1.refs_2_, ...), custom_call_target="tpu_custom_call" | custom-call | flops 1073741824 | bytes 3145728 | tf_op jit(solution)/shard_map/pairs/pallas_call | solution.py:71
  59.6 0.0 copy-start.2
  59.6 15.2 %all-to-all-start.1 = ((bf16[64,2,32,128]{3,2,1,0:T(8,128)(2,1)}), bf16[64,2,32,128]{3,2,1,0:T(8,128)(2,1)S(1)}, u32[]{:S(2)}, u32[]{:S(2)}) async-start(bf16[64,2,32,128]{3,2,1,0:T(8,128)(2,1)} %bitcast.4), calls=%async_computation.1 | async-start | bytes 2097152 | tf_op jit(solution)/shard_map/all_to_all | solution.py:231
  74.8 0.9 fusion
  75.7 3.3 %collective-permute-start.4 = (bf16[2,4,2,2,16,512]{5,4,3,2,1,0:T(8,128)(2,1)}, bf16[2,4,2,2,16,512]{5,4,3,2,1,0:T(8,128)(2,1)}, u32[]{:S(2)}, u32[]{:S(2)}) collective-permute-start(bf16[2,4,2,2,16,512]{5,4,3,2,1,0:T(8,128)(2,1)} %bitcast.5), channel_id=1, source_target_pairs={{0,8},{8,16},{16,24},{24,0},{1,9},{9,17},{17,25},{25,1},{2,10},{10... | collective-permute-start | bytes 1572872 | tf_op jit(solution)/shard_map/ppermute | solution.py:235
  79.0 3.2 %collective-permute-start.5 = (bf16[2,4,2,2,16,512]{5,4,3,2,1,0:T(8,128)(2,1)S(1)}, bf16[2,4,2,2,16,512]{5,4,3,2,1,0:T(8,128)(2,1)}, u32[]{:S(2)}, u32[]{:S(2)}) collective-permute-start(bf16[2,4,2,2,16,512]{5,4,3,2,1,0:T(8,128)(2,1)S(1)} %bitcast.11), channel_id=1, source_target_pairs={{0,24},{8,0},{16,8},{24,16},{1,25},{9,1},{17,9},{25,17},{2,26},{10... | collective-permute-start | bytes 1572872 | tf_op jit(solution)/shard_map/ppermute | solution.py:235
  82.2 52.7 %all-to-all-done.1.x_ref = bf16[64,2,32,128]{3,2,1,0:T(8,128)(2,1)S(1)} async-done(((bf16[64,2,32,128]{3,2,1,0:T(8,128)(2,1)}), bf16[64,2,32,128]{3,2,1,0:T(8,128)(2,1)S(1)}, u32[]{:S(2)}, u32[]{:S(2)}) %all-to-all-start.1) | async-done | bytes 1048608 | tf_op jit(solution)/shard_map/all_to_all | solution.py:231
  134.9 0.0 copy-done.2
  134.9 2.2 %spectral.1 = bf16[64,2,32,128]{3,2,1,0:T(8,128)(2,1)} custom-call(bf16[64,2,32,128]{3,2,1,0:T(8,128)(2,1)S(1)} %all-to-all-done.1.x_ref, bf16[64,32,128]{2,1,0:T(8,128)(2,1)S(1)} %copy-done.2), custom_call_target="tpu_custom_call" | custom-call | flops 8388608 | bytes 2621440 | tf_op jit(solution)/shard_map/spectral/pallas_call | solution.py:143
  137.2 0.0 collective-permute-done.4
  137.2 0.0 collective-permute-done.5
  137.2 4.9 %all-to-all-start.2 = ((bf16[16,4,2,32,128]{4,3,2,1,0:T(8,128)(2,1)}), bf16[16,4,2,32,128]{4,3,2,1,0:T(8,128)(2,1)}, u32[]{:S(2)}, u32[]{:S(2)}) async-start(bf16[16,4,2,32,128]{4,3,2,1,0:T(8,128)(2,1)} %bitcast.7), calls=%async_computation.2 | async-start | bytes 2097152 | tf_op jit(solution)/shard_map/all_to_all | solution.py:231
  142.1 2.9 %collective-permute-start.9 = (bf16[2,4,2,2,16,512]{5,4,3,2,1,0:T(8,128)(2,1)}, bf16[2,4,2,2,16,512]{5,4,3,2,1,0:T(8,128)(2,1)S(1)}, u32[]{:S(2)}, u32[]{:S(2)}) collective-permute-start(bf16[2,4,2,2,16,512]{5,4,3,2,1,0:T(8,128)(2,1)} %bitcast.5), channel_id=1, source_target_pairs={{0,24},{8,0},{16,8},{24,16},{1,25},{9,1},{17,9},{25,17},{2,26},{10... | collective-permute-start | bytes 1572872 | tf_op jit(solution)/shard_map/ppermute | solution.py:235
  144.9 2.4 %collective-permute-start.6 = (bf16[2,4,2,2,16,512]{5,4,3,2,1,0:T(8,128)(2,1)S(1)}, bf16[2,4,2,2,16,512]{5,4,3,2,1,0:T(8,128)(2,1)S(1)}, u32[]{:S(2)}, u32[]{:S(2)}) collective-permute-start(bf16[2,4,2,2,16,512]{5,4,3,2,1,0:T(8,128)(2,1)S(1)} %bitcast.12), channel_id=1, source_target_pairs={{0,8},{8,16},{16,24},{24,0},{1,9},{9,17},{17,25},{25,1},{2,10},{10... | collective-permute-start | bytes 1572872 | tf_op jit(solution)/shard_map/ppermute | solution.py:235
  147.4 2.3 %collective-permute-start.7 = (bf16[2,4,2,2,16,512]{5,4,3,2,1,0:T(8,128)(2,1)}, bf16[2,4,2,2,16,512]{5,4,3,2,1,0:T(8,128)(2,1)S(1)}, u32[]{:S(2)}, u32[]{:S(2)}) collective-permute-start(bf16[2,4,2,2,16,512]{5,4,3,2,1,0:T(8,128)(2,1)} %collective-permute-done.4), channel_id=1, source_target_pairs={{0,8},{8,16},{16,24},{24,0},{1,9},{9,17},{17,25},{25,1},{2,10},{10... | collective-permute-start | bytes 1572872 | tf_op jit(solution)/shard_map/ppermute | solution.py:235
  149.7 4.2 %collective-permute-start.8 = (bf16[2,4,2,2,16,512]{5,4,3,2,1,0:T(8,128)(2,1)}, bf16[2,4,2,2,16,512]{5,4,3,2,1,0:T(8,128)(2,1)S(1)}, u32[]{:S(2)}, u32[]{:S(2)}) collective-permute-start(bf16[2,4,2,2,16,512]{5,4,3,2,1,0:T(8,128)(2,1)} %collective-permute-done.5), channel_id=1, source_target_pairs={{0,24},{8,0},{16,8},{24,16},{1,25},{9,1},{17,9},{25,17},{2,26},{10... | collective-permute-start | bytes 1572872 | tf_op jit(solution)/shard_map/ppermute | solution.py:235
  153.9 2.3 %pad_maximum_fusion.1.refs_1_ = bf16[4,4,2,2,16,512]{5,4,3,2,1,0:T(8,128)(2,1)} fusion(bf16[2,4,2,2,16,512]{5,4,3,2,1,0:T(8,128)(2,1)} %collective-permute-done.5, bf16[2,4,2,2,16,512]{5,4,3,2,1,0:T(8,128)(2,1)} %collective-permute-done.4), kind=kLoop, calls=%fused_computation.1 | loop fusion | flops 524288 | bytes 2097152 | tf_op jit(solution)/shard_map/concatenate | solution.py:257
  156.1 1.4 collective-permute-done.9
  157.5 3.6 %collective-permute-done.6 = bf16[2,4,2,2,16,512]{5,4,3,2,1,0:T(8,128)(2,1)S(1)} collective-permute-done((bf16[2,4,2,2,16,512]{5,4,3,2,1,0:T(8,128)(2,1)S(1)}, bf16[2,4,2,2,16,512]{5,4,3,2,1,0:T(8,128)(2,1)S(1)}, u32[]{:S(2)}, u32[]{:S(2)}) %collective-permute-start.6) | collective-permute-done | bytes 524320 | tf_op jit(solution)/shard_map/ppermute | solution.py:235
  161.1 11.2 %collective-permute-done.7 = bf16[2,4,2,2,16,512]{5,4,3,2,1,0:T(8,128)(2,1)S(1)} collective-permute-done((bf16[2,4,2,2,16,512]{5,4,3,2,1,0:T(8,128)(2,1)}, bf16[2,4,2,2,16,512]{5,4,3,2,1,0:T(8,128)(2,1)S(1)}, u32[]{:S(2)}, u32[]{:S(2)}) %collective-permute-start.7) | collective-permute-done | bytes 524320 | tf_op jit(solution)/shard_map/ppermute | solution.py:235
  172.3 0.0 collective-permute-done.8
  172.3 0.3 pad_maximum_fusion.refs_2_
  172.6 5.6 %all-to-all-done.2 = bf16[16,4,2,32,128]{4,3,2,1,0:T(8,128)(2,1)} async-done(((bf16[16,4,2,32,128]{4,3,2,1,0:T(8,128)(2,1)}), bf16[16,4,2,32,128]{4,3,2,1,0:T(8,128)(2,1)}, u32[]{:S(2)}, u32[]{:S(2)}) %all-to-all-start.2) | async-done | bytes 1048608 | tf_op jit(solution)/shard_map/all_to_all | solution.py:231
  178.2 0.0 copy-start
  178.2 1.2 copy-done
  179.4 4.4 %apply.1 = f32[2,4,128,512]{3,2,1,0:T(8,128)} custom-call(s32[2]{0:T(128)S(1)} %pad_add_fusion.place_ref, bf16[4,2,2,4,2,32,128]{6,5,4,3,2,1,0:T(8,128)(2,1)} %bitcast.8.kernel_ref, bf16[4,4,2,2,16,512]{5,4,3,2,1,0:T(8,128)(2,1)S(1)} %bitcast.10, bf16[4,4,2,2,16,512]{5,4,3,2,1,0:T(8,128)(2,1)S(1)} %copy-done, ...), custom_call_target="tpu_custom_call" | custom-call | flops 1073741824 | bytes 7340032 | tf_op jit(solution)/shard_map/apply/pallas_call | solution.py:206
Async XLA Ops:
  0.0 17.9 %collective-permute-start.3 = (bf16[2,4,16,512]{3,2,1,0:T(8,128)(2,1)}, bf16[2,4,16,512]{3,2,1,0:T(8,128)(2,1)S(1)}, u32[]{:S(2)}, u32[]{:S(2)}) collective-permute-start(bf16[2,4,16,512]{3,2,1,0:T(8,128)(2,1)} %right_ref.1), channel_id=1, source_target_pairs={{0,4},{4,0},{1,5},{5,1},{2,6},{6,2},{3,7},{7,3},{8,12},{12,8},{9,1... | collective-permute-start | bytes 393224 | tf_op jit(solution)/shard_map/ppermute | solution.py:243
  8.8 0.9 copy-start.3
  10.6 17.6 %copy-start.1 = (bf16[2,4,128,512]{3,2,1,0:T(8,128)(2,1)S(1)}, bf16[2,4,128,512]{3,2,1,0:T(8,128)(2,1)}, u32[]{:S(2)}) copy-start(bf16[2,4,128,512]{3,2,1,0:T(8,128)(2,1)} %refs_0_.1) | copy-start | bytes 3145732
  18.7 38.2 %all-to-all-start = ((bf16[16,2,2,16,512]{4,3,2,1,0:T(8,128)(2,1)}), bf16[16,2,2,16,512]{4,3,2,1,0:T(8,128)(2,1)S(1)}, u32[]{:S(2)}, u32[]{:S(2)}) async-start(bf16[16,2,2,16,512]{4,3,2,1,0:T(8,128)(2,1)} %bitcast.2), calls=%async_computation | async-start | bytes 2097152 | tf_op jit(solution)/shard_map/all_to_all | solution.py:231
  28.9 13.0 %collective-permute-start.2 = (bf16[2,1,128,512]{3,2,1,0:T(8,128)(2,1)}, bf16[2,1,128,512]{3,2,1,0:T(8,128)(2,1)S(1)}, u32[]{:S(2)}, u32[]{:S(2)}) collective-permute-start(bf16[2,1,128,512]{3,2,1,0:T(8,128)(2,1)} %get-tuple-element.13), channel_id=1, source_target_pairs={{0,24},{8,0},{16,8},{24,16},{1,25},{9,1},{17,9},{25,17},{2,26},{10... | collective-permute-start | bytes 786440 | tf_op jit(solution)/shard_map/ppermute | solution.py:235
  33.2 13.1 %collective-permute-start.1 = (bf16[2,1,128,512]{3,2,1,0:T(8,128)(2,1)S(1)}, bf16[2,1,128,512]{3,2,1,0:T(8,128)(2,1)S(1)}, u32[]{:S(2)}, u32[]{:S(2)}) collective-permute-start(bf16[2,1,128,512]{3,2,1,0:T(8,128)(2,1)S(1)} %get-tuple-element.14), channel_id=1, source_target_pairs={{0,16},{8,24},{16,0},{24,8},{1,17},{9,25},{17,1},{25,9},{2,18},{10... | collective-permute-start | bytes 786440 | tf_op jit(solution)/shard_map/ppermute | solution.py:235
  35.7 21.2 %collective-permute-start = (bf16[2,1,128,512]{3,2,1,0:T(8,128)(2,1)S(1)}, bf16[2,1,128,512]{3,2,1,0:T(8,128)(2,1)S(1)}, u32[]{:S(2)}, u32[]{:S(2)}) collective-permute-start(bf16[2,1,128,512]{3,2,1,0:T(8,128)(2,1)S(1)} %get-tuple-element.15), channel_id=1, source_target_pairs={{0,8},{8,16},{16,24},{24,0},{1,9},{9,17},{17,25},{25,1},{2,10},{10... | collective-permute-start | bytes 786440 | tf_op jit(solution)/shard_map/ppermute | solution.py:235
  59.6 75.4 %copy-start.2 = (bf16[64,32,128]{2,1,0:T(8,128)(2,1)S(1)}, bf16[64,32,128]{2,1,0:T(8,128)(2,1)}, u32[]{:S(2)}) copy-start(bf16[64,32,128]{2,1,0:T(8,128)(2,1)} %c_ref.1) | copy-start | bytes 1572868
  59.6 75.3 %all-to-all-start.1 = ((bf16[64,2,32,128]{3,2,1,0:T(8,128)(2,1)}), bf16[64,2,32,128]{3,2,1,0:T(8,128)(2,1)S(1)}, u32[]{:S(2)}, u32[]{:S(2)}) async-start(bf16[64,2,32,128]{3,2,1,0:T(8,128)(2,1)} %bitcast.4), calls=%async_computation.1 | async-start | bytes 2097152 | tf_op jit(solution)/shard_map/all_to_all | solution.py:231
  75.7 61.5 %collective-permute-start.4 = (bf16[2,4,2,2,16,512]{5,4,3,2,1,0:T(8,128)(2,1)}, bf16[2,4,2,2,16,512]{5,4,3,2,1,0:T(8,128)(2,1)}, u32[]{:S(2)}, u32[]{:S(2)}) collective-permute-start(bf16[2,4,2,2,16,512]{5,4,3,2,1,0:T(8,128)(2,1)} %bitcast.5), channel_id=1, source_target_pairs={{0,8},{8,16},{16,24},{24,0},{1,9},{9,17},{17,25},{25,1},{2,10},{10... | collective-permute-start | bytes 1572872 | tf_op jit(solution)/shard_map/ppermute | solution.py:235
  79.0 58.2 %collective-permute-start.5 = (bf16[2,4,2,2,16,512]{5,4,3,2,1,0:T(8,128)(2,1)S(1)}, bf16[2,4,2,2,16,512]{5,4,3,2,1,0:T(8,128)(2,1)}, u32[]{:S(2)}, u32[]{:S(2)}) collective-permute-start(bf16[2,4,2,2,16,512]{5,4,3,2,1,0:T(8,128)(2,1)S(1)} %bitcast.11), channel_id=1, source_target_pairs={{0,24},{8,0},{16,8},{24,16},{1,25},{9,1},{17,9},{25,17},{2,26},{10... | collective-permute-start | bytes 1572872 | tf_op jit(solution)/shard_map/ppermute | solution.py:235
  137.2 41.0 %all-to-all-start.2 = ((bf16[16,4,2,32,128]{4,3,2,1,0:T(8,128)(2,1)}), bf16[16,4,2,32,128]{4,3,2,1,0:T(8,128)(2,1)}, u32[]{:S(2)}, u32[]{:S(2)}) async-start(bf16[16,4,2,32,128]{4,3,2,1,0:T(8,128)(2,1)} %bitcast.7), calls=%async_computation.2 | async-start | bytes 2097152 | tf_op jit(solution)/shard_map/all_to_all | solution.py:231
  142.1 15.4 %collective-permute-start.9 = (bf16[2,4,2,2,16,512]{5,4,3,2,1,0:T(8,128)(2,1)}, bf16[2,4,2,2,16,512]{5,4,3,2,1,0:T(8,128)(2,1)S(1)}, u32[]{:S(2)}, u32[]{:S(2)}) collective-permute-start(bf16[2,4,2,2,16,512]{5,4,3,2,1,0:T(8,128)(2,1)} %bitcast.5), channel_id=1, source_target_pairs={{0,24},{8,0},{16,8},{24,16},{1,25},{9,1},{17,9},{25,17},{2,26},{10... | collective-permute-start | bytes 1572872 | tf_op jit(solution)/shard_map/ppermute | solution.py:235
  144.9 16.1 %collective-permute-start.6 = (bf16[2,4,2,2,16,512]{5,4,3,2,1,0:T(8,128)(2,1)S(1)}, bf16[2,4,2,2,16,512]{5,4,3,2,1,0:T(8,128)(2,1)S(1)}, u32[]{:S(2)}, u32[]{:S(2)}) collective-permute-start(bf16[2,4,2,2,16,512]{5,4,3,2,1,0:T(8,128)(2,1)S(1)} %bitcast.12), channel_id=1, source_target_pairs={{0,8},{8,16},{16,24},{24,0},{1,9},{9,17},{17,25},{25,1},{2,10},{10... | collective-permute-start | bytes 1572872 | tf_op jit(solution)/shard_map/ppermute | solution.py:235
  147.4 24.9 %collective-permute-start.7 = (bf16[2,4,2,2,16,512]{5,4,3,2,1,0:T(8,128)(2,1)}, bf16[2,4,2,2,16,512]{5,4,3,2,1,0:T(8,128)(2,1)S(1)}, u32[]{:S(2)}, u32[]{:S(2)}) collective-permute-start(bf16[2,4,2,2,16,512]{5,4,3,2,1,0:T(8,128)(2,1)} %collective-permute-done.4), channel_id=1, source_target_pairs={{0,8},{8,16},{16,24},{24,0},{1,9},{9,17},{17,25},{25,1},{2,10},{10... | collective-permute-start | bytes 1572872 | tf_op jit(solution)/shard_map/ppermute | solution.py:235
  149.7 22.6 %collective-permute-start.8 = (bf16[2,4,2,2,16,512]{5,4,3,2,1,0:T(8,128)(2,1)}, bf16[2,4,2,2,16,512]{5,4,3,2,1,0:T(8,128)(2,1)S(1)}, u32[]{:S(2)}, u32[]{:S(2)}) collective-permute-start(bf16[2,4,2,2,16,512]{5,4,3,2,1,0:T(8,128)(2,1)} %collective-permute-done.5), channel_id=1, source_target_pairs={{0,24},{8,0},{16,8},{24,16},{1,25},{9,1},{17,9},{25,17},{2,26},{10... | collective-permute-start | bytes 1572872 | tf_op jit(solution)/shard_map/ppermute | solution.py:235
  178.2 1.2 copy-start

commit v9 on v8

--- a/solution.py
+++ b/solution.py
@@ -208,7 +208,8 @@
         grid_spec=pltpu.PrefetchScalarGridSpec(
             num_scalar_prefetch=1,
             grid=(1,),
-            in_specs=[pl.BlockSpec(memory_space=pl.ANY)] * (1 + len(arrays)),
+            in_specs=[pl.BlockSpec(memory_space=pl.ANY)] * 2
+            + [pl.BlockSpec(memory_space=pltpu.HBM)] * (len(arrays) - 1),
             out_specs=pl.BlockSpec(memory_space=pl.ANY),
             scratch_shapes=[
                 pltpu.VMEM((XS, xs, zhs, pairs, 2, rows, mu), jnp.bfloat16),

time: 185 us -> 185 us (level)
  no operation moved by 1% of the time
where the time goes in v9:
time: 185 us; the launch traced here: 184 us
  waiting for transfers between devices  100 us (54%)
  starting transfers between devices  65.8 us (36%)
  Pallas kernels  10.9 us (6%)
  local copies, waits for them, and re-layouts  3.79 us (2%)
  other arithmetic  2.61 us (1%)
    all_to_all x3, waiting for transfers between devices, swap(): return lax.all_to_all(blocks, axes, split_axis=0, concat_axis=0, tiled=True)  58.4 us
    ppermute x9, waiting for transfers between devices, shift(): return lax.ppermute(block, 'x', [(i, (i + d) % XS) for i in range(XS)])  34.8 us
    all_to_all x3, starting transfers between devices, swap(): return lax.all_to_all(blocks, axes, split_axis=0, concat_axis=0, tiled=True)  29.5 us
    ppermute x9, starting transfers between devices, shift(): return lax.ppermute(block, 'x', [(i, (i + d) % XS) for i in range(XS)])  27.5 us
    ppermute x1, starting transfers between devices, on_device(): other = lax.ppermute(right, 'zh', [(0, 1), (1, 0)])  8.8 us
    ppermute x1, waiting for transfers between devices, on_device(): other = lax.ppermute(right, 'zh', [(0, 1), (1, 0)])  7.33 us
    pallas_call x1, Pallas kernels, apply(): pl.pallas_call(functools.partial(apply_kernel, plan), grid_spec=pltpu.Pre...  4.37 us
  transfers between devices with their start and end apart: 13, of which 9 were waited for; matrix products, arithmetic and copies ran while one was open for 2% of the time, Pallas kernels for 1%

profile of v9, /device:TPU:33, one launch (start us, length us, event | category | flops | bytes accessed | tf_op | source)
XLA Modules:
  0.0 183.8 jit_solution(10690857982588073447)
XLA Ops:
  0.0 8.8 %collective-permute-start.3 = (bf16[2,4,16,512]{3,2,1,0:T(8,128)(2,1)}, bf16[2,4,16,512]{3,2,1,0:T(8,128)(2,1)S(1)}, u32[]{:S(2)}, u32[]{:S(2)}) collective-permute-start(bf16[2,4,16,512]{3,2,1,0:T(8,128)(2,1)} %right_ref.1), channel_id=1, source_target_pairs={{0,4},{4,0},{1,5},{5,1},{2,6},{6,2},{3,7},{7,3},{8,12},{12,8},{9,1... | collective-permute-start | bytes 393224 | tf_op jit(solution)/shard_map/ppermute | solution.py:244
  8.8 0.0 copy-start.3
  8.8 0.9 copy-done.3
  9.7 0.8 send.2.refs_0_
  10.6 0.0 copy-start.1
  10.6 7.3 %collective-permute-done.3.right_ref = bf16[2,4,16,512]{3,2,1,0:T(8,128)(2,1)S(1)} collective-permute-done((bf16[2,4,16,512]{3,2,1,0:T(8,128)(2,1)}, bf16[2,4,16,512]{3,2,1,0:T(8,128)(2,1)S(1)}, u32[]{:S(2)}, u32[]{:S(2)}) %collective-permute-start.3) | collective-permute-done | bytes 131104 | tf_op jit(solution)/shard_map/ppermute | solution.py:244
  17.9 0.8 send.3
  18.7 9.4 %all-to-all-start = ((bf16[16,2,2,16,512]{4,3,2,1,0:T(8,128)(2,1)}), bf16[16,2,2,16,512]{4,3,2,1,0:T(8,128)(2,1)S(1)}, u32[]{:S(2)}, u32[]{:S(2)}) async-start(bf16[16,2,2,16,512]{4,3,2,1,0:T(8,128)(2,1)} %bitcast.2), calls=%async_computation | async-start | bytes 2097152 | tf_op jit(solution)/shard_map/all_to_all | solution.py:232
  28.1 0.0 copy-done.1
  28.1 0.8 constant_dynamic-slice_fusion
  28.9 4.3 %collective-permute-start.2 = (bf16[2,1,128,512]{3,2,1,0:T(8,128)(2,1)}, bf16[2,1,128,512]{3,2,1,0:T(8,128)(2,1)S(1)}, u32[]{:S(2)}, u32[]{:S(2)}) collective-permute-start(bf16[2,1,128,512]{3,2,1,0:T(8,128)(2,1)} %get-tuple-element.13), channel_id=1, source_target_pairs={{0,24},{8,0},{16,8},{24,16},{1,25},{9,1},{17,9},{25,17},{2,26},{10... | collective-permute-start | bytes 786440 | tf_op jit(solution)/shard_map/ppermute | solution.py:236
  33.2 2.5 %collective-permute-start.1 = (bf16[2,1,128,512]{3,2,1,0:T(8,128)(2,1)S(1)}, bf16[2,1,128,512]{3,2,1,0:T(8,128)(2,1)S(1)}, u32[]{:S(2)}, u32[]{:S(2)}) collective-permute-start(bf16[2,1,128,512]{3,2,1,0:T(8,128)(2,1)S(1)} %get-tuple-element.14), channel_id=1, source_target_pairs={{0,16},{8,24},{16,0},{24,8},{1,17},{9,25},{17,1},{25,9},{2,18},{10... | collective-permute-start | bytes 786440 | tf_op jit(solution)/shard_map/ppermute | solution.py:236
  35.7 2.5 %collective-permute-start = (bf16[2,1,128,512]{3,2,1,0:T(8,128)(2,1)S(1)}, bf16[2,1,128,512]{3,2,1,0:T(8,128)(2,1)S(1)}, u32[]{:S(2)}, u32[]{:S(2)}) collective-permute-start(bf16[2,1,128,512]{3,2,1,0:T(8,128)(2,1)S(1)} %get-tuple-element.15), channel_id=1, source_target_pairs={{0,8},{8,16},{16,24},{24,0},{1,9},{9,17},{17,25},{25,1},{2,10},{10... | collective-permute-start | bytes 786440 | tf_op jit(solution)/shard_map/ppermute | solution.py:236
  38.2 0.1 pad_add_fusion.place_ref
  38.3 3.6 %collective-permute-done.2.refs_3_ = bf16[2,1,128,512]{3,2,1,0:T(8,128)(2,1)S(1)} collective-permute-done((bf16[2,1,128,512]{3,2,1,0:T(8,128)(2,1)}, bf16[2,1,128,512]{3,2,1,0:T(8,128)(2,1)S(1)}, u32[]{:S(2)}, u32[]{:S(2)}) %collective-permute-start.2) | collective-permute-done | bytes 262176 | tf_op jit(solution)/shard_map/ppermute | solution.py:236
  41.9 4.4 %collective-permute-done.1.refs_2_ = bf16[2,1,128,512]{3,2,1,0:T(8,128)(2,1)S(1)} collective-permute-done((bf16[2,1,128,512]{3,2,1,0:T(8,128)(2,1)S(1)}, bf16[2,1,128,512]{3,2,1,0:T(8,128)(2,1)S(1)}, u32[]{:S(2)}, u32[]{:S(2)}) %collective-permute-start.1) | collective-permute-done | bytes 262176 | tf_op jit(solution)/shard_map/ppermute | solution.py:236
  46.3 10.6 %collective-permute-done.refs_1_ = bf16[2,1,128,512]{3,2,1,0:T(8,128)(2,1)S(1)} collective-permute-done((bf16[2,1,128,512]{3,2,1,0:T(8,128)(2,1)S(1)}, bf16[2,1,128,512]{3,2,1,0:T(8,128)(2,1)S(1)}, u32[]{:S(2)}, u32[]{:S(2)}) %collective-permute-start) | collective-permute-done | bytes 262176 | tf_op jit(solution)/shard_map/ppermute | solution.py:236
  56.9 0.0 all-to-all-done
  56.9 2.6 %pairs.1 = bf16[4,2,2,4,2,32,128]{6,5,4,3,2,1,0:T(8,128)(2,1)} custom-call(s32[2]{0:T(128)S(1)} %pad_add_fusion.place_ref, bf16[2,4,128,512]{3,2,1,0:T(8,128)(2,1)S(1)} %copy-done.1, bf16[2,1,128,512]{3,2,1,0:T(8,128)(2,1)S(1)} %collective-permute-done.refs_1_, bf16[2,1,128,512]{3,2,1,0:T(8,128)(2,1)S(1)} %collective-permute-done.1.refs_2_, ...), custom_call_target="tpu_custom_call" | custom-call | flops 1073741824 | bytes 3145728 | tf_op jit(solution)/shard_map/pairs/pallas_call | solution.py:71
  59.6 0.0 copy-start.2
  59.6 15.2 %all-to-all-start.1 = ((bf16[64,2,32,128]{3,2,1,0:T(8,128)(2,1)}), bf16[64,2,32,128]{3,2,1,0:T(8,128)(2,1)S(1)}, u32[]{:S(2)}, u32[]{:S(2)}) async-start(bf16[64,2,32,128]{3,2,1,0:T(8,128)(2,1)} %bitcast.4), calls=%async_computation.1 | async-start | bytes 2097152 | tf_op jit(solution)/shard_map/all_to_all | solution.py:232
  74.8 0.9 fusion
  75.7 3.3 %collective-permute-start.4 = (bf16[2,4,2,2,16,512]{5,4,3,2,1,0:T(8,128)(2,1)}, bf16[2,4,2,2,16,512]{5,4,3,2,1,0:T(8,128)(2,1)}, u32[]{:S(2)}, u32[]{:S(2)}) collective-permute-start(bf16[2,4,2,2,16,512]{5,4,3,2,1,0:T(8,128)(2,1)} %bitcast.5), channel_id=1, source_target_pairs={{0,8},{8,16},{16,24},{24,0},{1,9},{9,17},{17,25},{25,1},{2,10},{10... | collective-permute-start | bytes 1572872 | tf_op jit(solution)/shard_map/ppermute | solution.py:236
  79.0 3.2 %collective-permute-start.5 = (bf16[2,4,2,2,16,512]{5,4,3,2,1,0:T(8,128)(2,1)S(1)}, bf16[2,4,2,2,16,512]{5,4,3,2,1,0:T(8,128)(2,1)}, u32[]{:S(2)}, u32[]{:S(2)}) collective-permute-start(bf16[2,4,2,2,16,512]{5,4,3,2,1,0:T(8,128)(2,1)S(1)} %bitcast.11), channel_id=1, source_target_pairs={{0,24},{8,0},{16,8},{24,16},{1,25},{9,1},{17,9},{25,17},{2,26},{10... | collective-permute-start | bytes 1572872 | tf_op jit(solution)/shard_map/ppermute | solution.py:236
  82.2 52.7 %all-to-all-done.1.x_ref = bf16[64,2,32,128]{3,2,1,0:T(8,128)(2,1)S(1)} async-done(((bf16[64,2,32,128]{3,2,1,0:T(8,128)(2,1)}), bf16[64,2,32,128]{3,2,1,0:T(8,128)(2,1)S(1)}, u32[]{:S(2)}, u32[]{:S(2)}) %all-to-all-start.1) | async-done | bytes 1048608 | tf_op jit(solution)/shard_map/all_to_all | solution.py:232
  134.9 0.0 copy-done.2
  134.9 2.2 %spectral.1 = bf16[64,2,32,128]{3,2,1,0:T(8,128)(2,1)} custom-call(bf16[64,2,32,128]{3,2,1,0:T(8,128)(2,1)S(1)} %all-to-all-done.1.x_ref, bf16[64,32,128]{2,1,0:T(8,128)(2,1)S(1)} %copy-done.2), custom_call_target="tpu_custom_call" | custom-call | flops 8388608 | bytes 2621440 | tf_op jit(solution)/shard_map/spectral/pallas_call | solution.py:143
  137.2 0.0 collective-permute-done.4
  137.2 0.0 collective-permute-done.5
  137.2 4.9 %all-to-all-start.2 = ((bf16[16,4,2,32,128]{4,3,2,1,0:T(8,128)(2,1)}), bf16[16,4,2,32,128]{4,3,2,1,0:T(8,128)(2,1)}, u32[]{:S(2)}, u32[]{:S(2)}) async-start(bf16[16,4,2,32,128]{4,3,2,1,0:T(8,128)(2,1)} %bitcast.7), calls=%async_computation.2 | async-start | bytes 2097152 | tf_op jit(solution)/shard_map/all_to_all | solution.py:232
  142.1 2.9 %collective-permute-start.9 = (bf16[2,4,2,2,16,512]{5,4,3,2,1,0:T(8,128)(2,1)}, bf16[2,4,2,2,16,512]{5,4,3,2,1,0:T(8,128)(2,1)S(1)}, u32[]{:S(2)}, u32[]{:S(2)}) collective-permute-start(bf16[2,4,2,2,16,512]{5,4,3,2,1,0:T(8,128)(2,1)} %bitcast.5), channel_id=1, source_target_pairs={{0,24},{8,0},{16,8},{24,16},{1,25},{9,1},{17,9},{25,17},{2,26},{10... | collective-permute-start | bytes 1572872 | tf_op jit(solution)/shard_map/ppermute | solution.py:236
  144.9 2.4 %collective-permute-start.6 = (bf16[2,4,2,2,16,512]{5,4,3,2,1,0:T(8,128)(2,1)S(1)}, bf16[2,4,2,2,16,512]{5,4,3,2,1,0:T(8,128)(2,1)S(1)}, u32[]{:S(2)}, u32[]{:S(2)}) collective-permute-start(bf16[2,4,2,2,16,512]{5,4,3,2,1,0:T(8,128)(2,1)S(1)} %bitcast.12), channel_id=1, source_target_pairs={{0,8},{8,16},{16,24},{24,0},{1,9},{9,17},{17,25},{25,1},{2,10},{10... | collective-permute-start | bytes 1572872 | tf_op jit(solution)/shard_map/ppermute | solution.py:236
  147.4 2.3 %collective-permute-start.7 = (bf16[2,4,2,2,16,512]{5,4,3,2,1,0:T(8,128)(2,1)}, bf16[2,4,2,2,16,512]{5,4,3,2,1,0:T(8,128)(2,1)S(1)}, u32[]{:S(2)}, u32[]{:S(2)}) collective-permute-start(bf16[2,4,2,2,16,512]{5,4,3,2,1,0:T(8,128)(2,1)} %collective-permute-done.4), channel_id=1, source_target_pairs={{0,8},{8,16},{16,24},{24,0},{1,9},{9,17},{17,25},{25,1},{2,10},{10... | collective-permute-start | bytes 1572872 | tf_op jit(solution)/shard_map/ppermute | solution.py:236
  149.7 4.2 %collective-permute-start.8 = (bf16[2,4,2,2,16,512]{5,4,3,2,1,0:T(8,128)(2,1)}, bf16[2,4,2,2,16,512]{5,4,3,2,1,0:T(8,128)(2,1)S(1)}, u32[]{:S(2)}, u32[]{:S(2)}) collective-permute-start(bf16[2,4,2,2,16,512]{5,4,3,2,1,0:T(8,128)(2,1)} %collective-permute-done.5), channel_id=1, source_target_pairs={{0,24},{8,0},{16,8},{24,16},{1,25},{9,1},{17,9},{25,17},{2,26},{10... | collective-permute-start | bytes 1572872 | tf_op jit(solution)/shard_map/ppermute | solution.py:236
  153.9 2.3 %pad_maximum_fusion.1.refs_1_ = bf16[4,4,2,2,16,512]{5,4,3,2,1,0:T(8,128)(2,1)} fusion(bf16[2,4,2,2,16,512]{5,4,3,2,1,0:T(8,128)(2,1)} %collective-permute-done.5, bf16[2,4,2,2,16,512]{5,4,3,2,1,0:T(8,128)(2,1)} %collective-permute-done.4), kind=kLoop, calls=%fused_computation.1 | loop fusion | flops 524288 | bytes 2097152 | tf_op jit(solution)/shard_map/concatenate | solution.py:258
  156.1 1.4 collective-permute-done.9
  157.5 3.6 %collective-permute-done.6 = bf16[2,4,2,2,16,512]{5,4,3,2,1,0:T(8,128)(2,1)S(1)} collective-permute-done((bf16[2,4,2,2,16,512]{5,4,3,2,1,0:T(8,128)(2,1)S(1)}, bf16[2,4,2,2,16,512]{5,4,3,2,1,0:T(8,128)(2,1)S(1)}, u32[]{:S(2)}, u32[]{:S(2)}) %collective-permute-start.6) | collective-permute-done | bytes 524320 | tf_op jit(solution)/shard_map/ppermute | solution.py:236
  161.1 11.2 %collective-permute-done.7 = bf16[2,4,2,2,16,512]{5,4,3,2,1,0:T(8,128)(2,1)S(1)} collective-permute-done((bf16[2,4,2,2,16,512]{5,4,3,2,1,0:T(8,128)(2,1)}, bf16[2,4,2,2,16,512]{5,4,3,2,1,0:T(8,128)(2,1)S(1)}, u32[]{:S(2)}, u32[]{:S(2)}) %collective-permute-start.7) | collective-permute-done | bytes 524320 | tf_op jit(solution)/shard_map/ppermute | solution.py:236
  172.3 0.0 collective-permute-done.8
  172.3 0.3 pad_maximum_fusion.refs_2_
  172.6 5.6 %all-to-all-done.2 = bf16[16,4,2,32,128]{4,3,2,1,0:T(8,128)(2,1)} async-done(((bf16[16,4,2,32,128]{4,3,2,1,0:T(8,128)(2,1)}), bf16[16,4,2,32,128]{4,3,2,1,0:T(8,128)(2,1)}, u32[]{:S(2)}, u32[]{:S(2)}) %all-to-all-start.2) | async-done | bytes 1048608 | tf_op jit(solution)/shard_map/all_to_all | solution.py:232
  178.2 0.0 copy-start
  178.2 1.2 copy-done
  179.4 4.4 %apply.1 = f32[2,4,128,512]{3,2,1,0:T(8,128)} custom-call(s32[2]{0:T(128)S(1)} %pad_add_fusion.place_ref, bf16[4,2,2,4,2,32,128]{6,5,4,3,2,1,0:T(8,128)(2,1)} %bitcast.8.kernel_ref, bf16[4,4,2,2,16,512]{5,4,3,2,1,0:T(8,128)(2,1)S(1)} %bitcast.10, bf16[4,4,2,2,16,512]{5,4,3,2,1,0:T(8,128)(2,1)S(1)} %copy-done, ...), custom_call_target="tpu_custom_call" | custom-call | flops 1073741824 | bytes 7340032 | tf_op jit(solution)/shard_map/apply/pallas_call | solution.py:206
Async XLA Ops:
  0.0 17.9 %collective-permute-start.3 = (bf16[2,4,16,512]{3,2,1,0:T(8,128)(2,1)}, bf16[2,4,16,512]{3,2,1,0:T(8,128)(2,1)S(1)}, u32[]{:S(2)}, u32[]{:S(2)}) collective-permute-start(bf16[2,4,16,512]{3,2,1,0:T(8,128)(2,1)} %right_ref.1), channel_id=1, source_target_pairs={{0,4},{4,0},{1,5},{5,1},{2,6},{6,2},{3,7},{7,3},{8,12},{12,8},{9,1... | collective-permute-start | bytes 393224 | tf_op jit(solution)/shard_map/ppermute | solution.py:244
  8.8 0.9 copy-start.3
  10.6 17.6 %copy-start.1 = (bf16[2,4,128,512]{3,2,1,0:T(8,128)(2,1)S(1)}, bf16[2,4,128,512]{3,2,1,0:T(8,128)(2,1)}, u32[]{:S(2)}) copy-start(bf16[2,4,128,512]{3,2,1,0:T(8,128)(2,1)} %refs_0_.1) | copy-start | bytes 3145732
  18.7 38.2 %all-to-all-start = ((bf16[16,2,2,16,512]{4,3,2,1,0:T(8,128)(2,1)}), bf16[16,2,2,16,512]{4,3,2,1,0:T(8,128)(2,1)S(1)}, u32[]{:S(2)}, u32[]{:S(2)}) async-start(bf16[16,2,2,16,512]{4,3,2,1,0:T(8,128)(2,1)} %bitcast.2), calls=%async_computation | async-start | bytes 2097152 | tf_op jit(solution)/shard_map/all_to_all | solution.py:232
  28.9 13.0 %collective-permute-start.2 = (bf16[2,1,128,512]{3,2,1,0:T(8,128)(2,1)}, bf16[2,1,128,512]{3,2,1,0:T(8,128)(2,1)S(1)}, u32[]{:S(2)}, u32[]{:S(2)}) collective-permute-start(bf16[2,1,128,512]{3,2,1,0:T(8,128)(2,1)} %get-tuple-element.13), channel_id=1, source_target_pairs={{0,24},{8,0},{16,8},{24,16},{1,25},{9,1},{17,9},{25,17},{2,26},{10... | collective-permute-start | bytes 786440 | tf_op jit(solution)/shard_map/ppermute | solution.py:236
  33.2 13.1 %collective-permute-start.1 = (bf16[2,1,128,512]{3,2,1,0:T(8,128)(2,1)S(1)}, bf16[2,1,128,512]{3,2,1,0:T(8,128)(2,1)S(1)}, u32[]{:S(2)}, u32[]{:S(2)}) collective-permute-start(bf16[2,1,128,512]{3,2,1,0:T(8,128)(2,1)S(1)} %get-tuple-element.14), channel_id=1, source_target_pairs={{0,16},{8,24},{16,0},{24,8},{1,17},{9,25},{17,1},{25,9},{2,18},{10... | collective-permute-start | bytes 786440 | tf_op jit(solution)/shard_map/ppermute | solution.py:236
  35.7 21.2 %collective-permute-start = (bf16[2,1,128,512]{3,2,1,0:T(8,128)(2,1)S(1)}, bf16[2,1,128,512]{3,2,1,0:T(8,128)(2,1)S(1)}, u32[]{:S(2)}, u32[]{:S(2)}) collective-permute-start(bf16[2,1,128,512]{3,2,1,0:T(8,128)(2,1)S(1)} %get-tuple-element.15), channel_id=1, source_target_pairs={{0,8},{8,16},{16,24},{24,0},{1,9},{9,17},{17,25},{25,1},{2,10},{10... | collective-permute-start | bytes 786440 | tf_op jit(solution)/shard_map/ppermute | solution.py:236
  59.6 75.4 %copy-start.2 = (bf16[64,32,128]{2,1,0:T(8,128)(2,1)S(1)}, bf16[64,32,128]{2,1,0:T(8,128)(2,1)}, u32[]{:S(2)}) copy-start(bf16[64,32,128]{2,1,0:T(8,128)(2,1)} %c_ref.1) | copy-start | bytes 1572868
  59.6 75.3 %all-to-all-start.1 = ((bf16[64,2,32,128]{3,2,1,0:T(8,128)(2,1)}), bf16[64,2,32,128]{3,2,1,0:T(8,128)(2,1)S(1)}, u32[]{:S(2)}, u32[]{:S(2)}) async-start(bf16[64,2,32,128]{3,2,1,0:T(8,128)(2,1)} %bitcast.4), calls=%async_computation.1 | async-start | bytes 2097152 | tf_op jit(solution)/shard_map/all_to_all | solution.py:232
  75.7 61.5 %collective-permute-start.4 = (bf16[2,4,2,2,16,512]{5,4,3,2,1,0:T(8,128)(2,1)}, bf16[2,4,2,2,16,512]{5,4,3,2,1,0:T(8,128)(2,1)}, u32[]{:S(2)}, u32[]{:S(2)}) collective-permute-start(bf16[2,4,2,2,16,512]{5,4,3,2,1,0:T(8,128)(2,1)} %bitcast.5), channel_id=1, source_target_pairs={{0,8},{8,16},{16,24},{24,0},{1,9},{9,17},{17,25},{25,1},{2,10},{10... | collective-permute-start | bytes 1572872 | tf_op jit(solution)/shard_map/ppermute | solution.py:236
  79.0 58.2 %collective-permute-start.5 = (bf16[2,4,2,2,16,512]{5,4,3,2,1,0:T(8,128)(2,1)S(1)}, bf16[2,4,2,2,16,512]{5,4,3,2,1,0:T(8,128)(2,1)}, u32[]{:S(2)}, u32[]{:S(2)}) collective-permute-start(bf16[2,4,2,2,16,512]{5,4,3,2,1,0:T(8,128)(2,1)S(1)} %bitcast.11), channel_id=1, source_target_pairs={{0,24},{8,0},{16,8},{24,16},{1,25},{9,1},{17,9},{25,17},{2,26},{10... | collective-permute-start | bytes 1572872 | tf_op jit(solution)/shard_map/ppermute | solution.py:236
  137.2 41.0 %all-to-all-start.2 = ((bf16[16,4,2,32,128]{4,3,2,1,0:T(8,128)(2,1)}), bf16[16,4,2,32,128]{4,3,2,1,0:T(8,128)(2,1)}, u32[]{:S(2)}, u32[]{:S(2)}) async-start(bf16[16,4,2,32,128]{4,3,2,1,0:T(8,128)(2,1)} %bitcast.7), calls=%async_computation.2 | async-start | bytes 2097152 | tf_op jit(solution)/shard_map/all_to_all | solution.py:232
  142.1 15.4 %collective-permute-start.9 = (bf16[2,4,2,2,16,512]{5,4,3,2,1,0:T(8,128)(2,1)}, bf16[2,4,2,2,16,512]{5,4,3,2,1,0:T(8,128)(2,1)S(1)}, u32[]{:S(2)}, u32[]{:S(2)}) collective-permute-start(bf16[2,4,2,2,16,512]{5,4,3,2,1,0:T(8,128)(2,1)} %bitcast.5), channel_id=1, source_target_pairs={{0,24},{8,0},{16,8},{24,16},{1,25},{9,1},{17,9},{25,17},{2,26},{10... | collective-permute-start | bytes 1572872 | tf_op jit(solution)/shard_map/ppermute | solution.py:236
  144.9 16.1 %collective-permute-start.6 = (bf16[2,4,2,2,16,512]{5,4,3,2,1,0:T(8,128)(2,1)S(1)}, bf16[2,4,2,2,16,512]{5,4,3,2,1,0:T(8,128)(2,1)S(1)}, u32[]{:S(2)}, u32[]{:S(2)}) collective-permute-start(bf16[2,4,2,2,16,512]{5,4,3,2,1,0:T(8,128)(2,1)S(1)} %bitcast.12), channel_id=1, source_target_pairs={{0,8},{8,16},{16,24},{24,0},{1,9},{9,17},{17,25},{25,1},{2,10},{10... | collective-permute-start | bytes 1572872 | tf_op jit(solution)/shard_map/ppermute | solution.py:236
  147.4 24.9 %collective-permute-start.7 = (bf16[2,4,2,2,16,512]{5,4,3,2,1,0:T(8,128)(2,1)}, bf16[2,4,2,2,16,512]{5,4,3,2,1,0:T(8,128)(2,1)S(1)}, u32[]{:S(2)}, u32[]{:S(2)}) collective-permute-start(bf16[2,4,2,2,16,512]{5,4,3,2,1,0:T(8,128)(2,1)} %collective-permute-done.4), channel_id=1, source_target_pairs={{0,8},{8,16},{16,24},{24,0},{1,9},{9,17},{17,25},{25,1},{2,10},{10... | collective-permute-start | bytes 1572872 | tf_op jit(solution)/shard_map/ppermute | solution.py:236
  149.7 22.6 %collective-permute-start.8 = (bf16[2,4,2,2,16,512]{5,4,3,2,1,0:T(8,128)(2,1)}, bf16[2,4,2,2,16,512]{5,4,3,2,1,0:T(8,128)(2,1)S(1)}, u32[]{:S(2)}, u32[]{:S(2)}) collective-permute-start(bf16[2,4,2,2,16,512]{5,4,3,2,1,0:T(8,128)(2,1)} %collective-permute-done.5), channel_id=1, source_target_pairs={{0,24},{8,0},{16,8},{24,16},{1,25},{9,1},{17,9},{25,17},{2,26},{10... | collective-permute-start | bytes 1572872 | tf_op jit(solution)/shard_map/ppermute | solution.py:236
  178.2 1.2 copy-start
